TPU v7x, 128 devices: a whole 4x4x4 slice. The times are simulated.
128 devices in a mesh: box: 8 (over z_hi, x), samp: 16 (over y, z_lo, core).
Axes of the slice: x: 4, y: 4, z: 4 (z_hi: 2, z_lo: 2; z = z_hi * 2 + z_lo), core: 2. Of those that a mesh axis runs over, the one named last changes fastest.
Arguments:
- child_patterns: float32 [1024, 2, 128, 256], P(('box', 'samp')), may hold values from -6 to 6
- octants: int32 [1024], P(('box', 'samp')), may hold values from 0 to 7
- parent_map: int32 [8, 128], P('box'), may hold values from 0 to 31, never falling along the last dimension, each value on 1 to 8 neighbouring positions
- far_boxes: int32 [256, 48], P('box'), may hold values from 0 to 255, as said below
- offsets: int32 [256, 48], P('box'), may hold values from 0 to 315
- translation: float32 [316, 2, 192, 384], P(None, None, 'samp'), may hold values from -0.5 to 0.5
Outputs:
- outgoing: float32 [256, 2, 192, 384], P('box', None, 'samp')
- incoming: float32 [256, 2, 192, 384], P('box', None, 'samp')
Inputs may be any that keep to these rules, and one draw needn't show every extreme that they name: `parent_map`: each row never falls, and every parent of a box group has 1 to 8 children. `far_boxes`: row p lists 48 different parent boxes, none equal to p.
All inputs are finite; a program needn't handle non-finite values.
Results may differ from a plain program's by a relative error of at most 0.0003.
Values sent between devices are 32-bit elements; how exact they have to be, the bound alone decides.
No kernel may reach another device: no remote copies, remote signals or barrier semaphores. Data moves between devices by JAX's collectives and lax.ppermute only.
A program may use at most 128 MiB of HBM per device.

v0:
```python
import math

import jax
import jax.numpy as jnp
from jax import lax
from jax.sharding import PartitionSpec as P

phase_scale = 12.0


def lagrange_table(n_old, n_new, periodic):
    rows = jnp.arange(n_new, dtype=jnp.int32)
    if periodic:
        numer = rows * n_old
        denom = n_new
    else:
        numer = (2 * rows + 1) * n_old - n_new
        denom = 2 * n_new
    start = numer // denom - 2
    if not periodic:
        start = jnp.clip(start, 0, n_old - 6)
    position = numer.astype(jnp.float32) / float(denom) - start.astype(jnp.float32)
    columns = jnp.arange(n_old, dtype=jnp.int32)
    table = jnp.zeros((n_new, n_old), jnp.float32)
    for node in range(6):
        weight = jnp.ones((n_new,), jnp.float32)
        for other in range(6):
            if other != node:
                weight = weight * (position - float(other)) / float(node - other)
        target = start + node
        if periodic:
            target = target % n_old
        table = table + weight[:, None] * (target[:, None] == columns[None, :]).astype(jnp.float32)
    return table


def phase_from_theta(octants, theta, n_phi):
    phi = jnp.arange(n_phi, dtype=jnp.float32) * (2.0 * math.pi / n_phi)
    sign_x = (1 - 2 * (octants % 2)).astype(jnp.float32)
    sign_y = (1 - 2 * (octants // 2 % 2)).astype(jnp.float32)
    sign_z = (1 - 2 * (octants // 4)).astype(jnp.float32)
    along_x = jnp.sin(theta)[:, None] * jnp.cos(phi)[None, :]
    along_y = jnp.sin(theta)[:, None] * jnp.sin(phi)[None, :]
    along_z = jnp.cos(theta)[:, None] * jnp.ones((n_phi,), jnp.float32)[None, :]
    angle = phase_scale * (
        sign_x[:, None, None] * along_x
        + sign_y[:, None, None] * along_y
        + sign_z[:, None, None] * along_z
    )
    return (jnp.cos(angle), jnp.sin(angle))


def apply_phase(fine, cos_part, sin_part):
    real = cos_part * fine[:, 0] - sin_part * fine[:, 1]
    imag = sin_part * fine[:, 0] + cos_part * fine[:, 1]
    return jnp.stack([real, imag], axis=1)


def aggregate(children, octants, theta_table, phi_table):
    along_phi = jnp.einsum("cktp,qp->cktq", children, phi_table, precision=lax.Precision.HIGHEST)
    fine = jnp.einsum("rt,cktq->ckrq", theta_table, along_phi, precision=lax.Precision.HIGHEST)
    n_theta = theta_table.shape[0]
    theta = (jnp.arange(n_theta, dtype=jnp.float32) + 0.5) * (math.pi / n_theta)
    cos_part, sin_part = phase_from_theta(octants, theta, phi_table.shape[0])
    return apply_phase(fine, cos_part, sin_part)


def shards(child_patterns, octants, parent_map, far_boxes, offsets, translation):
    count = child_patterns.shape[0]
    n_samp = lax.axis_size("samp")
    band, n_phi = (translation.shape[2], translation.shape[3])
    n_theta = band * n_samp
    n_child_theta = child_patterns.shape[2]
    parents = far_boxes.shape[0]
    theta_table = lagrange_table(n_child_theta, n_theta, False)
    phi_table = lagrange_table(child_patterns.shape[3], n_phi, True)
    owners_row = parent_map[0]
    parent_ids = jnp.arange(parents, dtype=jnp.int32)
    shifted = aggregate(child_patterns, octants, theta_table, phi_table)
    flat = shifted.reshape(count, -1)
    mine = lax.dynamic_slice_in_dim(owners_row, lax.axis_index("samp") * count, count, 0)
    select = (mine[None, :] == parent_ids[:, None]).astype(jnp.float32)
    partial_value = jnp.dot(select, flat, precision=lax.Precision.HIGHEST).reshape(
        parents, 2, n_theta, n_phi
    )
    outgoing = lax.psum_scatter(partial_value, "samp", scatter_dimension=2, tiled=True)
    everywhere = lax.all_gather(
        outgoing.reshape(parents, 2, band * n_phi), "box", axis=0, tiled=True
    )
    table = translation.reshape(translation.shape[0], 2, band * n_phi)
    width = 8

    def add_block(block_index, total):
        ids = lax.dynamic_slice_in_dim(far_boxes, block_index * width, width, 1)
        kinds = lax.dynamic_slice_in_dim(offsets, block_index * width, width, 1)
        source = jnp.take(everywhere, ids, axis=0)
        factor = jnp.take(table, kinds, axis=0)
        real = jnp.sum(
            factor[:, :, 0] * source[:, :, 0] - factor[:, :, 1] * source[:, :, 1], axis=1
        )
        imag = jnp.sum(
            factor[:, :, 0] * source[:, :, 1] + factor[:, :, 1] * source[:, :, 0], axis=1
        )
        return total + jnp.stack([real, imag], axis=1)

    start_total = jnp.zeros((parents, 2, band * n_phi), jnp.float32)
    incoming = lax.fori_loop(0, far_boxes.shape[1] // width, add_block, start_total)
    return (outgoing, incoming.reshape(parents, 2, band, n_phi))


def solution(mesh):
    in_specs = (
        P(("box", "samp"), None, None, None),
        P(("box", "samp")),
        P("box", None),
        P("box", None),
        P("box", None),
        P(None, None, "samp", None),
    )
    out_specs = (P("box", None, "samp", None), P("box", None, "samp", None))
    return jax.shard_map(shards, mesh=mesh, in_specs=in_specs, out_specs=out_specs, check_vma=False)
```

profile of v0, /device:TPU:32, one launch (start us, length us, event | category | flops | bytes accessed | tf_op | source)
XLA Modules:
  0.0 1068.8 jit_solution(10906394419859111804)
XLA Ops:
  16.5 9.5 multiply_subtract_fusion
  31.3 12.4 %fusion.59 = f32[32,2,192,384]{3,0,2,1:T(8,128)} fusion(f32[2,192,384,8]{2,3,1,0:T(8,128)} %bitcast.57, s32[8]{0:T(128)S(1)} %dynamic-slice_bitcast_fusion), kind=kOutput, calls=%fused_computation.89 | convolution fusion | flops 452985088 | bytes 23592992 | tf_op jit(solution)/shard_map/dot_general | solution.py:83
  45.6 402.9 %all-reduce.3.cloned.1.call-done = f32[32,2,192,384]{3,0,2,1:T(8,128)} async-done(((f32[32,2,192,384]{3,0,2,1:T(8,128)}), f32[32,2,192,384]{3,0,2,1:T(8,128)}) %all-reduce.3.cloned.1.call-update) | async-done | bytes 18874384
  454.4 117.0 %all-gather.2.cloned.1.call-done = f32[256,2,4608]{2,0,1:T(8,128)} async-done(((f32[32,2,4608]{2,0,1:T(8,128)}), f32[256,2,4608]{2,0,1:T(8,128)}) %all-gather.2.cloned.1.call-update) | async-done | bytes 9437200 | tf_op jit(solution)/shard_map/all_gather | solution.py:87
  571.4 17.1 %copy.19 = f32[256,2,4608]{2,1,0:T(2,128)} copy(f32[256,2,4608]{2,0,1:T(8,128)} %all-gather.2.cloned.1.call-done) | data formatting | bytes 18874368
  588.5 471.4 %while.14 = (s32[]{:T(128)}, f32[32,2,4608]{2,1,0:T(2,128)S(1)}, s32[32,48]{1,0:T(8,128)S(1)}, f32[316,2,4608]{2,1,0:T(2,128)}, s32[32,48]{1,0:T(8,128)S(1)}, /*...) while((s32[]{:T(128)}, f32[32,2,4608]{2,1,0:T(2,128)S(1)}, ...), condition=%wide.region_4.5_spmd.clone, body=%wide.region_1.4_spmd.clone.sunk | while | flops 14750727 | bytes 139220176 | solution.py:107
  589.0 19.8 %gather_fusion = f32[256,2,4608]{2,1,0:T(2,128)} fusion(f32[256,2,4608]{2,1,0:T(2,128)} %get-tuple-element.278, s32[1024]{0:T(1024)S(1)} %pad_clamp_fusion.4), kind=kCustom, calls=%fused_computation.1.clone.clone.1 | custom fusion | bytes 18875392 | tf_op jit(solution)/shard_map/while/body/eval_jaxpr/jit(_take)/gather | solution.py:96
  608.8 9.2 broadcast_select_fusion.4
  618.1 20.5 %gather_fusion.1 = f32[256,2,4608]{2,1,0:T(2,128)} fusion(f32[316,2,4608]{2,1,0:T(2,128)} %get-tuple-element.276, s32[1024]{0:T(1024)S(1)} %pad_clamp_fusion.5), kind=kCustom, calls=%fused_computation.clone.clone.1 | custom fusion | bytes 18875392 | tf_op jit(solution)/shard_map/while/body/eval_jaxpr/jit(_take)/gather | solution.py:97
  645.6 19.3 %subtract_reduce_fusion.2 = (f32[32,4608]{1,0:T(8,128)S(1)}, f32[32,4608]{1,0:T(8,128)S(1)}) fusion(f32[32,8,2,4608]{3,2,1,0:T(2,128)S(1)} %copy-done.2, f32[32,8,2,4608]{3,2,1,0:T(2,128)S(1)} %broadcast_select_fusion.5), kind=kLoop, calls=%fused_computation.5.clone.1 | loop fusion | flops 9142272 | bytes 20054016 | tf_op jit(solution)/shard_map/while/body/eval_jaxpr/reduce_sum | solution.py:98
  667.5 19.8 %gather_fusion = f32[256,2,4608]{2,1,0:T(2,128)} fusion(f32[256,2,4608]{2,1,0:T(2,128)} %get-tuple-element.278, s32[1024]{0:T(1024)S(1)} %pad_clamp_fusion.4), kind=kCustom, calls=%fused_computation.1.clone.clone.1 | custom fusion | bytes 18875392 | tf_op jit(solution)/shard_map/while/body/eval_jaxpr/jit(_take)/gather | solution.py:96
  687.4 9.2 broadcast_select_fusion.4
  696.6 20.5 %gather_fusion.1 = f32[256,2,4608]{2,1,0:T(2,128)} fusion(f32[316,2,4608]{2,1,0:T(2,128)} %get-tuple-element.276, s32[1024]{0:T(1024)S(1)} %pad_clamp_fusion.5), kind=kCustom, calls=%fused_computation.clone.clone.1 | custom fusion | bytes 18875392 | tf_op jit(solution)/shard_map/while/body/eval_jaxpr/jit(_take)/gather | solution.py:97
  717.1 7.1 broadcast_select_fusion.5
  724.1 19.3 %subtract_reduce_fusion.2 = (f32[32,4608]{1,0:T(8,128)S(1)}, f32[32,4608]{1,0:T(8,128)S(1)}) fusion(f32[32,8,2,4608]{3,2,1,0:T(2,128)S(1)} %copy-done.2, f32[32,8,2,4608]{3,2,1,0:T(2,128)S(1)} %broadcast_select_fusion.5), kind=kLoop, calls=%fused_computation.5.clone.1 | loop fusion | flops 9142272 | bytes 20054016 | tf_op jit(solution)/shard_map/while/body/eval_jaxpr/reduce_sum | solution.py:98
  746.1 19.8 %gather_fusion = f32[256,2,4608]{2,1,0:T(2,128)} fusion(f32[256,2,4608]{2,1,0:T(2,128)} %get-tuple-element.278, s32[1024]{0:T(1024)S(1)} %pad_clamp_fusion.4), kind=kCustom, calls=%fused_computation.1.clone.clone.1 | custom fusion | bytes 18875392 | tf_op jit(solution)/shard_map/while/body/eval_jaxpr/jit(_take)/gather | solution.py:96
  765.9 9.2 broadcast_select_fusion.4
  775.1 20.5 %gather_fusion.1 = f32[256,2,4608]{2,1,0:T(2,128)} fusion(f32[316,2,4608]{2,1,0:T(2,128)} %get-tuple-element.276, s32[1024]{0:T(1024)S(1)} %pad_clamp_fusion.5), kind=kCustom, calls=%fused_computation.clone.clone.1 | custom fusion | bytes 18875392 | tf_op jit(solution)/shard_map/while/body/eval_jaxpr/jit(_take)/gather | solution.py:97
  795.6 7.1 broadcast_select_fusion.5
  802.7 19.3 %subtract_reduce_fusion.2 = (f32[32,4608]{1,0:T(8,128)S(1)}, f32[32,4608]{1,0:T(8,128)S(1)}) fusion(f32[32,8,2,4608]{3,2,1,0:T(2,128)S(1)} %copy-done.2, f32[32,8,2,4608]{3,2,1,0:T(2,128)S(1)} %broadcast_select_fusion.5), kind=kLoop, calls=%fused_computation.5.clone.1 | loop fusion | flops 9142272 | bytes 20054016 | tf_op jit(solution)/shard_map/while/body/eval_jaxpr/reduce_sum | solution.py:98
  824.6 19.8 %gather_fusion = f32[256,2,4608]{2,1,0:T(2,128)} fusion(f32[256,2,4608]{2,1,0:T(2,128)} %get-tuple-element.278, s32[1024]{0:T(1024)S(1)} %pad_clamp_fusion.4), kind=kCustom, calls=%fused_computation.1.clone.clone.1 | custom fusion | bytes 18875392 | tf_op jit(solution)/shard_map/while/body/eval_jaxpr/jit(_take)/gather | solution.py:96
  844.4 9.2 broadcast_select_fusion.4
  853.7 20.5 %gather_fusion.1 = f32[256,2,4608]{2,1,0:T(2,128)} fusion(f32[316,2,4608]{2,1,0:T(2,128)} %get-tuple-element.276, s32[1024]{0:T(1024)S(1)} %pad_clamp_fusion.5), kind=kCustom, calls=%fused_computation.clone.clone.1 | custom fusion | bytes 18875392 | tf_op jit(solution)/shard_map/while/body/eval_jaxpr/jit(_take)/gather | solution.py:97
  881.2 19.3 %subtract_reduce_fusion.2 = (f32[32,4608]{1,0:T(8,128)S(1)}, f32[32,4608]{1,0:T(8,128)S(1)}) fusion(f32[32,8,2,4608]{3,2,1,0:T(2,128)S(1)} %copy-done.2, f32[32,8,2,4608]{3,2,1,0:T(2,128)S(1)} %broadcast_select_fusion.5), kind=kLoop, calls=%fused_computation.5.clone.1 | loop fusion | flops 9142272 | bytes 20054016 | tf_op jit(solution)/shard_map/while/body/eval_jaxpr/reduce_sum | solution.py:98
  903.1 19.8 %gather_fusion = f32[256,2,4608]{2,1,0:T(2,128)} fusion(f32[256,2,4608]{2,1,0:T(2,128)} %get-tuple-element.278, s32[1024]{0:T(1024)S(1)} %pad_clamp_fusion.4), kind=kCustom, calls=%fused_computation.1.clone.clone.1 | custom fusion | bytes 18875392 | tf_op jit(solution)/shard_map/while/body/eval_jaxpr/jit(_take)/gather | solution.py:96
  923.0 9.2 broadcast_select_fusion.4
  932.2 20.5 %gather_fusion.1 = f32[256,2,4608]{2,1,0:T(2,128)} fusion(f32[316,2,4608]{2,1,0:T(2,128)} %get-tuple-element.276, s32[1024]{0:T(1024)S(1)} %pad_clamp_fusion.5), kind=kCustom, calls=%fused_computation.clone.clone.1 | custom fusion | bytes 18875392 | tf_op jit(solution)/shard_map/while/body/eval_jaxpr/jit(_take)/gather | solution.py:97
  959.8 19.3 %subtract_reduce_fusion.2 = (f32[32,4608]{1,0:T(8,128)S(1)}, f32[32,4608]{1,0:T(8,128)S(1)}) fusion(f32[32,8,2,4608]{3,2,1,0:T(2,128)S(1)} %copy-done.2, f32[32,8,2,4608]{3,2,1,0:T(2,128)S(1)} %broadcast_select_fusion.5), kind=kLoop, calls=%fused_computation.5.clone.1 | loop fusion | flops 9142272 | bytes 20054016 | tf_op jit(solution)/shard_map/while/body/eval_jaxpr/reduce_sum | solution.py:98
  981.7 19.8 %gather_fusion = f32[256,2,4608]{2,1,0:T(2,128)} fusion(f32[256,2,4608]{2,1,0:T(2,128)} %get-tuple-element.278, s32[1024]{0:T(1024)S(1)} %pad_clamp_fusion.4), kind=kCustom, calls=%fused_computation.1.clone.clone.1 | custom fusion | bytes 18875392 | tf_op jit(solution)/shard_map/while/body/eval_jaxpr/jit(_take)/gather | solution.py:96
  1001.5 9.2 broadcast_select_fusion.4
  1010.7 20.5 %gather_fusion.1 = f32[256,2,4608]{2,1,0:T(2,128)} fusion(f32[316,2,4608]{2,1,0:T(2,128)} %get-tuple-element.276, s32[1024]{0:T(1024)S(1)} %pad_clamp_fusion.5), kind=kCustom, calls=%fused_computation.clone.clone.1 | custom fusion | bytes 18875392 | tf_op jit(solution)/shard_map/while/body/eval_jaxpr/jit(_take)/gather | solution.py:97
  1038.3 19.3 %subtract_reduce_fusion.2 = (f32[32,4608]{1,0:T(8,128)S(1)}, f32[32,4608]{1,0:T(8,128)S(1)}) fusion(f32[32,8,2,4608]{3,2,1,0:T(2,128)S(1)} %copy-done.2, f32[32,8,2,4608]{3,2,1,0:T(2,128)S(1)} %broadcast_select_fusion.5), kind=kLoop, calls=%fused_computation.5.clone.1 | loop fusion | flops 9142272 | bytes 20054016 | tf_op jit(solution)/shard_map/while/body/eval_jaxpr/reduce_sum | solution.py:98
  (110 shorter events, 67.2 us)
Async XLA Ops:
  7.2 1.6 copy-start
  7.2 441.4 %all-reduce.3.cloned.1.call-start = ((), (), s32[]{:S(2)}) async-start(), calls=%async_computation.1 | async-start | bytes 37748736
  26.4 4.9 copy-start.6
  43.7 0.7 copy-start.7
  43.8 527.6 %all-gather.2.cloned.1.call-start = ((), (), s32[]{:S(2)}) async-start(), calls=%async_computation | async-start | bytes 10616832 | tf_op jit(solution)/shard_map/all_gather | solution.py:87
  454.4 134.1 %copy-start.4 = (s32[32,48]{1,0:T(8,128)S(1)}, s32[32,48]{1,0:T(8,128)}, u32[]{:S(2)}) copy-start(s32[32,48]{1,0:T(8,128)} %param.12) | copy-start | bytes 18436
  454.4 134.1 %copy-start.5 = (s32[32,48]{1,0:T(8,128)S(1)}, s32[32,48]{1,0:T(8,128)}, u32[]{:S(2)}) copy-start(s32[32,48]{1,0:T(8,128)} %param.11) | copy-start | bytes 18436
  638.5 7.1 copy-start.2
  717.1 7.1 copy-start.2
  795.6 7.1 copy-start.2
  874.1 7.1 copy-start.2
  952.7 7.1 copy-start.2
  1031.2 7.1 copy-start.2
  1059.9 1.0 copy-start.3
  1059.9 2.0 copy-start.1
Sparse Core Ops, SparseCore 0:
  43.9 404.6 all-reduce.2
  451.4 119.9 all-gather.1
where the time goes:
time: 1070 us
  waiting for transfers between devices  520 us (49%)
  local copies, waits for them, and re-layouts  279 us (26%)
  other arithmetic  234 us (22%)
  matrix products  20.1 us (2%)
  between operations  14.8 us (1%)
    unnamed x3, waiting for transfers between devices  403 us
    gather x6, local copies, waits for them, and re-layouts, add_block(): factor = jnp.take(table, kinds, axis=0)  123 us
    gather x6, local copies, waits for them, and re-layouts, add_block(): source = jnp.take(everywhere, ids, axis=0)  119 us
    all_gather x1, waiting for transfers between devices, shards(): lax.all_gather(outgoing.reshape(parents, 2, band * n_phi), 'box', axis=0,...  117 us
    reduce_sum x6, other arithmetic, add_block(): jnp.sum(factor[:, :, 0] * source[:, :, 0] - factor[:, :, 1] * source[:, :...  116 us
    select_n x6, other arithmetic, add_block(): source = jnp.take(everywhere, ids, axis=0)  55.3 us
    select_n x6, other arithmetic, add_block(): factor = jnp.take(table, kinds, axis=0)  42.3 us
    unnamed x20, local copies, waits for them, and re-layouts  29.9 us
  transfers between devices with their start and end apart: 2, of which 2 were waited for; matrix products, arithmetic and copies ran while one was open for 0% of the time, Pallas kernels for 0%

commit v1 on v0

v1 whole, which is shorter than its diff:
```python
import functools
import math

import jax
import jax.numpy as jnp
import numpy as np
from jax import lax
from jax.experimental import pallas as pl
from jax.experimental.pallas import tpu as pltpu
from jax.sharding import PartitionSpec as P

phase_scale = 12.0
VMEM_LIMIT = 24 * 1024 * 1024


def lagrange_table(n_old, n_new, periodic):
    rows = np.arange(n_new)
    if periodic:
        numer, denom = rows * n_old, n_new
    else:
        numer, denom = (2 * rows + 1) * n_old - n_new, 2 * n_new
    start = numer // denom - 2
    if not periodic:
        start = np.clip(start, 0, n_old - 6)
    position = numer / denom - start
    table = np.zeros((n_new, n_old))
    for node in range(6):
        weight = np.ones(n_new)
        for other in range(6):
            if other != node:
                weight = weight * (position - other) / (node - other)
        target = start + node
        if periodic:
            target = target % n_old
        table[rows, target] += weight
    return table


def high_low(table):
    table = table.astype(np.float32)
    high = table.astype(jnp.bfloat16)
    low = (table - high.astype(np.float32)).astype(jnp.bfloat16)
    return high, low


def split(x):
    high = x.astype(jnp.bfloat16)
    low = (x - high.astype(jnp.float32)).astype(jnp.bfloat16)
    return high, low


def dot3(a, b):
    f = functools.partial(jnp.dot, preferred_element_type=jnp.float32)
    return f(a[0], b[0]) + (f(a[0], b[1]) + f(a[1], b[0]))


def theta_kernel(octants, table_high, table_low, child, out, token, tables, kids, bands, sems):
    n_kids, n_samp = child.shape[0], out.shape[0]
    loads = [pltpu.make_async_copy(child.at[c], kids.at[c], sems.at[c]) for c in range(n_kids)]
    loads[0].start()
    parts = [
        pltpu.make_async_copy(table, tables.at[i], sems.at[n_kids + i])
        for i, table in enumerate((table_high, table_low))
    ]
    for copy in parts:
        copy.start()
    for copy in loads[1:]:
        copy.start()
    row = lax.broadcasted_iota(jnp.int32, (8, out.shape[2]), 0)
    v = jnp.zeros((8, out.shape[2]), jnp.int32)
    for i in range(8):
        v = jnp.where(row == i, octants[i], v)
    v = v.astype(jnp.float32)
    for s in range(n_samp):
        bands[s, 192:200, :] = v
    token[...] = v[:, 0:128]
    for copy in parts:
        copy.wait()
    stores = []
    for c in range(n_kids):
        loads[c].wait()
        x = split(kids[c].reshape(kids.shape[1] * kids.shape[2], kids.shape[3]))
        y = dot3((tables[0], tables[1]), x)
        for s in range(n_samp):
            bands[s, 24 * c : 24 * c + 24, :] = y[24 * s : 24 * s + 24]
        if c % 2:
            first, last = 24 * (c - 1), 24 * (c + 1) + (8 if c == n_kids - 1 else 0)
            rows = pl.ds(first, last - first)
            stores.append(pltpu.make_async_copy(bands.at[:, rows], out.at[:, rows], sems.at[n_kids + 2 + c // 2]))
            stores[-1].start()
    for copy in stores:
        copy.wait()


def prepare_kernel(box, token, table, high, low, cos, sin, out, high_out, low_out, cos_out, sin_out, raw, sems):
    me = box[0]
    n_off = table.shape[0]
    pair, half = me // 2, me % 2
    copies = []
    for q in range(5):
        at = 4 * me + q if q < 4 else 32 + pair
        lanes = pl.ds(pl.multiple_of(128 * (at % 3), 128), 128)
        copies.append(
            pltpu.make_async_copy(table.at[:, at // 3, :, lanes], raw.at[:, q], sems.at[q])
        )
        copies[-1].start()
    high_out[...], low_out[...] = high[...], low[...]
    cos_out[...], sin_out[...] = cos[...], sin[...]
    for copy in copies:
        copy.wait()
    left = lax.broadcasted_iota(jnp.int32, (1, 128), 1) < 64
    upper = jnp.full((1, 128), half, jnp.int32) == 1

    def one(i, carry):
        out[i, 0:8] = jnp.concatenate([raw[i, q] for q in range(4)], 0)
        re, im = raw[i, 4, 0:1], raw[i, 4, 1:2]
        x = jnp.where(left, re, pltpu.roll(im, 64, 1))
        y = jnp.where(left, pltpu.roll(re, 64, 1), im)
        out[i, 8:16] = jnp.broadcast_to(jnp.where(upper, y, x), (8, 128))
        return carry

    lax.fori_loop(0, n_off // 4, lambda i, c: [one(4 * i + u, c) for u in range(4)][-1], 0)


def phi_kernel(owners, lists, table_high, table_low, cos_ref, sin_ref, recv, outgoing, send, total, rows_v, send_v, kinds_v, kinds, sems):
    for s in range(16):
        kinds_v[8 * s : 8 * s + 8, :] = recv[s, 192:200, 0:128].astype(jnp.int32)
    copy = pltpu.make_async_copy(kinds_v, kinds, sems.at[0])
    copy.start()
    total[...] = jnp.zeros_like(total)
    for d in range(8):
        send_v[d, 288:320, :] = lists[...]
    copy.wait()

    def source(s, carry):
        fine = dot3(split(recv[s, 0:192, :]), (table_high[...], table_low[...]))
        for c in range(8):
            child = s * 8 + c
            owner, octant = owners[child], kinds[child, 0]
            f = fine[24 * c : 24 * c + 24]
            cos_0, sin_0 = cos_ref[octant, 0:8], sin_ref[octant, 0:8]
            total[owner, 0:8] += cos_0 * f[0:8] - sin_0 * f[8:16]
            total[owner, 8:16] += sin_0 * f[0:8] + cos_0 * f[8:16]
            swapped = pltpu.roll(f[16:24], 4, 0)
            total[owner, 16:24] += cos_ref[octant, 8:16] * f[16:24] + sin_ref[octant, 8:16] * swapped
        return carry

    lax.fori_loop(0, 16, source, 0)

    def parent(p, carry):
        for l in range(3):
            v = total[p, :, 128 * l : 128 * l + 128]
            base = 72 * p + 2 * l
            rows_v[pl.ds(base, 8, stride=6), :] = v[0:8]
            rows_v[pl.ds(base + 1, 8, stride=6), :] = v[8:16]
            rows_v[pl.ds(base + 48, 4, stride=6), :] = v[16:20]
            rows_v[pl.ds(base + 49, 4, stride=6), :] = v[20:24]
        for d in range(8):
            at = pl.multiple_of(72 * p + 8 * d, 8)
            send_v[d, pl.ds(pl.multiple_of(8 * p, 8), 8), :] = rows_v[pl.ds(at, 8), :]
        return carry

    left = lax.broadcasted_iota(jnp.int32, (8, 128), 1) < 64
    copies = []
    for q in range(4):
        lax.fori_loop(8 * q, 8 * q + 8, parent, 0)
        rows = pl.ds(64 * q, 64)
        copies.append(pltpu.make_async_copy(send_v.at[:, rows], send.at[:, rows], sems.at[1 + q]))
        copies[-1].start()
        for r in range(4):
            at = 72 * 8 * q + 64 + 2 * r
            re, im = rows_v[pl.ds(at, 8, stride=72), :], rows_v[pl.ds(at + 1, 8, stride=72), :]
            rows = slice(256 + 8 * q, 264 + 8 * q)
            send_v[2 * r, rows, :] = jnp.where(left, re, pltpu.roll(im, 64, 1))
            send_v[2 * r + 1, rows, :] = jnp.where(left, pltpu.roll(re, 64, 1), im)
    rows = pl.ds(256, 64)
    copies.append(pltpu.make_async_copy(send_v.at[:, rows], send.at[:, rows], sems.at[5]))
    copies[-1].start()
    copies.append(pltpu.make_async_copy(rows_v, outgoing, sems.at[6]))
    copies[-1].start()
    for copy in copies:
        copy.wait()


def translate_kernel(recv, factor, send, source, sums, send_v, idx_v, idx, sems):
    copies = []
    for b in range(8):
        rows = pl.ds(32 * b, 32)
        idx_v[rows, :] = recv[b, 288:320, :].astype(jnp.int32)
        copies.append(pltpu.make_async_copy(idx_v.at[rows], idx.at[rows], sems.at[b]))
        copies[-1].start()
    left = lax.broadcasted_iota(jnp.int32, (8, 128), 1) < 64
    even = lax.broadcasted_iota(jnp.int32, (8, 128), 0) % 2 == 0
    for b in range(8):

        def prepare(p, carry):
            v = recv[b, pl.ds(pl.multiple_of(8 * p, 8), 8), :]
            at = pl.multiple_of((b * 32 + p) * 24, 8)
            source[pl.ds(at, 8), :] = jnp.where(even, v, pltpu.roll(v, 1, 0))
            source[pl.ds(at + 8, 8), :] = jnp.where(even, pltpu.roll(v, 7, 0), v)
            return carry

        lax.fori_loop(0, 32, prepare, 0, unroll=8)
        for q in range(4):
            v = recv[b, 256 + 8 * q : 264 + 8 * q, :]
            r = pltpu.roll(v, 64, 1)
            at = (b * 32 + 8 * q) * 24 + 16
            source[pl.ds(at, 8, stride=24), :] = jnp.where(left, v, r)
            source[pl.ds(at + 1, 8, stride=24), :] = jnp.where(left, r, v)

    n_far = 48

    def one(row, carry):
        acc = [jnp.zeros((8, 128), jnp.float32) for _ in range(3)]
        for j in range(n_far):
            f = pl.multiple_of(idx[row, j], 8)
            o = pl.multiple_of(idx[row, n_far + j], 8)
            t = factor[pl.ds(o, 8), :]
            acc[0] += t * source[pl.ds(f, 8), :]
            acc[1] += t * source[pl.ds(f + 8, 8), :]
            acc[2] += factor[pl.ds(o + 8, 8), :] * source[pl.ds(f + 16, 8), :]
        for k in range(3):
            sums[pl.ds(pl.multiple_of(24 * row, 8) + 8 * k, 8), :] = acc[k]
        return carry

    def finish(p, b):
        at = pl.multiple_of((b * 32 + p) * 24, 8)
        r = sums[pl.ds(at + 8, 8), :]
        r = jnp.where(even, -pltpu.roll(r, 7, 0), pltpu.roll(r, 1, 0))
        send_v[b, pl.ds(pl.multiple_of(8 * p, 8), 8), :] = sums[pl.ds(at, 8), :] + r
        return b

    for copy in copies:
        copy.wait()
    lax.fori_loop(0, 256, one, 0)
    copies = []
    for b in range(8):
        lax.fori_loop(0, 32, finish, b, unroll=8)
        for q in range(4):
            at = (b * 32 + 8 * q) * 24 + 16
            r = pltpu.roll(sums[pl.ds(at + 1, 8, stride=24), :], 64, 1)
            rows = slice(256 + 8 * q, 264 + 8 * q)
            send_v[b, rows, :] = sums[pl.ds(at, 8, stride=24), :] + jnp.where(left, -r, r)
        if b % 2:
            two = pl.ds(b - 1, 2)
            copies.append(pltpu.make_async_copy(send_v.at[two], send.at[two], sems.at[8 + b // 2]))
            copies[-1].start()
    for copy in copies:
        copy.wait()


def place_rows_kernel(rows, out):
    def one(p, carry):
        for at in range(36):
            v = rows[pl.ds(pl.multiple_of(72 * p, 8) + 2 * at, 2), :]
            out[p, at // 3, :, 128 * (at % 3) : 128 * (at % 3) + 128] = v
        return carry

    lax.fori_loop(0, 32, one, 0)


def place_kernel(recv, out, last):
    left = lax.broadcasted_iota(jnp.int32, (8, 128), 1) < 64
    for q in range(4):
        for r in range(4):
            rows = slice(256 + 8 * q, 264 + 8 * q)
            e, o = recv[2 * r, rows, :], recv[2 * r + 1, rows, :]
            at = 8 * 8 * q + 2 * r
            last[pl.ds(at, 8, stride=8), :] = jnp.where(left, e, pltpu.roll(o, 64, 1))
            last[pl.ds(at + 1, 8, stride=8), :] = jnp.where(left, pltpu.roll(e, 64, 1), o)

    def one(p, carry):
        base = pl.multiple_of(8 * p, 8)
        for at in range(36):
            rows = pl.ds(base + 2 * (at % 4), 2)
            v = recv[at // 4, rows, :] if at < 32 else last[rows, :]
            out[p, at // 3, :, 128 * (at % 3) : 128 * (at % 3) + 128] = v
        return carry

    lax.fori_loop(0, 32, one, 0)


def phase_tables(samp, n_theta, n_phi):
    polar = np.concatenate([np.arange(12), np.arange(8, 12)])
    sign = np.where((np.arange(16) >= 8) & (np.arange(16) < 12), -1.0, 1.0).astype(np.float32)
    theta = (samp * 12 + polar).astype(jnp.float32) * (math.pi / n_theta) + 0.5 * math.pi / n_theta
    phi = np.arange(n_phi) * (2.0 * math.pi / n_phi)
    o = np.arange(8)
    sx, sy, sz = 1.0 - 2 * (o % 2), 1.0 - 2 * (o // 2 % 2), 1.0 - 2 * (o // 4)
    around = (sx[:, None] * np.cos(phi) + sy[:, None] * np.sin(phi)).astype(np.float32)
    angle = phase_scale * (
        jnp.sin(theta)[None, :, None] * around[:, None, :]
        + (sz.astype(np.float32)[:, None] * jnp.cos(theta)[None, :])[:, :, None]
    )
    return jnp.cos(angle), jnp.sin(angle) * sign[None, :, None]


def vmem():
    return pl.BlockSpec(memory_space=pltpu.VMEM)


def smem():
    return pl.BlockSpec(memory_space=pltpu.SMEM)


def held(x):
    return pltpu.with_memory_space_constraint(x, pltpu.VMEM)


def params():
    return pltpu.CompilerParams(vmem_limit_bytes=VMEM_LIMIT)


def anywhere():
    return pl.BlockSpec(memory_space=pl.ANY)


def far_away(x):
    return pltpu.with_memory_space_constraint(x, pltpu.HBM)


def shards(child_patterns, octants, parent_map, far_boxes, offsets, translation):
    n_box, n_samp = lax.axis_size("box"), lax.axis_size("samp")
    count, _, n_t1, n_p1 = child_patterns.shape
    n_off, _, band, n_p2 = translation.shape
    n_t2 = band * n_samp
    parents, n_far = far_boxes.shape
    box, samp = lax.axis_index("box"), lax.axis_index("samp")
    f32, bf16 = jnp.float32, jnp.bfloat16

    theta_table = lagrange_table(n_t1, n_t2, False).reshape(n_samp, band, n_t1)
    both = np.zeros((n_samp, 24, 2, n_t1))
    both[:, 0:8, 0], both[:, 8:16, 1] = theta_table[:, 0:8], theta_table[:, 0:8]
    both[:, 16:20, 0], both[:, 20:24, 1] = theta_table[:, 8:12], theta_table[:, 8:12]
    theta_high, theta_low = high_low(both.reshape(n_samp * 24, 2 * n_t1))
    phi_high, phi_low = high_low(lagrange_table(n_p1, n_p2, True).T)

    sent = (n_samp, 24 * count + 8, n_p1)
    bands, token = pl.pallas_call(
        theta_kernel,
        in_specs=[smem()] + [anywhere()] * 3,
        out_specs=[anywhere(), vmem()],
        out_shape=[pltpu.HBM(sent, f32), jax.ShapeDtypeStruct((8, 128), f32)],
        scratch_shapes=[
            pltpu.VMEM((2, n_samp * 24, 2 * n_t1), bf16),
            pltpu.VMEM(child_patterns.shape, f32),
            pltpu.VMEM(sent, f32),
            pltpu.SemaphoreType.DMA((count + 2 + count // 2,)),
        ],
        compiler_params=params(),
        name="theta",
    )(octants, far_away(theta_high), far_away(theta_low), far_away(child_patterns))
    bands = lax.all_to_all(bands, "samp", 0, 0)

    cos_part, sin_part = phase_tables(samp, n_t2, n_p2)
    factor, *tables = pl.pallas_call(
        prepare_kernel,
        in_specs=[smem(), vmem(), anywhere()] + [vmem()] * 4,
        out_specs=[vmem()] * 5,
        out_shape=[
            pltpu.VMEM((n_off, 16, 128), f32),
            pltpu.VMEM(phi_high.shape, bf16),
            pltpu.VMEM(phi_high.shape, bf16),
            pltpu.VMEM(cos_part.shape, f32),
            pltpu.VMEM(cos_part.shape, f32),
        ],
        scratch_shapes=[pltpu.VMEM((n_off, 5, 2, 128), f32), pltpu.SemaphoreType.DMA((5,))],
        compiler_params=params(),
        cost_estimate=pl.CostEstimate(flops=10**7, bytes_accessed=10**7, transcendentals=0),
        name="prepare",
    )(box.reshape(1), token, far_away(translation.transpose(0, 2, 1, 3)), phi_high, phi_low, cos_part, sin_part)
    lists = jnp.concatenate([far_boxes * 24, offsets * 16, jnp.zeros((parents, 128 - 2 * n_far), jnp.int32)], 1)

    outgoing, send = pl.pallas_call(
        phi_kernel,
        in_specs=[smem()] + [vmem()] * 6,
        out_specs=[anywhere()] * 2,
        out_shape=[pltpu.HBM((parents * 72, 128), f32), pltpu.HBM((n_box, 10 * parents, 128), f32)],
        scratch_shapes=[
            pltpu.VMEM((parents, 24, n_p2), f32),
            pltpu.VMEM((parents * 72, 128), f32),
            pltpu.VMEM((n_box, 10 * parents, 128), f32),
            pltpu.VMEM((n_samp * count, 128), jnp.int32),
            pltpu.SMEM((n_samp * count, 128), jnp.int32),
            pltpu.SemaphoreType.DMA((7,)),
        ],
        compiler_params=params(),
        name="phi",
    )(parent_map[0], lists.astype(f32), *[held(x) for x in tables], held(bands))

    everywhere = lax.all_to_all(send, "box", 0, 0)
    n_all = n_box * parents
    back = pl.pallas_call(
        translate_kernel,
        in_specs=[vmem(), vmem()],
        out_specs=anywhere(),
        out_shape=pltpu.HBM((n_box, 9 * parents, 128), f32),
        scratch_shapes=[
            pltpu.VMEM((n_all * 24, 128), f32),
            pltpu.VMEM((n_all * 24, 128), f32),
            pltpu.VMEM((n_box, 9 * parents, 128), f32),
            pltpu.VMEM((n_all, 128), jnp.int32),
            pltpu.SMEM((n_all, 128), jnp.int32),
            pltpu.SemaphoreType.DMA((12,)),
        ],
        compiler_params=params(),
        name="translate",
    )(held(everywhere), held(factor.reshape(n_off * 16, 128)))
    back = lax.all_to_all(back, "box", 0, 0)
    shape = jax.ShapeDtypeStruct((parents, band, 2, n_p2), f32)
    outgoing = pl.pallas_call(
        place_rows_kernel,
        in_specs=[vmem()],
        out_specs=vmem(),
        out_shape=shape,
        compiler_params=params(),
        cost_estimate=pl.CostEstimate(flops=10**6, bytes_accessed=4 * 10**6, transcendentals=0),
        name="place_rows",
    )(outgoing)
    incoming = pl.pallas_call(
        place_kernel,
        in_specs=[vmem()],
        out_specs=vmem(),
        out_shape=shape,
        scratch_shapes=[pltpu.VMEM((8 * parents, 128), f32)],
        compiler_params=params(),
        name="place",
    )(held(back))
    return outgoing.transpose(0, 2, 1, 3), incoming.transpose(0, 2, 1, 3)


def solution(mesh):
    in_specs = (
        P(("box", "samp"), None, None, None),
        P(("box", "samp")),
        P("box", None),
        P("box", None),
        P("box", None),
        P(None, None, "samp", None),
    )
    out_specs = (P("box", None, "samp", None), P("box", None, "samp", None))
    return jax.shard_map(shards, mesh=mesh, in_specs=in_specs, out_specs=out_specs, check_vma=False)
```

time: 1070 us -> 148 us (0.14)
  waiting for transfers between devices: 520 us -> 48 us
  local copies, waits for them, and re-layouts: 279 us -> 8.91 us
  other arithmetic: 234 us -> 0.98 us
  Pallas kernels: 0 us -> 51.4 us
  blocking collectives: 0 us -> 27.3 us
  matrix products: 20.1 us -> 0 us
  between operations: 14.8 us -> 0.79 us
    unnamed x3 -> x0, waiting for transfers between devices: 403 us -> none
    gather x12 -> x0, local copies, waits for them, and re-layouts: 242 us -> none  [the longest x6 123 us: add_block(): factor = jnp.take(table, kinds, axis=0)]
    all_gather x1 -> x0, waiting for transfers between devices: 117 us -> none  [shards(): lax.all_gather(outgoing.reshape(parents, 2, band * n_phi), 'box', axis=0,...]
    reduce_sum x6 -> x0, other arithmetic: 116 us -> none  [add_block(): jnp.sum(factor[:, :, 0] * source[:, :, 0] - factor[:, :, 1] * source[:, :...]
    select_n x15 -> x0, other arithmetic: 97.7 us -> none  [the longest x6 55.3 us: add_block(): source = jnp.take(everywhere, ids, axis=0)]
    pallas_call x0 -> x6, Pallas kernels: none -> 51.4 us  [the longest x1 25.5 us: shards(): pl.pallas_call(translate_kernel, in_specs=[vmem(), vmem()], out_specs=any...]
    all_to_all x0 -> x2, waiting for transfers between devices: none -> 48 us  [the longest x1 30.5 us: shards(): bands = lax.all_to_all(bands, 'samp', 0, 0)]
    all_to_all x0 -> x1, blocking collectives: none -> 27.3 us  [shards(): everywhere = lax.all_to_all(send, 'box', 0, 0)]
  transfers between devices with their start and end apart: 2 -> 2, of which waited for: 2 -> 2; matrix products, arithmetic and copies ran while one was open for 0% -> 1% of each run, Pallas kernels for 0% -> 6%
where the time goes in v1:
time: 148 us; the launch traced here: 147 us
  Pallas kernels  51.4 us (35%)
  waiting for transfers between devices  48 us (32%)
  blocking collectives  27.3 us (18%)
  starting transfers between devices  9.8 us (7%)
  local copies, waits for them, and re-layouts  8.91 us (6%)
    all_to_all x1, waiting for transfers between devices, shards(): bands = lax.all_to_all(bands, 'samp', 0, 0)  30.5 us
    all_to_all x1, blocking collectives, shards(): everywhere = lax.all_to_all(send, 'box', 0, 0)  27.3 us
    pallas_call x1, Pallas kernels, shards(): pl.pallas_call(translate_kernel, in_specs=[vmem(), vmem()], out_specs=any...  25.5 us
    all_to_all x1, waiting for transfers between devices, shards(): back = lax.all_to_all(back, 'box', 0, 0)  17.5 us
    pallas_call x1, Pallas kernels, shards(): pl.pallas_call(phi_kernel, in_specs=[smem()] + [vmem()] * 6, out_specs=[a...  9.36 us
    unnamed x38, local copies, waits for them, and re-layouts  8.83 us
    pallas_call x1, Pallas kernels, shards(): pl.pallas_call(prepare_kernel, in_specs=[smem(), vmem(), anywhere()] + [v...  7.63 us
    pallas_call x1, Pallas kernels, shards(): pl.pallas_call(theta_kernel, in_specs=[smem()] + [anywhere()] * 3, out_sp...  6.36 us
  transfers between devices with their start and end apart: 2, of which 2 were waited for; matrix products, arithmetic and copies ran while one was open for 1% of the time, Pallas kernels for 6%

profile of v1, /device:TPU:32, one launch (start us, length us, event | category | flops | bytes accessed | tf_op | source)
XLA Modules:
  0.0 147.2 jit_solution(1962882012174002553)
XLA Ops:
  0.6 0.6 copy-done.12
  1.3 6.4 %theta.1 = (f32[16,200,256]{2,1,0:T(8,128)}, f32[8,128]{1,0:T(8,128)S(1)}) custom-call(s32[8]{0:T(128)S(1)} %copy-done.12, bf16[384,256]{1,0:T(8,128)(2,1)} %constant.39.clone.table_high, bf16[384,256]{1,0:T(8,128)(2,1)} %constant.40.clone.table_low, f32[8,2,128,256]{3,2,1,0:T(8,128)} %child.1), custom_call_target="tpu_custom_call" | custom-call | tf_op jit(solution)/shard_map/theta/pallas_call | solution.py:339
  7.7 0.0 copy-start.18
  7.7 0.0 copy-start.17
  7.7 0.0 copy-start.15
  7.7 0.0 copy-start.16
  7.7 6.1 %all-to-all-start = ((f32[16,200,256]{2,1,0:T(8,128)}), f32[16,200,256]{2,1,0:T(8,128)S(1)}, u32[]{:S(2)}, u32[]{:S(2)}) async-start(f32[16,200,256]{2,1,0:T(8,128)} %get-tuple-element.16), calls=%async_computation | async-start | bytes 6553600 | tf_op jit(solution)/shard_map/all_to_all | solution.py:353
  13.8 0.1 pad.2.clone
  13.9 0.0 copy-done.18
  13.9 0.1 broadcast_multiply_fusion.2
  14.0 0.8 sine_multiply_fusion
  14.8 0.0 copy-start.9
  14.8 0.9 copy-done.9
  15.7 0.9 copy-done.10
  16.7 7.6 %prepare.1 = (f32[316,16,128]{2,1,0:T(8,128)S(1)}, bf16[256,384]{1,0:T(8,128)(2,1)S(1)}, bf16[256,384]{1,0:T(8,128)(2,1)S(1)}, f32[8,16,384]{2,1,0:T(8,128)S(1)}, f32[8,16,384]{2,1,0:T(8,128)S(1)}) custom-call(s32[1]{0:T(128)} %bitcast.1.box, f32[8,128]{1,0:T(8,128)S(1)} %get-tuple-element.11.token, f32[316,12,2,384]{3,2,1,0:T(2,128)} %bitcast.8, ...), custom_call_target="tpu_custom_call" | custom-call | flops 10000000 | bytes 10000000 | tf_op jit(solution)/shard_map/prepare/pallas_call | solution.py:356
  24.3 1.5 copy-done
  25.8 0.7 copy-done.3
  26.4 0.7 copy-done.5
  27.1 0.7 copy-done.7
  27.8 0.1 add_convert_fusion.lists
  27.9 30.5 %all-to-all-done.recv = f32[16,200,256]{2,1,0:T(8,128)S(1)} async-done(((f32[16,200,256]{2,1,0:T(8,128)}), f32[16,200,256]{2,1,0:T(8,128)S(1)}, u32[]{:S(2)}, u32[]{:S(2)}) %all-to-all-start) | async-done | bytes 3276832 | tf_op jit(solution)/shard_map/all_to_all | solution.py:353
  58.4 0.9 copy-done.4
  59.3 0.9 copy-done.6
  60.3 0.9 copy-done.8
  61.2 9.4 %phi.1 = (f32[2304,128]{1,0:T(8,128)}, f32[8,320,128]{2,1,0:T(8,128)}) custom-call(s32[128]{0:T(128)S(1)} %bitcast.7, f32[32,128]{1,0:T(8,128)S(1)} %add_convert_fusion.lists, bf16[256,384]{1,0:T(8,128)(2,1)S(1)} %get-tuple-element.12.table_high, bf16[256,384]{1,0:T(8,128)(2,1)S(1)} %copy-done.4, f32[8,16,384]{2,1,0:T(8,128)S(1)} %copy-done.6, ...), custom_call_target="tpu_custom_call" | custom-call | tf_op jit(solution)/shard_map/phi/pallas_call | solution.py:374
  70.6 27.3 %all_to_all.15.recv = f32[8,320,128]{2,1,0:T(8,128)S(1)} all-to-all(f32[8,320,128]{2,1,0:T(8,128)} %get-tuple-element.18), channel_id=1, replica_groups=mesh['box'=8,'samp'=16] {'box'}, dimensions={0} | all-to-all | bytes 2621440 | tf_op jit(solution)/shard_map/all_to_all | solution.py:391
  97.9 25.5 %translate.1 = f32[8,288,128]{2,1,0:T(8,128)} custom-call(f32[8,320,128]{2,1,0:T(8,128)S(1)} %all_to_all.15.recv, f32[5056,128]{1,0:T(8,128)S(1)} %bitcast.6), custom_call_target="tpu_custom_call" | custom-call | tf_op jit(solution)/shard_map/translate/pallas_call | solution.py:393
  123.4 0.0 copy-start.2
  123.5 3.7 %all-to-all-start.2 = ((f32[8,288,128]{2,1,0:T(8,128)}), f32[8,288,128]{2,1,0:T(8,128)S(1)}, u32[]{:S(2)}, u32[]{:S(2)}) async-start(f32[8,288,128]{2,1,0:T(8,128)} %translate.1), calls=%async_computation.2 | async-start | bytes 2359296 | tf_op jit(solution)/shard_map/all_to_all | solution.py:409
  127.2 1.2 place_rows.1
  128.4 17.5 %all-to-all-done.2.recv = f32[8,288,128]{2,1,0:T(8,128)S(1)} async-done(((f32[8,288,128]{2,1,0:T(8,128)}), f32[8,288,128]{2,1,0:T(8,128)S(1)}, u32[]{:S(2)}, u32[]{:S(2)}) %all-to-all-start.2) | async-done | bytes 1179680 | tf_op jit(solution)/shard_map/all_to_all | solution.py:409
  145.9 1.3 place.1
  (24 shorter events, 0.1 us)
Async XLA Ops:
  0.6 0.7 copy-start.12
  7.7 6.2 %copy-start.18 = (s32[16]{0:T(128)S(1)}, s32[16]{0:T(128)}, u32[]{:S(2)}) copy-start(s32[16]{0:T(128)} %constant.41.clone) | copy-start | bytes 196
  7.7 6.3 %copy-start.17 = (f32[8]{0:T(128)S(1)}, f32[8]{0:T(128)}, u32[]{:S(2)}) copy-start(f32[8]{0:T(128)} %constant.52) | copy-start | bytes 100
  7.7 6.3 %copy-start.15 = (f32[8,384]{1,0:T(8,128)S(1)}, f32[8,384]{1,0:T(8,128)}, u32[]{:S(2)}) copy-start(f32[8,384]{1,0:T(8,128)} %constant.51) | copy-start | bytes 36868
  7.7 6.3 %copy-start.16 = (f32[16]{0:T(128)S(1)}, f32[16]{0:T(128)}, u32[]{:S(2)}) copy-start(f32[16]{0:T(128)} %constant.53) | copy-start | bytes 196
  7.7 50.7 %all-to-all-start = ((f32[16,200,256]{2,1,0:T(8,128)}), f32[16,200,256]{2,1,0:T(8,128)S(1)}, u32[]{:S(2)}, u32[]{:S(2)}) async-start(f32[16,200,256]{2,1,0:T(8,128)} %get-tuple-element.16), calls=%async_computation | async-start | bytes 6553600 | tf_op jit(solution)/shard_map/all_to_all | solution.py:353
  14.8 0.9 copy-start.9
  15.7 0.9 copy-start.10
  16.7 11.2 %copy-start.13 = (s32[32,48]{1,0:T(8,128)S(1)}, s32[32,48]{1,0:T(8,128)}, u32[]{:S(2)}) copy-start(s32[32,48]{1,0:T(8,128)} %param.18) | copy-start | bytes 18436
  16.7 11.2 %copy-start.14 = (s32[32,48]{1,0:T(8,128)S(1)}, s32[32,48]{1,0:T(8,128)}, u32[]{:S(2)}) copy-start(s32[32,48]{1,0:T(8,128)} %param.17) | copy-start | bytes 18436
  16.7 41.7 %copy-start.11 = (s32[1,128]{1,0:T(1,128)S(1)}, s32[1,128]{1,0:T(1,128)}, u32[]{:S(2)}) copy-start(s32[1,128]{1,0:T(1,128)} %param.16) | copy-start | bytes 1540
  24.3 1.5 copy-start
  25.8 0.7 copy-start.3
  26.4 0.7 copy-start.5
  27.1 0.7 copy-start.7
  58.4 0.9 copy-start.4
  59.3 0.9 copy-start.6
  60.3 0.9 copy-start.8
  70.6 27.3 %copy-start.1 = (f32[316,16,128]{2,1,0:T(8,128)S(1)}, f32[316,16,128]{2,1,0:T(8,128)}, u32[]{:S(2)}) copy-start(f32[316,16,128]{2,1,0:T(8,128)} %copy-done) | copy-start | bytes 7766020
  123.4 3.7 %copy-start.2 = (f32[2304,128]{1,0:T(8,128)S(1)}, f32[2304,128]{1,0:T(8,128)}, u32[]{:S(2)}) copy-start(f32[2304,128]{1,0:T(8,128)} %get-tuple-element.17.rows) | copy-start | bytes 3538948
  123.5 22.4 %all-to-all-start.2 = ((f32[8,288,128]{2,1,0:T(8,128)}), f32[8,288,128]{2,1,0:T(8,128)S(1)}, u32[]{:S(2)}, u32[]{:S(2)}) async-start(f32[8,288,128]{2,1,0:T(8,128)} %translate.1), calls=%async_computation.2 | async-start | bytes 2359296 | tf_op jit(solution)/shard_map/all_to_all | solution.py:409

commit v2 on v1

--- a/solution.py
+++ b/solution.py
@@ -54,7 +54,7 @@
     return f(a[0], b[0]) + (f(a[0], b[1]) + f(a[1], b[0]))
 
 
-def theta_kernel(octants, table_high, table_low, child, out, token, tables, kids, bands, sems):
+def theta_kernel(octants, table_high, table_low, child, out, token, tables, kids, bands, kinds, sems):
     n_kids, n_samp = child.shape[0], out.shape[0]
     loads = [pltpu.make_async_copy(child.at[c], kids.at[c], sems.at[c]) for c in range(n_kids)]
     loads[0].start()
@@ -64,35 +64,43 @@
     ]
     for copy in parts:
         copy.start()
+    small = pltpu.make_async_copy(octants, kinds, sems.at[n_kids + 2])
+    small.start()
     for copy in loads[1:]:
         copy.start()
-    row = lax.broadcasted_iota(jnp.int32, (8, out.shape[2]), 0)
-    v = jnp.zeros((8, out.shape[2]), jnp.int32)
+    small.wait()
+    row = lax.broadcasted_iota(jnp.int32, (8, 128), 0)
+    v = jnp.zeros((8, 128), jnp.int32)
     for i in range(8):
-        v = jnp.where(row == i, octants[i], v)
+        v = jnp.where(row == i, kinds[0, i], v)
     v = v.astype(jnp.float32)
     for s in range(n_samp):
-        bands[s, 192:200, :] = v
-    token[...] = v[:, 0:128]
+        bands[s, 384:392, :] = v
+    token[...] = v
+    stores = []
+
+    def store(first, count):
+        rows = pl.ds(first, count)
+        stores.append(pltpu.make_async_copy(bands.at[:, rows], out.at[:, rows], sems.at[n_kids + 3 + len(stores)]))
+        stores[-1].start()
+
     for copy in parts:
         copy.wait()
-    stores = []
     for c in range(n_kids):
         loads[c].wait()
         x = split(kids[c].reshape(kids.shape[1] * kids.shape[2], kids.shape[3]))
         y = dot3((tables[0], tables[1]), x)
         for s in range(n_samp):
-            bands[s, 24 * c : 24 * c + 24, :] = y[24 * s : 24 * s + 24]
+            bands[s, 24 * c : 24 * c + 24, :] = y[24 * s : 24 * s + 24, 0:128]
+            bands[s, 192 + 24 * c : 216 + 24 * c, :] = y[24 * s : 24 * s + 24, 128:256]
         if c % 2:
-            first, last = 24 * (c - 1), 24 * (c + 1) + (8 if c == n_kids - 1 else 0)
-            rows = pl.ds(first, last - first)
-            stores.append(pltpu.make_async_copy(bands.at[:, rows], out.at[:, rows], sems.at[n_kids + 2 + c // 2]))
-            stores[-1].start()
+            store(24 * (c - 1), 48)
+            store(192 + 24 * (c - 1), 48 + 8 * (c == n_kids - 1))
     for copy in stores:
         copy.wait()
 
 
-def prepare_kernel(box, token, table, high, low, cos, sin, out, high_out, low_out, cos_out, sin_out, raw, sems):
+def prepare_kernel(box, token, table, out, done, raw, sems):
     me = box[0]
     n_off = table.shape[0]
     pair, half = me // 2, me % 2
@@ -104,8 +112,7 @@
             pltpu.make_async_copy(table.at[:, at // 3, :, lanes], raw.at[:, q], sems.at[q])
         )
         copies[-1].start()
-    high_out[...], low_out[...] = high[...], low[...]
-    cos_out[...], sin_out[...] = cos[...], sin[...]
+    done[...] = token[...]
     for copy in copies:
         copy.wait()
     left = lax.broadcasted_iota(jnp.int32, (1, 128), 1) < 64
@@ -122,30 +129,54 @@
     lax.fori_loop(0, n_off // 4, lambda i, c: [one(4 * i + u, c) for u in range(4)][-1], 0)
 
 
-def phi_kernel(owners, lists, table_high, table_low, cos_ref, sin_ref, recv, outgoing, send, total, rows_v, send_v, kinds_v, kinds, sems):
+def phi_kernel(
+    owners, token, lists, table_high, table_low, cos_hbm, sin_hbm, recv, outgoing, send,
+    total, fine, rows_v, send_v, tables, cos_ref, sin_ref, kinds_v, kinds, sems,
+):
+    pairs = [(table_high, tables.at[0]), (table_low, tables.at[1]), (cos_hbm, cos_ref), (sin_hbm, sin_ref)]
+    loads = [pltpu.make_async_copy(a, b, sems.at[i]) for i, (a, b) in enumerate(pairs)]
+    for copy in loads:
+        copy.start()
     for s in range(16):
-        kinds_v[8 * s : 8 * s + 8, :] = recv[s, 192:200, 0:128].astype(jnp.int32)
-    copy = pltpu.make_async_copy(kinds_v, kinds, sems.at[0])
+        kinds_v[8 * s : 8 * s + 8, :] = recv[s, 384:392, :].astype(jnp.int32)
+    copy = pltpu.make_async_copy(kinds_v, kinds, sems.at[4])
     copy.start()
     total[...] = jnp.zeros_like(total)
     for d in range(8):
-        send_v[d, 288:320, :] = lists[...]
-    copy.wait()
-
-    def source(s, carry):
-        fine = dot3(split(recv[s, 0:192, :]), (table_high[...], table_low[...]))
+        send_v[d, 288:312, :] = lists[...]
+    for load in loads[:2]:
+        load.wait()
+    table = jnp.concatenate([tables[0], tables[0], tables[1]], 0)
+
+    def product(s):
+        high, low = split(jnp.concatenate([recv[s, 0:192, :], recv[s, 192:384, :]], 1))
+        return jnp.dot(jnp.concatenate([high, low, high], 1), table, preferred_element_type=jnp.float32)
+
+    def add(s, fine):
         for c in range(8):
             child = s * 8 + c
             owner, octant = owners[child], kinds[child, 0]
-            f = fine[24 * c : 24 * c + 24]
+            f = fine[24 * c : 24 * c + 24, :]
             cos_0, sin_0 = cos_ref[octant, 0:8], sin_ref[octant, 0:8]
             total[owner, 0:8] += cos_0 * f[0:8] - sin_0 * f[8:16]
             total[owner, 8:16] += sin_0 * f[0:8] + cos_0 * f[8:16]
             swapped = pltpu.roll(f[16:24], 4, 0)
             total[owner, 16:24] += cos_ref[octant, 8:16] * f[16:24] + sin_ref[octant, 8:16] * swapped
-        return carry
-
-    lax.fori_loop(0, 16, source, 0)
+
+    fine[0] = product(0)
+    for load in loads[2:]:
+        load.wait()
+    copy.wait()
+
+    def two(i, carry):
+        s = 2 * i
+        fine[1] = product(s + 1)
+        add(s, fine.at[0])
+        fine[0] = product(lax.rem(s + 2, 16))
+        add(s + 1, fine.at[1])
+        return carry
+
+    lax.fori_loop(0, 8, two, 0, unroll=2)
 
     def parent(p, carry):
         for l in range(3):
@@ -165,7 +196,10 @@
     for q in range(4):
         lax.fori_loop(8 * q, 8 * q + 8, parent, 0)
         rows = pl.ds(64 * q, 64)
-        copies.append(pltpu.make_async_copy(send_v.at[:, rows], send.at[:, rows], sems.at[1 + q]))
+        copies.append(pltpu.make_async_copy(send_v.at[:, rows], send.at[:, rows], sems.at[5 + q]))
+        copies[-1].start()
+        rows = pl.ds(576 * q, 576)
+        copies.append(pltpu.make_async_copy(rows_v.at[rows], outgoing.at[rows], sems.at[9 + q]))
         copies[-1].start()
         for r in range(4):
             at = 72 * 8 * q + 64 + 2 * r
@@ -173,80 +207,83 @@
             rows = slice(256 + 8 * q, 264 + 8 * q)
             send_v[2 * r, rows, :] = jnp.where(left, re, pltpu.roll(im, 64, 1))
             send_v[2 * r + 1, rows, :] = jnp.where(left, pltpu.roll(re, 64, 1), im)
-    rows = pl.ds(256, 64)
-    copies.append(pltpu.make_async_copy(send_v.at[:, rows], send.at[:, rows], sems.at[5]))
-    copies[-1].start()
-    copies.append(pltpu.make_async_copy(rows_v, outgoing, sems.at[6]))
+    rows = pl.ds(256, 56)
+    copies.append(pltpu.make_async_copy(send_v.at[:, rows], send.at[:, rows], sems.at[13]))
     copies[-1].start()
     for copy in copies:
         copy.wait()
 
 
-def translate_kernel(recv, factor, send, source, sums, send_v, idx_v, idx, sems):
-    copies = []
+def translate_kernel(recv, factor, send, source, sums, send_v, idx_v, idx, load_sems, store_sems):
+    n_far, n_own = 48, 32
+    loads = []
     for b in range(8):
-        rows = pl.ds(32 * b, 32)
-        idx_v[rows, :] = recv[b, 288:320, :].astype(jnp.int32)
-        copies.append(pltpu.make_async_copy(idx_v.at[rows], idx.at[rows], sems.at[b]))
-        copies[-1].start()
+        rows = pl.ds(24 * b, 24)
+        idx_v[rows, :] = recv[b, 288:312, :].astype(jnp.int32)
+        loads.append(pltpu.make_async_copy(idx_v.at[rows], idx.at[rows], load_sems.at[b]))
+        loads[-1].start()
     left = lax.broadcasted_iota(jnp.int32, (8, 128), 1) < 64
     even = lax.broadcasted_iota(jnp.int32, (8, 128), 0) % 2 == 0
     for b in range(8):
 
         def prepare(p, carry):
             v = recv[b, pl.ds(pl.multiple_of(8 * p, 8), 8), :]
-            at = pl.multiple_of((b * 32 + p) * 24, 8)
+            at = pl.multiple_of((b * n_own + p) * 24, 8)
             source[pl.ds(at, 8), :] = jnp.where(even, v, pltpu.roll(v, 1, 0))
             source[pl.ds(at + 8, 8), :] = jnp.where(even, pltpu.roll(v, 7, 0), v)
             return carry
 
-        lax.fori_loop(0, 32, prepare, 0, unroll=8)
+        lax.fori_loop(0, n_own, prepare, 0, unroll=8)
         for q in range(4):
             v = recv[b, 256 + 8 * q : 264 + 8 * q, :]
             r = pltpu.roll(v, 64, 1)
-            at = (b * 32 + 8 * q) * 24 + 16
+            at = (b * n_own + 8 * q) * 24 + 16
             source[pl.ds(at, 8, stride=24), :] = jnp.where(left, v, r)
             source[pl.ds(at + 1, 8, stride=24), :] = jnp.where(left, r, v)
 
-    n_far = 48
-
-    def one(row, carry):
-        acc = [jnp.zeros((8, 128), jnp.float32) for _ in range(3)]
+    def index(j, b, p):
+        return pl.multiple_of(idx.at[pl.ds(j // 4, 169), pl.ds(n_own * (j % 4), n_own)][24 * b, p], 8)
+
+    def some(i, b):
+        acc = [[jnp.zeros((8, 128), jnp.float32) for _ in range(3)] for _ in range(4)]
         for j in range(n_far):
-            f = pl.multiple_of(idx[row, j], 8)
-            o = pl.multiple_of(idx[row, n_far + j], 8)
-            t = factor[pl.ds(o, 8), :]
-            acc[0] += t * source[pl.ds(f, 8), :]
-            acc[1] += t * source[pl.ds(f + 8, 8), :]
-            acc[2] += factor[pl.ds(o + 8, 8), :] * source[pl.ds(f + 16, 8), :]
-        for k in range(3):
-            sums[pl.ds(pl.multiple_of(24 * row, 8) + 8 * k, 8), :] = acc[k]
-        return carry
+            for h in range(4):
+                f, o = index(j, b, 4 * i + h), index(n_far + j, b, 4 * i + h)
+                t = factor[pl.ds(o, 8), :]
+                acc[h][0] += t * source[pl.ds(f, 8), :]
+                acc[h][1] += t * source[pl.ds(f + 8, 8), :]
+                acc[h][2] += factor[pl.ds(o + 8, 8), :] * source[pl.ds(f + 16, 8), :]
+        for h in range(4):
+            for k in range(3):
+                sums[pl.ds(pl.multiple_of(24 * (b * n_own + 4 * i), 8) + 24 * h + 8 * k, 8), :] = acc[h][k]
+        return b
 
     def finish(p, b):
-        at = pl.multiple_of((b * 32 + p) * 24, 8)
+        at = pl.multiple_of((b * n_own + p) * 24, 8)
         r = sums[pl.ds(at + 8, 8), :]
         r = jnp.where(even, -pltpu.roll(r, 7, 0), pltpu.roll(r, 1, 0))
         send_v[b, pl.ds(pl.multiple_of(8 * p, 8), 8), :] = sums[pl.ds(at, 8), :] + r
         return b
 
-    for copy in copies:
-        copy.wait()
-    lax.fori_loop(0, 256, one, 0)
-    copies = []
-    for b in range(8):
-        lax.fori_loop(0, 32, finish, b, unroll=8)
+    def store(b):
+        return pltpu.make_async_copy(send_v.at[pl.ds(b, 1)], send.at[pl.ds(b, 1)], store_sems.at[b])
+
+    def box(b, carry):
+        rows = pl.ds(pl.multiple_of(24 * b, 8), 24)
+        pltpu.make_async_copy(idx_v.at[rows], idx.at[rows], load_sems.at[b]).wait()
+        lax.fori_loop(0, n_own // 4, some, b)
+        lax.fori_loop(0, n_own, finish, b, unroll=8)
         for q in range(4):
-            at = (b * 32 + 8 * q) * 24 + 16
+            at = (b * n_own + 8 * q) * 24 + 16
             r = pltpu.roll(sums[pl.ds(at + 1, 8, stride=24), :], 64, 1)
             rows = slice(256 + 8 * q, 264 + 8 * q)
             send_v[b, rows, :] = sums[pl.ds(at, 8, stride=24), :] + jnp.where(left, -r, r)
-        if b % 2:
-            two = pl.ds(b - 1, 2)
-            copies.append(pltpu.make_async_copy(send_v.at[two], send.at[two], sems.at[8 + b // 2]))
-            copies[-1].start()
-    for copy in copies:
-        copy.wait()
+        store(b).start()
+        return carry
+
+    lax.fori_loop(0, 8, box, 0)
+    for b in range(8):
+        store(b).wait()
 
 
 def place_rows_kernel(rows, out):
@@ -335,58 +372,60 @@
     theta_high, theta_low = high_low(both.reshape(n_samp * 24, 2 * n_t1))
     phi_high, phi_low = high_low(lagrange_table(n_p1, n_p2, True).T)
 
-    sent = (n_samp, 24 * count + 8, n_p1)
+    sent = (n_samp, 48 * count + 8, 128)
     bands, token = pl.pallas_call(
         theta_kernel,
-        in_specs=[smem()] + [anywhere()] * 3,
+        in_specs=[anywhere()] * 4,
         out_specs=[anywhere(), vmem()],
         out_shape=[pltpu.HBM(sent, f32), jax.ShapeDtypeStruct((8, 128), f32)],
         scratch_shapes=[
             pltpu.VMEM((2, n_samp * 24, 2 * n_t1), bf16),
             pltpu.VMEM(child_patterns.shape, f32),
             pltpu.VMEM(sent, f32),
-            pltpu.SemaphoreType.DMA((count + 2 + count // 2,)),
+            pltpu.SMEM((1, count), jnp.int32),
+            pltpu.SemaphoreType.DMA((2 * count + 3,)),
         ],
         compiler_params=params(),
         name="theta",
-    )(octants, far_away(theta_high), far_away(theta_low), far_away(child_patterns))
+    )(far_away(octants.reshape(1, count)), far_away(theta_high), far_away(theta_low), far_away(child_patterns))
     bands = lax.all_to_all(bands, "samp", 0, 0)
 
     cos_part, sin_part = phase_tables(samp, n_t2, n_p2)
-    factor, *tables = pl.pallas_call(
+    factor, token = pl.pallas_call(
         prepare_kernel,
-        in_specs=[smem(), vmem(), anywhere()] + [vmem()] * 4,
-        out_specs=[vmem()] * 5,
-        out_shape=[
-            pltpu.VMEM((n_off, 16, 128), f32),
-            pltpu.VMEM(phi_high.shape, bf16),
-            pltpu.VMEM(phi_high.shape, bf16),
+        in_specs=[smem(), vmem(), anywhere()],
+        out_specs=[vmem()] * 2,
+        out_shape=[pltpu.VMEM((n_off, 16, 128), f32), jax.ShapeDtypeStruct((8, 128), f32)],
+        scratch_shapes=[pltpu.VMEM((n_off, 5, 2, 128), f32), pltpu.SemaphoreType.DMA((5,))],
+        compiler_params=params(),
+        cost_estimate=pl.CostEstimate(flops=10**7, bytes_accessed=10**7, transcendentals=0),
+        name="prepare",
+    )(box.reshape(1), token, far_away(translation.transpose(0, 2, 1, 3)))
+    lists = jnp.concatenate([far_boxes.T * 24, offsets.T * 16], 0).reshape(24, 128)
+
+    outgoing, send = pl.pallas_call(
+        phi_kernel,
+        in_specs=[smem(), vmem(), vmem()] + [anywhere()] * 4 + [vmem()],
+        out_specs=[anywhere()] * 2,
+        out_shape=[pltpu.HBM((parents * 72, 128), f32), pltpu.HBM((n_box, 9 * parents + 24, 128), f32)],
+        scratch_shapes=[
+            pltpu.VMEM((parents, 24, n_p2), f32),
+            pltpu.VMEM((2, 24 * count, n_p2), f32),
+            pltpu.VMEM((parents * 72, 128), f32),
+            pltpu.VMEM((n_box, 9 * parents + 24, 128), f32),
+            pltpu.VMEM((2, n_p1, n_p2), bf16),
             pltpu.VMEM(cos_part.shape, f32),
             pltpu.VMEM(cos_part.shape, f32),
-        ],
-        scratch_shapes=[pltpu.VMEM((n_off, 5, 2, 128), f32), pltpu.SemaphoreType.DMA((5,))],
-        compiler_params=params(),
-        cost_estimate=pl.CostEstimate(flops=10**7, bytes_accessed=10**7, transcendentals=0),
-        name="prepare",
-    )(box.reshape(1), token, far_away(translation.transpose(0, 2, 1, 3)), phi_high, phi_low, cos_part, sin_part)
-    lists = jnp.concatenate([far_boxes * 24, offsets * 16, jnp.zeros((parents, 128 - 2 * n_far), jnp.int32)], 1)
-
-    outgoing, send = pl.pallas_call(
-        phi_kernel,
-        in_specs=[smem()] + [vmem()] * 6,
-        out_specs=[anywhere()] * 2,
-        out_shape=[pltpu.HBM((parents * 72, 128), f32), pltpu.HBM((n_box, 10 * parents, 128), f32)],
-        scratch_shapes=[
-            pltpu.VMEM((parents, 24, n_p2), f32),
-            pltpu.VMEM((parents * 72, 128), f32),
-            pltpu.VMEM((n_box, 10 * parents, 128), f32),
             pltpu.VMEM((n_samp * count, 128), jnp.int32),
             pltpu.SMEM((n_samp * count, 128), jnp.int32),
-            pltpu.SemaphoreType.DMA((7,)),
+            pltpu.SemaphoreType.DMA((14,)),
         ],
         compiler_params=params(),
         name="phi",
-    )(parent_map[0], lists.astype(f32), *[held(x) for x in tables], held(bands))
+    )(
+        parent_map[0], token, lists.astype(f32),
+        *[far_away(x) for x in (phi_high, phi_low, cos_part, sin_part)], held(bands),
+    )
 
     everywhere = lax.all_to_all(send, "box", 0, 0)
     n_all = n_box * parents
@@ -399,9 +438,10 @@
             pltpu.VMEM((n_all * 24, 128), f32),
             pltpu.VMEM((n_all * 24, 128), f32),
             pltpu.VMEM((n_box, 9 * parents, 128), f32),
-            pltpu.VMEM((n_all, 128), jnp.int32),
-            pltpu.SMEM((n_all, 128), jnp.int32),
-            pltpu.SemaphoreType.DMA((12,)),
+            pltpu.VMEM((24 * n_box, 128), jnp.int32),
+            pltpu.SMEM((24 * n_box, 128), jnp.int32),
+            pltpu.SemaphoreType.DMA((n_box,)),
+            pltpu.SemaphoreType.DMA((n_box,)),
         ],
         compiler_params=params(),
         name="translate",

time: 148 us -> 132 us (0.89)
  Pallas kernels: 51.4 us -> 41.4 us
  local copies, waits for them, and re-layouts: 8.91 us -> 1.71 us
  waiting for transfers between devices: 48 us -> 49.5 us
    pallas_call x1, Pallas kernels: 25.5 us -> 18.1 us  [shards(): pl.pallas_call(translate_kernel, in_specs=[vmem(), vmem()], out_specs=any...]
    unnamed x38 -> x20, local copies, waits for them, and re-layouts: 8.83 us -> 1.55 us
    pallas_call x3, Pallas kernels: 23.4 us -> 20.8 us  [the longest x1 7.62 us: shards(): pl.pallas_call(prepare_kernel, in_specs=[smem(), vmem(), anywhere()], out...]
    all_to_all x1, waiting for transfers between devices: 30.5 us -> 32.6 us  [shards(): bands = lax.all_to_all(bands, 'samp', 0, 0)]
  transfers between devices with their start and end apart: 2 -> 2, of which waited for: 2 -> 2; matrix products, arithmetic and copies ran while one was open for 1% -> 1% of each run, Pallas kernels for 6% -> 7%
where the time goes in v2:
time: 132 us
  waiting for transfers between devices  49.5 us (38%)
  Pallas kernels  41.4 us (31%)
  blocking collectives  26.8 us (20%)
  starting transfers between devices  9.66 us (7%)
  other arithmetic  1.73 us (1%)
  local copies, waits for them, and re-layouts  1.71 us (1%)
    all_to_all x1, waiting for transfers between devices, shards(): bands = lax.all_to_all(bands, 'samp', 0, 0)  32.6 us
    all_to_all x1, blocking collectives, shards(): everywhere = lax.all_to_all(send, 'box', 0, 0)  26.8 us
    pallas_call x1, Pallas kernels, shards(): pl.pallas_call(translate_kernel, in_specs=[vmem(), vmem()], out_specs=any...  18.1 us
    all_to_all x1, waiting for transfers between devices, shards(): back = lax.all_to_all(back, 'box', 0, 0)  16.8 us
    pallas_call x1, Pallas kernels, shards(): pl.pallas_call(prepare_kernel, in_specs=[smem(), vmem(), anywhere()], out...  7.62 us
    pallas_call x1, Pallas kernels, shards(): pl.pallas_call(phi_kernel, in_specs=[smem(), vmem(), vmem()] + [anywhere(...  7.29 us
    all_to_all x1, starting transfers between devices, shards(): bands = lax.all_to_all(bands, 'samp', 0, 0)  5.96 us
    pallas_call x1, Pallas kernels, shards(): pl.pallas_call(theta_kernel, in_specs=[anywhere()] * 4, out_specs=[anywhe...  5.85 us
  transfers between devices with their start and end apart: 2, of which 2 were waited for; matrix products, arithmetic and copies ran while one was open for 1% of the time, Pallas kernels for 7%

profile of v2, /device:TPU:32, one launch (start us, length us, event | category | flops | bytes accessed | tf_op | source)
XLA Modules:
  0.0 131.6 jit_solution(12670298816129947288)
XLA Ops:
  0.6 5.9 %theta.1 = (f32[16,392,128]{2,1,0:T(8,128)}, f32[8,128]{1,0:T(8,128)S(1)}) custom-call(s32[1,8]{1,0:T(1,128)} %bitcast.16, bf16[384,256]{1,0:T(8,128)(2,1)} %constant.37.clone.table_high, bf16[384,256]{1,0:T(8,128)(2,1)} %constant.38.clone.table_low, f32[8,2,128,256]{3,2,1,0:T(8,128)} %child.1), custom_call_target="tpu_custom_call" | custom-call | tf_op jit(solution)/shard_map/theta/pallas_call | solution.py:376
  6.5 0.0 copy-start.4
  6.5 0.0 copy-start.5
  6.5 6.0 %all-to-all-start = ((f32[16,392,128]{2,1,0:T(8,128)}), f32[16,392,128]{2,1,0:T(8,128)S(1)}, u32[]{:S(2)}, u32[]{:S(2)}) async-start(f32[16,392,128]{2,1,0:T(8,128)} %get-tuple-element.10), calls=%async_computation | async-start | bytes 6422528 | tf_op jit(solution)/shard_map/all_to_all | solution.py:391
  12.5 0.0 copy-done.4
  12.5 0.0 copy-done.5
  12.5 0.1 add_convert_fusion
  12.6 0.1 copy.17
  12.7 0.1 convert_element_type.9.lists
  12.8 0.0 copy-start.8
  12.8 0.0 copy-start.6
  12.8 0.0 copy-start.7
  12.8 0.0 copy-start.3
  12.8 7.6 %prepare.1 = (f32[316,16,128]{2,1,0:T(8,128)S(1)}, f32[8,128]{1,0:T(8,128)S(1)}) custom-call(s32[1]{0:T(128)} %bitcast.1.box, f32[8,128]{1,0:T(8,128)S(1)} %get-tuple-element.8.token, f32[316,12,2,384]{3,2,1,0:T(2,128)} %bitcast.13), custom_call_target="tpu_custom_call" | custom-call | flops 10000000 | bytes 10000000 | tf_op jit(solution)/shard_map/prepare/pallas_call | solution.py:394
  20.4 0.0 copy-start
  20.4 1.5 %copy-done = f32[316,16,128]{2,1,0:T(8,128)} copy-done((f32[316,16,128]{2,1,0:T(8,128)}, f32[316,16,128]{2,1,0:T(8,128)S(1)}, u32[]{:S(2)}) %copy-start) | copy-done | bytes 2588696
  21.9 0.0 copy-done.9
  22.0 0.0 copy-done.8
  22.0 0.1 broadcast_multiply_fusion
  22.1 0.0 copy-done.6
  22.1 0.0 copy-done.7
  22.1 1.5 %sine_multiply_fusion = (f32[8,16,384]{2,1,0:T(8,128)}, f32[8,16,384]{2,1,0:T(8,128)}) fusion(f32[16]{0:T(128)S(1)} %copy-done.7, f32[8,16]{1,0:T(8,128)S(1)} %broadcast_multiply_fusion, f32[8,384]{1,0:T(8,128)S(1)} %copy-done.6, f32[16]{0:T(128)S(1)} %get-tuple-element.16), kind=kLoop, calls=%fused_computation | loop fusion | flops 196608 | bytes 406144 | tf_op jit(solution)/shard_map/mul | solution.py:332
  23.6 32.6 %all-to-all-done.recv = f32[16,392,128]{2,1,0:T(8,128)S(1)} async-done(((f32[16,392,128]{2,1,0:T(8,128)}), f32[16,392,128]{2,1,0:T(8,128)S(1)}, u32[]{:S(2)}, u32[]{:S(2)}) %all-to-all-start) | async-done | bytes 3211296 | tf_op jit(solution)/shard_map/all_to_all | solution.py:391
  56.2 7.3 %phi.1 = (f32[2304,128]{1,0:T(8,128)}, f32[8,312,128]{2,1,0:T(8,128)}) custom-call(s32[128]{0:T(128)S(1)} %bitcast.12, f32[8,128]{1,0:T(8,128)S(1)} %get-tuple-element.9.token, f32[24,128]{1,0:T(8,128)S(1)} %convert_element_type.9.lists, bf16[256,384]{1,0:T(8,128)(2,1)} %constant.43.clone.table_high, bf16[256,384]{1,0:T(8,128)(2,1)} %constant.44.clone.table_low, ...), custom_call_target="tpu_custom_call" | custom-call | tf_op jit(solution)/shard_map/phi/pallas_call | solution.py:406
  63.5 26.8 %all_to_all.15.recv = f32[8,312,128]{2,1,0:T(8,128)S(1)} all-to-all(f32[8,312,128]{2,1,0:T(8,128)} %get-tuple-element.12), channel_id=1, replica_groups=mesh['box'=8,'samp'=16] {'box'}, dimensions={0} | all-to-all | bytes 2555904 | tf_op jit(solution)/shard_map/all_to_all | solution.py:430
  90.4 0.0 copy-done.1
  90.4 18.1 %translate.1 = f32[8,288,128]{2,1,0:T(8,128)} custom-call(f32[8,312,128]{2,1,0:T(8,128)S(1)} %all_to_all.15.recv, f32[5056,128]{1,0:T(8,128)S(1)} %bitcast.11), custom_call_target="tpu_custom_call" | custom-call | tf_op jit(solution)/shard_map/translate/pallas_call | solution.py:432
  108.5 0.0 copy-start.2
  108.5 3.7 %all-to-all-start.2 = ((f32[8,288,128]{2,1,0:T(8,128)}), f32[8,288,128]{2,1,0:T(8,128)S(1)}, u32[]{:S(2)}, u32[]{:S(2)}) async-start(f32[8,288,128]{2,1,0:T(8,128)} %translate.1), calls=%async_computation.2 | async-start | bytes 2359296 | tf_op jit(solution)/shard_map/all_to_all | solution.py:449
  112.3 1.2 place_rows.1
  113.5 16.8 %all-to-all-done.2.recv = f32[8,288,128]{2,1,0:T(8,128)S(1)} async-done(((f32[8,288,128]{2,1,0:T(8,128)}), f32[8,288,128]{2,1,0:T(8,128)S(1)}, u32[]{:S(2)}, u32[]{:S(2)}) %all-to-all-start.2) | async-done | bytes 1179680 | tf_op jit(solution)/shard_map/all_to_all | solution.py:449
  130.3 1.3 %place.1 = f32[32,12,2,384]{3,2,1,0:T(2,128)} custom-call(f32[8,288,128]{2,1,0:T(8,128)S(1)} %all-to-all-done.2.recv), custom_call_target="tpu_custom_call" | custom-call | tf_op jit(solution)/shard_map/place/pallas_call | solution.py:460
  (6 shorter events, 0.1 us)
Async XLA Ops:
  6.5 6.0 %copy-start.4 = (s32[32,48]{1,0:T(8,128)S(1)}, s32[32,48]{1,0:T(8,128)}, u32[]{:S(2)}) copy-start(s32[32,48]{1,0:T(8,128)} %param.18) | copy-start | bytes 18436
  6.5 6.0 %copy-start.5 = (s32[32,48]{1,0:T(8,128)S(1)}, s32[32,48]{1,0:T(8,128)}, u32[]{:S(2)}) copy-start(s32[32,48]{1,0:T(8,128)} %param.17) | copy-start | bytes 18436
  6.5 49.7 %all-to-all-start = ((f32[16,392,128]{2,1,0:T(8,128)}), f32[16,392,128]{2,1,0:T(8,128)S(1)}, u32[]{:S(2)}, u32[]{:S(2)}) async-start(f32[16,392,128]{2,1,0:T(8,128)} %get-tuple-element.10), calls=%async_computation | async-start | bytes 6422528 | tf_op jit(solution)/shard_map/all_to_all | solution.py:391
  12.7 9.2 %copy-start.9 = (s32[16]{0:T(128)S(1)}, s32[16]{0:T(128)}, u32[]{:S(2)}) copy-start(s32[16]{0:T(128)} %constant.39.clone) | copy-start | bytes 196
  12.8 9.2 %copy-start.8 = (f32[8]{0:T(128)S(1)}, f32[8]{0:T(128)}, u32[]{:S(2)}) copy-start(f32[8]{0:T(128)} %constant.50) | copy-start | bytes 100
  12.8 9.3 %copy-start.6 = (f32[8,384]{1,0:T(8,128)S(1)}, f32[8,384]{1,0:T(8,128)}, u32[]{:S(2)}) copy-start(f32[8,384]{1,0:T(8,128)} %constant.49) | copy-start | bytes 36868
  12.8 9.3 %copy-start.7 = (f32[16]{0:T(128)S(1)}, f32[16]{0:T(128)}, u32[]{:S(2)}) copy-start(f32[16]{0:T(128)} %constant.51) | copy-start | bytes 196
  12.8 43.4 %copy-start.3 = (s32[1,128]{1,0:T(1,128)S(1)}, s32[1,128]{1,0:T(1,128)}, u32[]{:S(2)}) copy-start(s32[1,128]{1,0:T(1,128)} %param.16) | copy-start | bytes 1540
  20.4 1.5 %copy-start = (f32[316,16,128]{2,1,0:T(8,128)}, f32[316,16,128]{2,1,0:T(8,128)S(1)}, u32[]{:S(2)}) copy-start(f32[316,16,128]{2,1,0:T(8,128)S(1)} %get-tuple-element.13) | copy-start | bytes 7766020
  56.2 34.1 %copy-start.1 = (f32[316,16,128]{2,1,0:T(8,128)S(1)}, f32[316,16,128]{2,1,0:T(8,128)}, u32[]{:S(2)}) copy-start(f32[316,16,128]{2,1,0:T(8,128)} %copy-done) | copy-start | bytes 7766020
  108.5 3.7 %copy-start.2 = (f32[2304,128]{1,0:T(8,128)S(1)}, f32[2304,128]{1,0:T(8,128)}, u32[]{:S(2)}) copy-start(f32[2304,128]{1,0:T(8,128)} %get-tuple-element.11.rows) | copy-start | bytes 3538948
  108.5 21.7 %all-to-all-start.2 = ((f32[8,288,128]{2,1,0:T(8,128)}), f32[8,288,128]{2,1,0:T(8,128)S(1)}, u32[]{:S(2)}, u32[]{:S(2)}) async-start(f32[8,288,128]{2,1,0:T(8,128)} %translate.1), calls=%async_computation.2 | async-start | bytes 2359296 | tf_op jit(solution)/shard_map/all_to_all | solution.py:449

commit v3 on v2

--- a/solution.py
+++ b/solution.py
@@ -10,7 +10,6 @@
 from jax.sharding import PartitionSpec as P
 
 phase_scale = 12.0
-VMEM_LIMIT = 24 * 1024 * 1024
 
 
 def lagrange_table(n_old, n_new, periodic):
@@ -57,7 +56,6 @@
 def theta_kernel(octants, table_high, table_low, child, out, token, tables, kids, bands, kinds, sems):
     n_kids, n_samp = child.shape[0], out.shape[0]
     loads = [pltpu.make_async_copy(child.at[c], kids.at[c], sems.at[c]) for c in range(n_kids)]
-    loads[0].start()
     parts = [
         pltpu.make_async_copy(table, tables.at[i], sems.at[n_kids + i])
         for i, table in enumerate((table_high, table_low))
@@ -66,13 +64,13 @@
         copy.start()
     small = pltpu.make_async_copy(octants, kinds, sems.at[n_kids + 2])
     small.start()
-    for copy in loads[1:]:
+    for copy in loads:
         copy.start()
     small.wait()
-    row = lax.broadcasted_iota(jnp.int32, (8, 128), 0)
+    lane = lax.broadcasted_iota(jnp.int32, (8, 128), 1)
     v = jnp.zeros((8, 128), jnp.int32)
     for i in range(8):
-        v = jnp.where(row == i, kinds[0, i], v)
+        v = jnp.where(lane == i, kinds[0, i], v)
     v = v.astype(jnp.float32)
     for s in range(n_samp):
         bands[s, 384:392, :] = v
@@ -86,16 +84,21 @@
 
     for copy in parts:
         copy.wait()
+    table = jnp.concatenate([tables[0], tables[0], tables[1]], 1)
     for c in range(n_kids):
         loads[c].wait()
-        x = split(kids[c].reshape(kids.shape[1] * kids.shape[2], kids.shape[3]))
-        y = dot3((tables[0], tables[1]), x)
+        high, low = split(jnp.concatenate([kids[c, 0], kids[c, 1]], 1))
+        y = jnp.dot(table, jnp.concatenate([high, low, high], 0), preferred_element_type=jnp.float32)
         for s in range(n_samp):
-            bands[s, 24 * c : 24 * c + 24, :] = y[24 * s : 24 * s + 24, 0:128]
-            bands[s, 192 + 24 * c : 216 + 24 * c, :] = y[24 * s : 24 * s + 24, 128:256]
-        if c % 2:
-            store(24 * (c - 1), 48)
-            store(192 + 24 * (c - 1), 48 + 8 * (c == n_kids - 1))
+            for half in range(2):
+                at = 192 * half + 24 * c
+                for k in range(2):
+                    cols = slice(256 * k + 128 * half, 256 * k + 128 * half + 128)
+                    bands[s, at + 8 * k : at + 8 * k + 8, :] = y[8 * s : 8 * s + 8, cols]
+                    rest = y[128 + 4 * s : 132 + 4 * s, cols]
+                    bands[s, at + 16 + 4 * k : at + 20 + 4 * k, :] = rest
+        store(24 * c, 24)
+        store(192 + 24 * c, 24 + 8 * (c == n_kids - 1))
     for copy in stores:
         copy.wait()
 
@@ -130,7 +133,7 @@
 
 
 def phi_kernel(
-    owners, token, lists, table_high, table_low, cos_hbm, sin_hbm, recv, outgoing, send,
+    owners, token, lists, table_high, table_low, cos_hbm, sin_hbm, recv, send,
     total, fine, rows_v, send_v, tables, cos_ref, sin_ref, kinds_v, kinds, sems,
 ):
     pairs = [(table_high, tables.at[0]), (table_low, tables.at[1]), (cos_hbm, cos_ref), (sin_hbm, sin_ref)]
@@ -138,7 +141,7 @@
     for copy in loads:
         copy.start()
     for s in range(16):
-        kinds_v[8 * s : 8 * s + 8, :] = recv[s, 384:392, :].astype(jnp.int32)
+        kinds_v[s : s + 1, :] = recv[s, 384:385, :].astype(jnp.int32)
     copy = pltpu.make_async_copy(kinds_v, kinds, sems.at[4])
     copy.start()
     total[...] = jnp.zeros_like(total)
@@ -155,7 +158,7 @@
     def add(s, fine):
         for c in range(8):
             child = s * 8 + c
-            owner, octant = owners[child], kinds[child, 0]
+            owner, octant = owners[child], kinds[s, c]
             f = fine[24 * c : 24 * c + 24, :]
             cos_0, sin_0 = cos_ref[octant, 0:8], sin_ref[octant, 0:8]
             total[owner, 0:8] += cos_0 * f[0:8] - sin_0 * f[8:16]
@@ -198,9 +201,6 @@
         rows = pl.ds(64 * q, 64)
         copies.append(pltpu.make_async_copy(send_v.at[:, rows], send.at[:, rows], sems.at[5 + q]))
         copies[-1].start()
-        rows = pl.ds(576 * q, 576)
-        copies.append(pltpu.make_async_copy(rows_v.at[rows], outgoing.at[rows], sems.at[9 + q]))
-        copies[-1].start()
         for r in range(4):
             at = 72 * 8 * q + 64 + 2 * r
             re, im = rows_v[pl.ds(at, 8, stride=72), :], rows_v[pl.ds(at + 1, 8, stride=72), :]
@@ -208,7 +208,7 @@
             send_v[2 * r, rows, :] = jnp.where(left, re, pltpu.roll(im, 64, 1))
             send_v[2 * r + 1, rows, :] = jnp.where(left, pltpu.roll(re, 64, 1), im)
     rows = pl.ds(256, 56)
-    copies.append(pltpu.make_async_copy(send_v.at[:, rows], send.at[:, rows], sems.at[13]))
+    copies.append(pltpu.make_async_copy(send_v.at[:, rows], send.at[:, rows], sems.at[9]))
     copies[-1].start()
     for copy in copies:
         copy.wait()
@@ -245,17 +245,17 @@
         return pl.multiple_of(idx.at[pl.ds(j // 4, 169), pl.ds(n_own * (j % 4), n_own)][24 * b, p], 8)
 
     def some(i, b):
-        acc = [[jnp.zeros((8, 128), jnp.float32) for _ in range(3)] for _ in range(4)]
+        acc = [[jnp.zeros((8, 128), jnp.float32) for _ in range(3)] for _ in range(8)]
         for j in range(n_far):
-            for h in range(4):
-                f, o = index(j, b, 4 * i + h), index(n_far + j, b, 4 * i + h)
+            for h in range(8):
+                f, o = index(j, b, 8 * i + h), index(n_far + j, b, 8 * i + h)
                 t = factor[pl.ds(o, 8), :]
                 acc[h][0] += t * source[pl.ds(f, 8), :]
                 acc[h][1] += t * source[pl.ds(f + 8, 8), :]
                 acc[h][2] += factor[pl.ds(o + 8, 8), :] * source[pl.ds(f + 16, 8), :]
-        for h in range(4):
+        for h in range(8):
             for k in range(3):
-                sums[pl.ds(pl.multiple_of(24 * (b * n_own + 4 * i), 8) + 24 * h + 8 * k, 8), :] = acc[h][k]
+                sums[pl.ds(pl.multiple_of(24 * (b * n_own + 8 * i), 8) + 24 * h + 8 * k, 8), :] = acc[h][k]
         return b
 
     def finish(p, b):
@@ -271,7 +271,7 @@
     def box(b, carry):
         rows = pl.ds(pl.multiple_of(24 * b, 8), 24)
         pltpu.make_async_copy(idx_v.at[rows], idx.at[rows], load_sems.at[b]).wait()
-        lax.fori_loop(0, n_own // 4, some, b)
+        lax.fori_loop(0, n_own // 8, some, b)
         lax.fori_loop(0, n_own, finish, b, unroll=8)
         for q in range(4):
             at = (b * n_own + 8 * q) * 24 + 16
@@ -286,18 +286,9 @@
         store(b).wait()
 
 
-def place_rows_kernel(rows, out):
-    def one(p, carry):
-        for at in range(36):
-            v = rows[pl.ds(pl.multiple_of(72 * p, 8) + 2 * at, 2), :]
-            out[p, at // 3, :, 128 * (at % 3) : 128 * (at % 3) + 128] = v
-        return carry
-
-    lax.fori_loop(0, 32, one, 0)
-
-
-def place_kernel(recv, out, last):
+def place_kernel(recv, out, last, out_v, sems):
     left = lax.broadcasted_iota(jnp.int32, (8, 128), 1) < 64
+    copies = []
     for q in range(4):
         for r in range(4):
             rows = slice(256 + 8 * q, 264 + 8 * q)
@@ -306,15 +297,20 @@
             last[pl.ds(at, 8, stride=8), :] = jnp.where(left, e, pltpu.roll(o, 64, 1))
             last[pl.ds(at + 1, 8, stride=8), :] = jnp.where(left, pltpu.roll(e, 64, 1), o)
 
-    def one(p, carry):
-        base = pl.multiple_of(8 * p, 8)
-        for at in range(36):
-            rows = pl.ds(base + 2 * (at % 4), 2)
-            v = recv[at // 4, rows, :] if at < 32 else last[rows, :]
-            out[p, at // 3, :, 128 * (at % 3) : 128 * (at % 3) + 128] = v
-        return carry
-
-    lax.fori_loop(0, 32, one, 0)
+        def one(p, carry):
+            base = pl.multiple_of(8 * p, 8)
+            for at in range(36):
+                rows = pl.ds(base + 2 * (at % 4), 2)
+                v = recv[at // 4, rows, :] if at < 32 else last[rows, :]
+                out_v[p, at // 3, :, 128 * (at % 3) : 128 * (at % 3) + 128] = v
+            return carry
+
+        lax.fori_loop(8 * q, 8 * q + 8, one, 0)
+        some = pl.ds(8 * q, 8)
+        copies.append(pltpu.make_async_copy(out_v.at[some], out.at[some], sems.at[q]))
+        copies[-1].start()
+    for copy in copies:
+        copy.wait()
 
 
 def phase_tables(samp, n_theta, n_phi):
@@ -344,8 +340,8 @@
     return pltpu.with_memory_space_constraint(x, pltpu.VMEM)
 
 
-def params():
-    return pltpu.CompilerParams(vmem_limit_bytes=VMEM_LIMIT)
+def params(mib):
+    return pltpu.CompilerParams(vmem_limit_bytes=mib * 2**20)
 
 
 def anywhere():
@@ -366,10 +362,8 @@
     f32, bf16 = jnp.float32, jnp.bfloat16
 
     theta_table = lagrange_table(n_t1, n_t2, False).reshape(n_samp, band, n_t1)
-    both = np.zeros((n_samp, 24, 2, n_t1))
-    both[:, 0:8, 0], both[:, 8:16, 1] = theta_table[:, 0:8], theta_table[:, 0:8]
-    both[:, 16:20, 0], both[:, 20:24, 1] = theta_table[:, 8:12], theta_table[:, 8:12]
-    theta_high, theta_low = high_low(both.reshape(n_samp * 24, 2 * n_t1))
+    parts = [theta_table[:, 0:8].reshape(-1, n_t1), theta_table[:, 8:12].reshape(-1, n_t1)]
+    theta_high, theta_low = high_low(np.concatenate(parts))
     phi_high, phi_low = high_low(lagrange_table(n_p1, n_p2, True).T)
 
     sent = (n_samp, 48 * count + 8, 128)
@@ -379,13 +373,13 @@
         out_specs=[anywhere(), vmem()],
         out_shape=[pltpu.HBM(sent, f32), jax.ShapeDtypeStruct((8, 128), f32)],
         scratch_shapes=[
-            pltpu.VMEM((2, n_samp * 24, 2 * n_t1), bf16),
+            pltpu.VMEM((2, n_t2, n_t1), bf16),
             pltpu.VMEM(child_patterns.shape, f32),
             pltpu.VMEM(sent, f32),
             pltpu.SMEM((1, count), jnp.int32),
-            pltpu.SemaphoreType.DMA((2 * count + 3,)),
+            pltpu.SemaphoreType.DMA((3 * count + 3,)),
         ],
-        compiler_params=params(),
+        compiler_params=params(9),
         name="theta",
     )(far_away(octants.reshape(1, count)), far_away(theta_high), far_away(theta_low), far_away(child_patterns))
     bands = lax.all_to_all(bands, "samp", 0, 0)
@@ -397,17 +391,17 @@
         out_specs=[vmem()] * 2,
         out_shape=[pltpu.VMEM((n_off, 16, 128), f32), jax.ShapeDtypeStruct((8, 128), f32)],
         scratch_shapes=[pltpu.VMEM((n_off, 5, 2, 128), f32), pltpu.SemaphoreType.DMA((5,))],
-        compiler_params=params(),
+        compiler_params=params(6),
         cost_estimate=pl.CostEstimate(flops=10**7, bytes_accessed=10**7, transcendentals=0),
         name="prepare",
     )(box.reshape(1), token, far_away(translation.transpose(0, 2, 1, 3)))
     lists = jnp.concatenate([far_boxes.T * 24, offsets.T * 16], 0).reshape(24, 128)
 
-    outgoing, send = pl.pallas_call(
+    send = pl.pallas_call(
         phi_kernel,
         in_specs=[smem(), vmem(), vmem()] + [anywhere()] * 4 + [vmem()],
-        out_specs=[anywhere()] * 2,
-        out_shape=[pltpu.HBM((parents * 72, 128), f32), pltpu.HBM((n_box, 9 * parents + 24, 128), f32)],
+        out_specs=anywhere(),
+        out_shape=pltpu.HBM((n_box, 9 * parents + 24, 128), f32),
         scratch_shapes=[
             pltpu.VMEM((parents, 24, n_p2), f32),
             pltpu.VMEM((2, 24 * count, n_p2), f32),
@@ -416,11 +410,11 @@
             pltpu.VMEM((2, n_p1, n_p2), bf16),
             pltpu.VMEM(cos_part.shape, f32),
             pltpu.VMEM(cos_part.shape, f32),
-            pltpu.VMEM((n_samp * count, 128), jnp.int32),
-            pltpu.SMEM((n_samp * count, 128), jnp.int32),
-            pltpu.SemaphoreType.DMA((14,)),
+            pltpu.VMEM((n_samp, 128), jnp.int32),
+            pltpu.SMEM((n_samp, 128), jnp.int32),
+            pltpu.SemaphoreType.DMA((10,)),
         ],
-        compiler_params=params(),
+        compiler_params=params(12),
         name="phi",
     )(
         parent_map[0], token, lists.astype(f32),
@@ -443,29 +437,26 @@
             pltpu.SemaphoreType.DMA((n_box,)),
             pltpu.SemaphoreType.DMA((n_box,)),
         ],
-        compiler_params=params(),
+        compiler_params=params(12),
         name="translate",
     )(held(everywhere), held(factor.reshape(n_off * 16, 128)))
     back = lax.all_to_all(back, "box", 0, 0)
-    shape = jax.ShapeDtypeStruct((parents, band, 2, n_p2), f32)
-    outgoing = pl.pallas_call(
-        place_rows_kernel,
-        in_specs=[vmem()],
-        out_specs=vmem(),
-        out_shape=shape,
-        compiler_params=params(),
-        cost_estimate=pl.CostEstimate(flops=10**6, bytes_accessed=4 * 10**6, transcendentals=0),
-        name="place_rows",
-    )(outgoing)
-    incoming = pl.pallas_call(
+    shape = (parents, band, 2, n_p2)
+    place = pl.pallas_call(
         place_kernel,
         in_specs=[vmem()],
-        out_specs=vmem(),
-        out_shape=shape,
-        scratch_shapes=[pltpu.VMEM((8 * parents, 128), f32)],
-        compiler_params=params(),
+        out_specs=anywhere(),
+        out_shape=pltpu.HBM(shape, f32),
+        scratch_shapes=[
+            pltpu.VMEM((8 * parents, 128), f32),
+            pltpu.VMEM(shape, f32),
+            pltpu.SemaphoreType.DMA((4,)),
+        ],
+        compiler_params=params(6),
+        cost_estimate=pl.CostEstimate(flops=10**6, bytes_accessed=4 * 10**6, transcendentals=0),
         name="place",
-    )(held(back))
+    )
+    outgoing, incoming = place(send), place(held(back))
     return outgoing.transpose(0, 2, 1, 3), incoming.transpose(0, 2, 1, 3)
 
 

time: 132 us -> 130 us (0.985)
  Pallas kernels: 41.4 us -> 39.3 us
    pallas_call x1, Pallas kernels: 5.85 us -> 4.25 us  [shards(): pl.pallas_call(theta_kernel, in_specs=[anywhere()] * 4, out_specs=[anywhe...]
where the time goes in v3:
time: 130 us; the launch traced here: 129 us
  waiting for transfers between devices  49.4 us (38%)
  Pallas kernels  39.3 us (30%)
  blocking collectives  26.9 us (21%)
  starting transfers between devices  9.66 us (7%)
  other arithmetic  1.73 us (1%)
  local copies, waits for them, and re-layouts  1.72 us (1%)
    all_to_all x1, waiting for transfers between devices, shards(): bands = lax.all_to_all(bands, 'samp', 0, 0)  32.6 us
    all_to_all x1, blocking collectives, shards(): everywhere = lax.all_to_all(send, 'box', 0, 0)  26.9 us
    pallas_call x1, Pallas kernels, shards(): pl.pallas_call(translate_kernel, in_specs=[vmem(), vmem()], out_specs=any...  17.9 us
    all_to_all x1, waiting for transfers between devices, shards(): back = lax.all_to_all(back, 'box', 0, 0)  16.8 us
    pallas_call x1, Pallas kernels, shards(): pl.pallas_call(prepare_kernel, in_specs=[smem(), vmem(), anywhere()], out...  7.62 us
    pallas_call x1, Pallas kernels, shards(): pl.pallas_call(phi_kernel, in_specs=[smem(), vmem(), vmem()] + [anywhere(...  7.05 us
    all_to_all x1, starting transfers between devices, shards(): bands = lax.all_to_all(bands, 'samp', 0, 0)  5.95 us
    pallas_call x1, Pallas kernels, shards(): pl.pallas_call(theta_kernel, in_specs=[anywhere()] * 4, out_specs=[anywhe...  4.25 us
  transfers between devices with their start and end apart: 2, of which 2 were waited for; matrix products, arithmetic and copies ran while one was open for 1% of the time, Pallas kernels for 7%

profile of v3, /device:TPU:32, one launch (start us, length us, event | category | flops | bytes accessed | tf_op | source)
XLA Modules:
  0.0 129.4 jit_solution(8867460226181493354)
XLA Ops:
  0.6 4.3 %theta.1 = (f32[16,392,128]{2,1,0:T(8,128)}, f32[8,128]{1,0:T(8,128)S(1)}) custom-call(s32[1,8]{1,0:T(1,128)} %bitcast.16, bf16[192,128]{1,0:T(8,128)(2,1)} %constant.37.clone.table_high, bf16[192,128]{1,0:T(8,128)(2,1)} %constant.38.clone.table_low, f32[8,2,128,256]{3,2,1,0:T(8,128)} %child.1), custom_call_target="tpu_custom_call" | custom-call | tf_op jit(solution)/shard_map/theta/pallas_call | solution.py:370
  4.9 0.0 copy-start.4
  4.9 0.0 copy-start.5
  4.9 6.0 %all-to-all-start = ((f32[16,392,128]{2,1,0:T(8,128)}), f32[16,392,128]{2,1,0:T(8,128)S(1)}, u32[]{:S(2)}, u32[]{:S(2)}) async-start(f32[16,392,128]{2,1,0:T(8,128)} %get-tuple-element.8), calls=%async_computation | async-start | bytes 6422528 | tf_op jit(solution)/shard_map/all_to_all | solution.py:385
  10.9 0.0 copy-done.4
  10.9 0.0 copy-done.5
  10.9 0.1 add_convert_fusion
  11.0 0.1 copy.17
  11.1 0.1 convert_element_type.9.lists
  11.1 0.0 copy-start.8
  11.2 0.0 copy-start.6
  11.2 0.0 copy-start.7
  11.2 0.0 copy-start.3
  11.2 7.6 %prepare.1 = (f32[316,16,128]{2,1,0:T(8,128)S(1)}, f32[8,128]{1,0:T(8,128)S(1)}) custom-call(s32[1]{0:T(128)} %bitcast.1.box, f32[8,128]{1,0:T(8,128)S(1)} %get-tuple-element.6.token, f32[316,12,2,384]{3,2,1,0:T(2,128)} %bitcast.13), custom_call_target="tpu_custom_call" | custom-call | flops 10000000 | bytes 10000000 | tf_op jit(solution)/shard_map/prepare/pallas_call | solution.py:388
  18.8 0.0 copy-start.1
  18.8 1.5 %copy-done.1 = f32[316,16,128]{2,1,0:T(8,128)} copy-done((f32[316,16,128]{2,1,0:T(8,128)}, f32[316,16,128]{2,1,0:T(8,128)S(1)}, u32[]{:S(2)}) %copy-start.1) | copy-done | bytes 2588696
  20.3 0.0 copy-done.9
  20.4 0.0 copy-done.8
  20.4 0.1 broadcast_multiply_fusion
  20.5 0.0 copy-done.6
  20.5 0.0 copy-done.7
  20.5 1.5 %sine_multiply_fusion = (f32[8,16,384]{2,1,0:T(8,128)}, f32[8,16,384]{2,1,0:T(8,128)}) fusion(f32[16]{0:T(128)S(1)} %copy-done.7, f32[8,16]{1,0:T(8,128)S(1)} %broadcast_multiply_fusion, f32[8,384]{1,0:T(8,128)S(1)} %copy-done.6, f32[16]{0:T(128)S(1)} %get-tuple-element.12), kind=kLoop, calls=%fused_computation | loop fusion | flops 196608 | bytes 406144 | tf_op jit(solution)/shard_map/mul | solution.py:328
  22.0 32.6 %all-to-all-done.recv = f32[16,392,128]{2,1,0:T(8,128)S(1)} async-done(((f32[16,392,128]{2,1,0:T(8,128)}), f32[16,392,128]{2,1,0:T(8,128)S(1)}, u32[]{:S(2)}, u32[]{:S(2)}) %all-to-all-start) | async-done | bytes 3211296 | tf_op jit(solution)/shard_map/all_to_all | solution.py:385
  54.6 0.0 copy-done.3
  54.6 7.0 %phi.1.recv = f32[8,312,128]{2,1,0:T(8,128)} custom-call(s32[128]{0:T(128)S(1)} %bitcast.12, f32[8,128]{1,0:T(8,128)S(1)} %get-tuple-element.7.token, f32[24,128]{1,0:T(8,128)S(1)} %convert_element_type.9.lists, bf16[256,384]{1,0:T(8,128)(2,1)} %constant.43.clone.table_high, bf16[256,384]{1,0:T(8,128)(2,1)} %constant.44.clone.table_low, ...), custom_call_target="tpu_custom_call" | custom-call | tf_op jit(solution)/shard_map/phi/pallas_call | solution.py:400
  61.7 26.9 %all_to_all.15.recv = f32[8,312,128]{2,1,0:T(8,128)S(1)} all-to-all(f32[8,312,128]{2,1,0:T(8,128)} %phi.1.recv), channel_id=1, replica_groups=mesh['box'=8,'samp'=16] {'box'}, dimensions={0} | all-to-all | bytes 2555904 | tf_op jit(solution)/shard_map/all_to_all | solution.py:424
  88.5 0.0 copy-done.2
  88.5 17.9 %translate.1 = f32[8,288,128]{2,1,0:T(8,128)} custom-call(f32[8,312,128]{2,1,0:T(8,128)S(1)} %all_to_all.15.recv, f32[5056,128]{1,0:T(8,128)S(1)} %bitcast.11), custom_call_target="tpu_custom_call" | custom-call | tf_op jit(solution)/shard_map/translate/pallas_call | solution.py:426
  106.4 3.7 %all-to-all-start.2 = ((f32[8,288,128]{2,1,0:T(8,128)}), f32[8,288,128]{2,1,0:T(8,128)S(1)}, u32[]{:S(2)}, u32[]{:S(2)}) async-start(f32[8,288,128]{2,1,0:T(8,128)} %translate.1), calls=%async_computation.2 | async-start | bytes 2359296 | tf_op jit(solution)/shard_map/all_to_all | solution.py:443
  110.2 1.2 place.2
  111.4 16.8 %all-to-all-done.2.recv = f32[8,288,128]{2,1,0:T(8,128)S(1)} async-done(((f32[8,288,128]{2,1,0:T(8,128)}), f32[8,288,128]{2,1,0:T(8,128)S(1)}, u32[]{:S(2)}, u32[]{:S(2)}) %all-to-all-start.2) | async-done | bytes 1179680 | tf_op jit(solution)/shard_map/all_to_all | solution.py:443
  128.2 1.2 place.3
  (6 shorter events, 0.1 us)
Async XLA Ops:
  4.9 6.0 %copy-start.4 = (s32[32,48]{1,0:T(8,128)S(1)}, s32[32,48]{1,0:T(8,128)}, u32[]{:S(2)}) copy-start(s32[32,48]{1,0:T(8,128)} %param.18) | copy-start | bytes 18436
  4.9 6.0 %copy-start.5 = (s32[32,48]{1,0:T(8,128)S(1)}, s32[32,48]{1,0:T(8,128)}, u32[]{:S(2)}) copy-start(s32[32,48]{1,0:T(8,128)} %param.17) | copy-start | bytes 18436
  4.9 49.7 %all-to-all-start = ((f32[16,392,128]{2,1,0:T(8,128)}), f32[16,392,128]{2,1,0:T(8,128)S(1)}, u32[]{:S(2)}, u32[]{:S(2)}) async-start(f32[16,392,128]{2,1,0:T(8,128)} %get-tuple-element.8), calls=%async_computation | async-start | bytes 6422528 | tf_op jit(solution)/shard_map/all_to_all | solution.py:385
  11.1 9.2 %copy-start.9 = (s32[16]{0:T(128)S(1)}, s32[16]{0:T(128)}, u32[]{:S(2)}) copy-start(s32[16]{0:T(128)} %constant.39.clone) | copy-start | bytes 196
  11.1 9.2 %copy-start.8 = (f32[8]{0:T(128)S(1)}, f32[8]{0:T(128)}, u32[]{:S(2)}) copy-start(f32[8]{0:T(128)} %constant.50) | copy-start | bytes 100
  11.2 9.3 %copy-start.6 = (f32[8,384]{1,0:T(8,128)S(1)}, f32[8,384]{1,0:T(8,128)}, u32[]{:S(2)}) copy-start(f32[8,384]{1,0:T(8,128)} %constant.49) | copy-start | bytes 36868
  11.2 9.3 %copy-start.7 = (f32[16]{0:T(128)S(1)}, f32[16]{0:T(128)}, u32[]{:S(2)}) copy-start(f32[16]{0:T(128)} %constant.51) | copy-start | bytes 196
  11.2 43.4 %copy-start.3 = (s32[1,128]{1,0:T(1,128)S(1)}, s32[1,128]{1,0:T(1,128)}, u32[]{:S(2)}) copy-start(s32[1,128]{1,0:T(1,128)} %param.16) | copy-start | bytes 1540
  18.8 1.5 %copy-start.1 = (f32[316,16,128]{2,1,0:T(8,128)}, f32[316,16,128]{2,1,0:T(8,128)S(1)}, u32[]{:S(2)}) copy-start(f32[316,16,128]{2,1,0:T(8,128)S(1)} %get-tuple-element.9) | copy-start | bytes 7766020
  54.6 33.9 %copy-start.2 = (f32[316,16,128]{2,1,0:T(8,128)S(1)}, f32[316,16,128]{2,1,0:T(8,128)}, u32[]{:S(2)}) copy-start(f32[316,16,128]{2,1,0:T(8,128)} %copy-done.1) | copy-start | bytes 7766020
  106.4 3.7 %copy-start = (f32[8,312,128]{2,1,0:T(8,128)S(1)}, f32[8,312,128]{2,1,0:T(8,128)}, u32[]{:S(2)}) copy-start(f32[8,312,128]{2,1,0:T(8,128)} %phi.1.recv) | copy-start | bytes 3833860
  106.4 21.7 %all-to-all-start.2 = ((f32[8,288,128]{2,1,0:T(8,128)}), f32[8,288,128]{2,1,0:T(8,128)S(1)}, u32[]{:S(2)}, u32[]{:S(2)}) async-start(f32[8,288,128]{2,1,0:T(8,128)} %translate.1), calls=%async_computation.2 | async-start | bytes 2359296 | tf_op jit(solution)/shard_map/all_to_all | solution.py:443

commit v4 on v3

--- a/solution.py
+++ b/solution.py
@@ -103,7 +103,7 @@
         copy.wait()
 
 
-def prepare_kernel(box, token, table, out, done, raw, sems):
+def prepare_kernel(box, token, lists, table, out, done, lists_out, raw, sems):
     me = box[0]
     n_off = table.shape[0]
     pair, half = me // 2, me % 2
@@ -116,6 +116,7 @@
         )
         copies[-1].start()
     done[...] = token[...]
+    lists_out[...] = lists[...]
     for copy in copies:
         copy.wait()
     left = lax.broadcasted_iota(jnp.int32, (1, 128), 1) < 64
@@ -133,8 +134,8 @@
 
 
 def phi_kernel(
-    owners, token, lists, table_high, table_low, cos_hbm, sin_hbm, recv, send,
-    total, fine, rows_v, send_v, tables, cos_ref, sin_ref, kinds_v, kinds, sems,
+    owners, token, lists, table_high, table_low, cos_hbm, sin_hbm, recv, send_v,
+    total, fine, rows_v,  tables, cos_ref, sin_ref, kinds_v, kinds, sems,
 ):
     pairs = [(table_high, tables.at[0]), (table_low, tables.at[1]), (cos_hbm, cos_ref), (sin_hbm, sin_ref)]
     loads = [pltpu.make_async_copy(a, b, sems.at[i]) for i, (a, b) in enumerate(pairs)]
@@ -145,8 +146,6 @@
     copy = pltpu.make_async_copy(kinds_v, kinds, sems.at[4])
     copy.start()
     total[...] = jnp.zeros_like(total)
-    for d in range(8):
-        send_v[d, 288:312, :] = lists[...]
     for load in loads[:2]:
         load.wait()
     table = jnp.concatenate([tables[0], tables[0], tables[1]], 0)
@@ -195,33 +194,26 @@
         return carry
 
     left = lax.broadcasted_iota(jnp.int32, (8, 128), 1) < 64
-    copies = []
     for q in range(4):
         lax.fori_loop(8 * q, 8 * q + 8, parent, 0)
-        rows = pl.ds(64 * q, 64)
-        copies.append(pltpu.make_async_copy(send_v.at[:, rows], send.at[:, rows], sems.at[5 + q]))
-        copies[-1].start()
         for r in range(4):
             at = 72 * 8 * q + 64 + 2 * r
             re, im = rows_v[pl.ds(at, 8, stride=72), :], rows_v[pl.ds(at + 1, 8, stride=72), :]
             rows = slice(256 + 8 * q, 264 + 8 * q)
             send_v[2 * r, rows, :] = jnp.where(left, re, pltpu.roll(im, 64, 1))
             send_v[2 * r + 1, rows, :] = jnp.where(left, pltpu.roll(re, 64, 1), im)
-    rows = pl.ds(256, 56)
-    copies.append(pltpu.make_async_copy(send_v.at[:, rows], send.at[:, rows], sems.at[9]))
-    copies[-1].start()
-    for copy in copies:
-        copy.wait()
-
-
-def translate_kernel(recv, factor, send, source, sums, send_v, idx_v, idx, load_sems, store_sems):
+
+
+def translate_kernel(box_id, lists, recv, factor, send, source, sums, send_v, idx, load_sems, store_sems):
     n_far, n_own = 48, 32
-    loads = []
+    me = box_id[0]
+
+    def load(b):
+        rows = pl.ds(pl.multiple_of(24 * b, 8), 24)
+        return pltpu.make_async_copy(lists.at[lax.bitwise_xor(me, b)], idx.at[rows], load_sems.at[b])
+
     for b in range(8):
-        rows = pl.ds(24 * b, 24)
-        idx_v[rows, :] = recv[b, 288:312, :].astype(jnp.int32)
-        loads.append(pltpu.make_async_copy(idx_v.at[rows], idx.at[rows], load_sems.at[b]))
-        loads[-1].start()
+        load(jnp.int32(b)).start()
     left = lax.broadcasted_iota(jnp.int32, (8, 128), 1) < 64
     even = lax.broadcasted_iota(jnp.int32, (8, 128), 0) % 2 == 0
     for b in range(8):
@@ -269,8 +261,7 @@
         return pltpu.make_async_copy(send_v.at[pl.ds(b, 1)], send.at[pl.ds(b, 1)], store_sems.at[b])
 
     def box(b, carry):
-        rows = pl.ds(pl.multiple_of(24 * b, 8), 24)
-        pltpu.make_async_copy(idx_v.at[rows], idx.at[rows], load_sems.at[b]).wait()
+        load(b).wait()
         lax.fori_loop(0, n_own // 8, some, b)
         lax.fori_loop(0, n_own, finish, b, unroll=8)
         for q in range(4):
@@ -385,28 +376,33 @@
     bands = lax.all_to_all(bands, "samp", 0, 0)
 
     cos_part, sin_part = phase_tables(samp, n_t2, n_p2)
-    factor, token = pl.pallas_call(
+    lists = jnp.concatenate([far_boxes.T * 24, offsets.T * 16], 0).reshape(24, 128).astype(f32)
+    factor, token, lists = pl.pallas_call(
         prepare_kernel,
-        in_specs=[smem(), vmem(), anywhere()],
-        out_specs=[vmem()] * 2,
-        out_shape=[pltpu.VMEM((n_off, 16, 128), f32), jax.ShapeDtypeStruct((8, 128), f32)],
+        in_specs=[smem(), vmem(), vmem(), anywhere()],
+        out_specs=[vmem()] * 3,
+        out_shape=[
+            pltpu.VMEM((n_off, 16, 128), f32),
+            jax.ShapeDtypeStruct((8, 128), f32),
+            jax.ShapeDtypeStruct((24, 128), f32),
+        ],
         scratch_shapes=[pltpu.VMEM((n_off, 5, 2, 128), f32), pltpu.SemaphoreType.DMA((5,))],
         compiler_params=params(6),
         cost_estimate=pl.CostEstimate(flops=10**7, bytes_accessed=10**7, transcendentals=0),
         name="prepare",
-    )(box.reshape(1), token, far_away(translation.transpose(0, 2, 1, 3)))
-    lists = jnp.concatenate([far_boxes.T * 24, offsets.T * 16], 0).reshape(24, 128)
+    )(box.reshape(1), token, lists, far_away(translation.transpose(0, 2, 1, 3)))
+    pairs = [[(i, i ^ k) for i in range(n_box)] for k in range(1, n_box)]
+    lists = jnp.stack([lists] + [lax.ppermute(lists, "box", p) for p in pairs]).astype(jnp.int32)
 
     send = pl.pallas_call(
         phi_kernel,
-        in_specs=[smem(), vmem(), vmem()] + [anywhere()] * 4 + [vmem()],
-        out_specs=anywhere(),
-        out_shape=pltpu.HBM((n_box, 9 * parents + 24, 128), f32),
+        in_specs=[smem(), vmem()] + [anywhere()] * 5 + [vmem()],
+        out_specs=vmem(),
+        out_shape=pltpu.VMEM((n_box, 9 * parents, 128), f32),
         scratch_shapes=[
             pltpu.VMEM((parents, 24, n_p2), f32),
             pltpu.VMEM((2, 24 * count, n_p2), f32),
             pltpu.VMEM((parents * 72, 128), f32),
-            pltpu.VMEM((n_box, 9 * parents + 24, 128), f32),
             pltpu.VMEM((2, n_p1, n_p2), bf16),
             pltpu.VMEM(cos_part.shape, f32),
             pltpu.VMEM(cos_part.shape, f32),
@@ -417,7 +413,7 @@
         compiler_params=params(12),
         name="phi",
     )(
-        parent_map[0], token, lists.astype(f32),
+        parent_map[0], token, far_away(lists),
         *[far_away(x) for x in (phi_high, phi_low, cos_part, sin_part)], held(bands),
     )
 
@@ -425,21 +421,20 @@
     n_all = n_box * parents
     back = pl.pallas_call(
         translate_kernel,
-        in_specs=[vmem(), vmem()],
+        in_specs=[smem(), anywhere(), vmem(), vmem()],
         out_specs=anywhere(),
         out_shape=pltpu.HBM((n_box, 9 * parents, 128), f32),
         scratch_shapes=[
             pltpu.VMEM((n_all * 24, 128), f32),
             pltpu.VMEM((n_all * 24, 128), f32),
             pltpu.VMEM((n_box, 9 * parents, 128), f32),
-            pltpu.VMEM((24 * n_box, 128), jnp.int32),
             pltpu.SMEM((24 * n_box, 128), jnp.int32),
             pltpu.SemaphoreType.DMA((n_box,)),
             pltpu.SemaphoreType.DMA((n_box,)),
         ],
         compiler_params=params(12),
         name="translate",
-    )(held(everywhere), held(factor.reshape(n_off * 16, 128)))
+    )(box.reshape(1), far_away(lists), held(everywhere), held(factor.reshape(n_off * 16, 128)))
     back = lax.all_to_all(back, "box", 0, 0)
     shape = (parents, band, 2, n_p2)
     place = pl.pallas_call(

time: 130 us -> 129 us (level)
  waiting for transfers between devices: 49.4 us -> 32.6 us
  starting transfers between devices: 9.66 us -> 26.4 us
    all_to_all x1, waiting for transfers between devices: 32.6 us -> 10.6 us  [shards(): bands = lax.all_to_all(bands, 'samp', 0, 0)]
    ppermute x0 -> x7, starting transfers between devices: none -> 16.7 us  [shards(): lax.ppermute(lists, 'box', p)]
    ppermute x0 -> x7, waiting for transfers between devices: none -> 4.85 us  [shards(): lax.ppermute(lists, 'box', p)]
  transfers between devices with their start and end apart: 2 -> 9, of which waited for: 2 -> 5; matrix products, arithmetic and copies ran while one was open for 1% -> 2% of each run, Pallas kernels for 7% -> 7%
where the time goes in v4:
time: 129 us; the launch traced here: 128 us
  Pallas kernels  38.5 us (30%)
  waiting for transfers between devices  32.6 us (25%)
  starting transfers between devices  26.4 us (20%)
  blocking collectives  25.6 us (20%)
  other arithmetic  2.4 us (2%)
  local copies, waits for them, and re-layouts  1.73 us (1%)
    all_to_all x1, blocking collectives, shards(): everywhere = lax.all_to_all(send, 'box', 0, 0)  25.6 us
    pallas_call x1, Pallas kernels, shards(): pl.pallas_call(translate_kernel, in_specs=[smem(), anywhere(), vmem(), vm...  17.9 us
    all_to_all x1, waiting for transfers between devices, shards(): back = lax.all_to_all(back, 'box', 0, 0)  17.1 us
    ppermute x7, starting transfers between devices, shards(): lax.ppermute(lists, 'box', p)  16.7 us
    all_to_all x1, waiting for transfers between devices, shards(): bands = lax.all_to_all(bands, 'samp', 0, 0)  10.6 us
    pallas_call x1, Pallas kernels, shards(): pl.pallas_call(prepare_kernel, in_specs=[smem(), vmem(), vmem(), anywhere...  7.62 us
    pallas_call x1, Pallas kernels, shards(): pl.pallas_call(phi_kernel, in_specs=[smem(), vmem()] + [anywhere()] * 5 +...  6.25 us
    all_to_all x1, starting transfers between devices, shards(): bands = lax.all_to_all(bands, 'samp', 0, 0)  5.95 us
  transfers between devices with their start and end apart: 9, of which 5 were waited for; matrix products, arithmetic and copies ran while one was open for 2% of the time, Pallas kernels for 7%

profile of v4, /device:TPU:32, one launch (start us, length us, event | category | flops | bytes accessed | tf_op | source)
XLA Modules:
  0.0 128.1 jit_solution(10380820935383752143)
XLA Ops:
  0.6 4.2 %theta.1 = (f32[16,392,128]{2,1,0:T(8,128)}, f32[8,128]{1,0:T(8,128)S(1)}) custom-call(s32[1,8]{1,0:T(1,128)} %bitcast.32, bf16[192,128]{1,0:T(8,128)(2,1)} %constant.37.clone.table_high, bf16[192,128]{1,0:T(8,128)(2,1)} %constant.38.clone.table_low, f32[8,2,128,256]{3,2,1,0:T(8,128)} %child.1), custom_call_target="tpu_custom_call" | custom-call | tf_op jit(solution)/shard_map/theta/pallas_call | solution.py:361
  4.9 0.0 copy-start.6
  4.9 6.0 %all-to-all-start = ((f32[16,392,128]{2,1,0:T(8,128)}), f32[16,392,128]{2,1,0:T(8,128)S(1)}, u32[]{:S(2)}, u32[]{:S(2)}) async-start(f32[16,392,128]{2,1,0:T(8,128)} %get-tuple-element.10), calls=%async_computation | async-start | bytes 6422528 | tf_op jit(solution)/shard_map/all_to_all | solution.py:376
  10.8 0.1 add_convert_fusion
  10.9 0.1 copy.17
  11.0 0.1 convert_element_type.12.lists
  11.1 0.0 copy-start.9
  11.1 0.0 copy-start.7
  11.1 0.0 copy-start.8
  11.2 7.6 %prepare.1 = (f32[316,16,128]{2,1,0:T(8,128)S(1)}, f32[8,128]{1,0:T(8,128)S(1)}, f32[24,128]{1,0:T(8,128)S(1)}) custom-call(s32[1]{0:T(128)} %bitcast.1.box.box_id, f32[8,128]{1,0:T(8,128)S(1)} %get-tuple-element.7.token, f32[24,128]{1,0:T(8,128)S(1)} %convert_element_type.12.lists, f32[316,12,2,384]{3,2,1,0:T(2,128)} %bitcast.29), custom_call_target="tpu_custom_call" | custom-call | flops 10000000 | bytes 10000000 | tf_op jit(solution)/shard_map/prepare/pallas_call | solution.py:380
  18.8 1.5 %copy-done.2 = f32[316,16,128]{2,1,0:T(8,128)} copy-done((f32[316,16,128]{2,1,0:T(8,128)}, f32[316,16,128]{2,1,0:T(8,128)S(1)}, u32[]{:S(2)}) %copy-start.2) | copy-done | bytes 2588696
  20.3 5.2 %collective-permute-start.6 = (f32[24,128]{1,0:T(8,128)S(1)}, f32[24,128]{1,0:T(8,128)S(1)}, u32[]{:S(2)}, u32[]{:S(2)}) collective-permute-start(f32[24,128]{1,0:T(8,128)S(1)} %get-tuple-element.9), channel_id=1, source_target_pairs={{0,112},{16,96},{32,80},{48,64},{64,48},{80,32},{96,16},{112,0},{1... | collective-permute-start | bytes 36872 | tf_op jit(solution)/shard_map/ppermute | solution.py:395
  25.4 0.8 collective-permute-start.5
  26.2 2.9 %collective-permute-start.4 = (f32[24,128]{1,0:T(8,128)S(1)}, f32[24,128]{1,0:T(8,128)S(1)}, u32[]{:S(2)}, u32[]{:S(2)}) collective-permute-start(f32[24,128]{1,0:T(8,128)S(1)} %get-tuple-element.9), channel_id=1, source_target_pairs={{0,80},{16,64},{32,112},{48,96},{64,16},{80,0},{96,48},{112,32},{1... | collective-permute-start | bytes 36872 | tf_op jit(solution)/shard_map/ppermute | solution.py:395
  29.2 0.6 collective-permute-start.3
  29.7 1.5 %collective-permute-start = (f32[24,128]{1,0:T(8,128)S(1)}, f32[24,128]{1,0:T(8,128)S(1)}, u32[]{:S(2)}, u32[]{:S(2)}) collective-permute-start(f32[24,128]{1,0:T(8,128)S(1)} %get-tuple-element.9), channel_id=1, source_target_pairs={{0,16},{16,0},{32,48},{48,32},{64,80},{80,64},{96,112},{112,96},{1... | collective-permute-start | bytes 36872 | tf_op jit(solution)/shard_map/ppermute | solution.py:395
  31.3 0.1 broadcast_multiply_fusion
  31.4 1.5 %sine_multiply_fusion = (f32[8,16,384]{2,1,0:T(8,128)}, f32[8,16,384]{2,1,0:T(8,128)}) fusion(f32[16]{0:T(128)S(1)} %copy-done.8, f32[8,16]{1,0:T(8,128)S(1)} %broadcast_multiply_fusion, f32[8,384]{1,0:T(8,128)S(1)} %copy-done.7, f32[16]{0:T(128)S(1)} %get-tuple-element.14), kind=kLoop, calls=%fused_computation | loop fusion | flops 196608 | bytes 406144 | tf_op jit(solution)/shard_map/mul | solution.py:319
  32.9 0.5 collective-permute-done
  33.4 3.0 %collective-permute-start.1 = (f32[24,128]{1,0:T(8,128)S(1)}, f32[24,128]{1,0:T(8,128)S(1)}, u32[]{:S(2)}, u32[]{:S(2)}) collective-permute-start(f32[24,128]{1,0:T(8,128)S(1)} %get-tuple-element.9), channel_id=1, source_target_pairs={{0,32},{16,48},{32,0},{48,16},{64,96},{80,112},{96,64},{112,80},{1... | collective-permute-start | bytes 36872 | tf_op jit(solution)/shard_map/ppermute | solution.py:395
  36.5 2.2 %collective-permute-done.1 = f32[24,128]{1,0:T(8,128)S(1)} collective-permute-done((f32[24,128]{1,0:T(8,128)S(1)}, f32[24,128]{1,0:T(8,128)S(1)}, u32[]{:S(2)}, u32[]{:S(2)}) %collective-permute-start.1) | collective-permute-done | bytes 12320 | tf_op jit(solution)/shard_map/ppermute | solution.py:395
  38.6 2.8 %collective-permute-start.2 = (f32[24,128]{1,0:T(8,128)S(1)}, f32[24,128]{1,0:T(8,128)S(1)}, u32[]{:S(2)}, u32[]{:S(2)}) collective-permute-start(f32[24,128]{1,0:T(8,128)S(1)} %get-tuple-element.9), channel_id=1, source_target_pairs={{0,48},{16,32},{32,16},{48,0},{64,112},{80,96},{96,80},{112,64},{1... | collective-permute-start | bytes 36872 | tf_op jit(solution)/shard_map/ppermute | solution.py:395
  41.4 2.1 %collective-permute-done.2 = f32[24,128]{1,0:T(8,128)S(1)} collective-permute-done((f32[24,128]{1,0:T(8,128)S(1)}, f32[24,128]{1,0:T(8,128)S(1)}, u32[]{:S(2)}, u32[]{:S(2)}) %collective-permute-start.2) | collective-permute-done | bytes 12320 | tf_op jit(solution)/shard_map/ppermute | solution.py:395
  43.6 0.7 convert_element_type.13.lists
  44.3 10.6 %all-to-all-done.recv = f32[16,392,128]{2,1,0:T(8,128)S(1)} async-done(((f32[16,392,128]{2,1,0:T(8,128)}), f32[16,392,128]{2,1,0:T(8,128)S(1)}, u32[]{:S(2)}, u32[]{:S(2)}) %all-to-all-start) | async-done | bytes 3211296 | tf_op jit(solution)/shard_map/all_to_all | solution.py:376
  54.9 6.2 %phi.1.recv = f32[8,288,128]{2,1,0:T(8,128)S(1)} custom-call(s32[128]{0:T(128)S(1)} %bitcast.28, f32[8,128]{1,0:T(8,128)S(1)} %get-tuple-element.8.token, s32[8,24,128]{2,1,0:T(8,128)} %convert_element_type.13.lists, bf16[256,384]{1,0:T(8,128)(2,1)} %constant.43.clone.table_high, bf16[256,384]{1,0:T(8,128)(2,1)} %constant.44.clone.table_low, ...), custom_call_target="tpu_custom_call" | custom-call | tf_op jit(solution)/shard_map/phi/pallas_call | solution.py:397
  61.2 25.6 %all_to_all.15.recv = f32[8,288,128]{2,1,0:T(8,128)S(1)} all-to-all(f32[8,288,128]{2,1,0:T(8,128)S(1)} %phi.1.recv), channel_id=1, replica_groups=mesh['box'=8,'samp'=16] {'box'}, dimensions={0} | all-to-all | bytes 2359296 | tf_op jit(solution)/shard_map/all_to_all | solution.py:420
  86.8 17.9 %translate.1 = f32[8,288,128]{2,1,0:T(8,128)} custom-call(s32[1]{0:T(128)} %bitcast.1.box.box_id, s32[8,24,128]{2,1,0:T(8,128)} %convert_element_type.13.lists, f32[8,288,128]{2,1,0:T(8,128)S(1)} %all_to_all.15.recv, f32[5056,128]{1,0:T(8,128)S(1)} %bitcast.27), custom_call_target="tpu_custom_call" | custom-call | tf_op jit(solution)/shard_map/translate/pallas_call | solution.py:422
  104.8 3.7 %all-to-all-start.2 = ((f32[8,288,128]{2,1,0:T(8,128)}), f32[8,288,128]{2,1,0:T(8,128)S(1)}, u32[]{:S(2)}, u32[]{:S(2)}) async-start(f32[8,288,128]{2,1,0:T(8,128)} %translate.1), calls=%async_computation.2 | async-start | bytes 2359296 | tf_op jit(solution)/shard_map/all_to_all | solution.py:438
  108.5 1.2 place.2
  109.7 17.1 %all-to-all-done.2.recv = f32[8,288,128]{2,1,0:T(8,128)S(1)} async-done(((f32[8,288,128]{2,1,0:T(8,128)}), f32[8,288,128]{2,1,0:T(8,128)S(1)}, u32[]{:S(2)}, u32[]{:S(2)}) %all-to-all-start.2) | async-done | bytes 1179680 | tf_op jit(solution)/shard_map/all_to_all | solution.py:438
  126.8 1.2 place.3
  (31 shorter events, 0.1 us)
Async XLA Ops:
  4.8 6.0 %copy-start.5 = (s32[32,48]{1,0:T(8,128)S(1)}, s32[32,48]{1,0:T(8,128)}, u32[]{:S(2)}) copy-start(s32[32,48]{1,0:T(8,128)} %param.18) | copy-start | bytes 18436
  4.9 6.0 %copy-start.6 = (s32[32,48]{1,0:T(8,128)S(1)}, s32[32,48]{1,0:T(8,128)}, u32[]{:S(2)}) copy-start(s32[32,48]{1,0:T(8,128)} %param.17) | copy-start | bytes 18436
  4.9 50.0 %all-to-all-start = ((f32[16,392,128]{2,1,0:T(8,128)}), f32[16,392,128]{2,1,0:T(8,128)S(1)}, u32[]{:S(2)}, u32[]{:S(2)}) async-start(f32[16,392,128]{2,1,0:T(8,128)} %get-tuple-element.10), calls=%async_computation | async-start | bytes 6422528 | tf_op jit(solution)/shard_map/all_to_all | solution.py:376
  11.1 20.1 %copy-start.10 = (s32[16]{0:T(128)S(1)}, s32[16]{0:T(128)}, u32[]{:S(2)}) copy-start(s32[16]{0:T(128)} %constant.39.clone) | copy-start | bytes 196
  11.1 20.2 %copy-start.9 = (f32[8]{0:T(128)S(1)}, f32[8]{0:T(128)}, u32[]{:S(2)}) copy-start(f32[8]{0:T(128)} %constant.50) | copy-start | bytes 100
  11.1 20.2 %copy-start.7 = (f32[8,384]{1,0:T(8,128)S(1)}, f32[8,384]{1,0:T(8,128)}, u32[]{:S(2)}) copy-start(f32[8,384]{1,0:T(8,128)} %constant.49) | copy-start | bytes 36868
  11.1 20.2 %copy-start.8 = (f32[16]{0:T(128)S(1)}, f32[16]{0:T(128)}, u32[]{:S(2)}) copy-start(f32[16]{0:T(128)} %constant.51) | copy-start | bytes 196
  11.1 43.8 %copy-start.4 = (s32[1,128]{1,0:T(1,128)S(1)}, s32[1,128]{1,0:T(1,128)}, u32[]{:S(2)}) copy-start(s32[1,128]{1,0:T(1,128)} %param.16) | copy-start | bytes 1540
  18.8 1.5 %copy-start.2 = (f32[316,16,128]{2,1,0:T(8,128)}, f32[316,16,128]{2,1,0:T(8,128)S(1)}, u32[]{:S(2)}) copy-start(f32[316,16,128]{2,1,0:T(8,128)S(1)} %get-tuple-element.11) | copy-start | bytes 7766020
  20.3 23.3 %collective-permute-start.6 = (f32[24,128]{1,0:T(8,128)S(1)}, f32[24,128]{1,0:T(8,128)S(1)}, u32[]{:S(2)}, u32[]{:S(2)}) collective-permute-start(f32[24,128]{1,0:T(8,128)S(1)} %get-tuple-element.9), channel_id=1, source_target_pairs={{0,112},{16,96},{32,80},{48,64},{64,48},{80,32},{96,16},{112,0},{1... | collective-permute-start | bytes 36872 | tf_op jit(solution)/shard_map/ppermute | solution.py:395
  25.4 18.1 %collective-permute-start.5 = (f32[24,128]{1,0:T(8,128)S(1)}, f32[24,128]{1,0:T(8,128)S(1)}, u32[]{:S(2)}, u32[]{:S(2)}) collective-permute-start(f32[24,128]{1,0:T(8,128)S(1)} %get-tuple-element.9), channel_id=1, source_target_pairs={{0,96},{16,112},{32,64},{48,80},{64,32},{80,48},{96,0},{112,16},{1... | collective-permute-start | bytes 36872 | tf_op jit(solution)/shard_map/ppermute | solution.py:395
  26.2 17.3 %collective-permute-start.4 = (f32[24,128]{1,0:T(8,128)S(1)}, f32[24,128]{1,0:T(8,128)S(1)}, u32[]{:S(2)}, u32[]{:S(2)}) collective-permute-start(f32[24,128]{1,0:T(8,128)S(1)} %get-tuple-element.9), channel_id=1, source_target_pairs={{0,80},{16,64},{32,112},{48,96},{64,16},{80,0},{96,48},{112,32},{1... | collective-permute-start | bytes 36872 | tf_op jit(solution)/shard_map/ppermute | solution.py:395
  29.2 14.4 %collective-permute-start.3 = (f32[24,128]{1,0:T(8,128)S(1)}, f32[24,128]{1,0:T(8,128)S(1)}, u32[]{:S(2)}, u32[]{:S(2)}) collective-permute-start(f32[24,128]{1,0:T(8,128)S(1)} %get-tuple-element.9), channel_id=1, source_target_pairs={{0,64},{16,80},{32,96},{48,112},{64,0},{80,16},{96,32},{112,48},{1... | collective-permute-start | bytes 36872 | tf_op jit(solution)/shard_map/ppermute | solution.py:395
  29.7 3.7 %collective-permute-start = (f32[24,128]{1,0:T(8,128)S(1)}, f32[24,128]{1,0:T(8,128)S(1)}, u32[]{:S(2)}, u32[]{:S(2)}) collective-permute-start(f32[24,128]{1,0:T(8,128)S(1)} %get-tuple-element.9), channel_id=1, source_target_pairs={{0,16},{16,0},{32,48},{48,32},{64,80},{80,64},{96,112},{112,96},{1... | collective-permute-start | bytes 36872 | tf_op jit(solution)/shard_map/ppermute | solution.py:395
  33.4 5.2 %collective-permute-start.1 = (f32[24,128]{1,0:T(8,128)S(1)}, f32[24,128]{1,0:T(8,128)S(1)}, u32[]{:S(2)}, u32[]{:S(2)}) collective-permute-start(f32[24,128]{1,0:T(8,128)S(1)} %get-tuple-element.9), channel_id=1, source_target_pairs={{0,32},{16,48},{32,0},{48,16},{64,96},{80,112},{96,64},{112,80},{1... | collective-permute-start | bytes 36872 | tf_op jit(solution)/shard_map/ppermute | solution.py:395
  38.6 4.9 %collective-permute-start.2 = (f32[24,128]{1,0:T(8,128)S(1)}, f32[24,128]{1,0:T(8,128)S(1)}, u32[]{:S(2)}, u32[]{:S(2)}) collective-permute-start(f32[24,128]{1,0:T(8,128)S(1)} %get-tuple-element.9), channel_id=1, source_target_pairs={{0,48},{16,32},{32,16},{48,0},{64,112},{80,96},{96,80},{112,64},{1... | collective-permute-start | bytes 36872 | tf_op jit(solution)/shard_map/ppermute | solution.py:395
  54.9 31.9 %copy-start.3 = (f32[316,16,128]{2,1,0:T(8,128)S(1)}, f32[316,16,128]{2,1,0:T(8,128)}, u32[]{:S(2)}) copy-start(f32[316,16,128]{2,1,0:T(8,128)} %copy-done.2) | copy-start | bytes 7766020
  61.2 25.7 %copy-start = (f32[8,288,128]{2,1,0:T(8,128)}, f32[8,288,128]{2,1,0:T(8,128)S(1)}, u32[]{:S(2)}) copy-start(f32[8,288,128]{2,1,0:T(8,128)S(1)} %phi.1.recv) | copy-start | bytes 3538948
  104.7 3.7 %copy-start.1 = (f32[8,288,128]{2,1,0:T(8,128)S(1)}, f32[8,288,128]{2,1,0:T(8,128)}, u32[]{:S(2)}) copy-start(f32[8,288,128]{2,1,0:T(8,128)} %copy-done) | copy-start | bytes 3538948
  104.8 22.1 %all-to-all-start.2 = ((f32[8,288,128]{2,1,0:T(8,128)}), f32[8,288,128]{2,1,0:T(8,128)S(1)}, u32[]{:S(2)}, u32[]{:S(2)}) async-start(f32[8,288,128]{2,1,0:T(8,128)} %translate.1), calls=%async_computation.2 | async-start | bytes 2359296 | tf_op jit(solution)/shard_map/all_to_all | solution.py:438

commit v5 on v4

--- a/solution.py
+++ b/solution.py
@@ -103,7 +103,7 @@
         copy.wait()
 
 
-def prepare_kernel(box, token, lists, table, out, done, lists_out, raw, sems):
+def prepare_kernel(box, token, lists, stencil, table, out, stencil_out, lists_out, raw, sems):
     me = box[0]
     n_off = table.shape[0]
     pair, half = me // 2, me % 2
@@ -115,7 +115,7 @@
             pltpu.make_async_copy(table.at[:, at // 3, :, lanes], raw.at[:, q], sems.at[q])
         )
         copies[-1].start()
-    done[...] = token[...]
+    stencil_out[...] = stencil[...]
     lists_out[...] = lists[...]
     for copy in copies:
         copy.wait()
@@ -134,21 +134,23 @@
 
 
 def phi_kernel(
-    owners, token, lists, table_high, table_low, cos_hbm, sin_hbm, recv, send_v,
-    total, fine, rows_v,  tables, cos_ref, sin_ref, kinds_v, kinds, sems,
+    owners, stencil, lists, cos_hbm, sin_hbm, recv, send_v, total, fine, rows_v, cos_ref, sin_ref, kinds_v, kinds, sems
 ):
-    pairs = [(table_high, tables.at[0]), (table_low, tables.at[1]), (cos_hbm, cos_ref), (sin_hbm, sin_ref)]
-    loads = [pltpu.make_async_copy(a, b, sems.at[i]) for i, (a, b) in enumerate(pairs)]
-    for copy in loads:
-        copy.start()
+    loads = [pltpu.make_async_copy(a, b, sems.at[i]) for i, (a, b) in enumerate(((cos_hbm, cos_ref), (sin_hbm, sin_ref)))]
+    for load in loads:
+        load.start()
     for s in range(16):
         kinds_v[s : s + 1, :] = recv[s, 384:385, :].astype(jnp.int32)
     copy = pltpu.make_async_copy(kinds_v, kinds, sems.at[4])
     copy.start()
     total[...] = jnp.zeros_like(total)
-    for load in loads[:2]:
-        load.wait()
-    table = jnp.concatenate([tables[0], tables[0], tables[1]], 0)
+    shape = (recv.shape[2] * 2, stencil.shape[1])
+    node = (lax.broadcasted_iota(jnp.int32, shape, 0) - stencil[6:7, :].astype(jnp.int32)) & (shape[0] - 1)
+    table = jnp.zeros(shape, jnp.float32)
+    for i in range(6):
+        table = jnp.where(node == i, stencil[i : i + 1, :], table)
+    high, low = split(table)
+    table = jnp.concatenate([high, high, low], 0)
 
     def product(s):
         high, low = split(jnp.concatenate([recv[s, 0:192, :], recv[s, 192:384, :]], 1))
@@ -166,7 +168,7 @@
             total[owner, 16:24] += cos_ref[octant, 8:16] * f[16:24] + sin_ref[octant, 8:16] * swapped
 
     fine[0] = product(0)
-    for load in loads[2:]:
+    for load in loads:
         load.wait()
     copy.wait()
 
@@ -178,7 +180,7 @@
         add(s + 1, fine.at[1])
         return carry
 
-    lax.fori_loop(0, 8, two, 0, unroll=2)
+    lax.fori_loop(0, 8, two, 0, unroll=4)
 
     def parent(p, carry):
         for l in range(3):
@@ -195,7 +197,7 @@
 
     left = lax.broadcasted_iota(jnp.int32, (8, 128), 1) < 64
     for q in range(4):
-        lax.fori_loop(8 * q, 8 * q + 8, parent, 0)
+        lax.fori_loop(8 * q, 8 * q + 8, parent, 0, unroll=4)
         for r in range(4):
             at = 72 * 8 * q + 64 + 2 * r
             re, im = rows_v[pl.ds(at, 8, stride=72), :], rows_v[pl.ds(at + 1, 8, stride=72), :]
@@ -210,7 +212,8 @@
 
     def load(b):
         rows = pl.ds(pl.multiple_of(24 * b, 8), 24)
-        return pltpu.make_async_copy(lists.at[lax.bitwise_xor(me, b)], idx.at[rows], load_sems.at[b])
+        away = lax.bitwise_xor(me, b)
+        return pltpu.make_async_copy(lists.at[2 * (away & 3) + (away >> 2)], idx.at[rows], load_sems.at[b])
 
     for b in range(8):
         load(jnp.int32(b)).start()
@@ -355,7 +358,12 @@
     theta_table = lagrange_table(n_t1, n_t2, False).reshape(n_samp, band, n_t1)
     parts = [theta_table[:, 0:8].reshape(-1, n_t1), theta_table[:, 8:12].reshape(-1, n_t1)]
     theta_high, theta_low = high_low(np.concatenate(parts))
-    phi_high, phi_low = high_low(lagrange_table(n_p1, n_p2, True).T)
+    phi_table = lagrange_table(n_p1, n_p2, True)
+    first = np.arange(n_p2) * n_p1 // n_p2 - 2
+    stencil = np.zeros((8, n_p2), np.float32)
+    for i in range(6):
+        stencil[i] = phi_table[np.arange(n_p2), (first + i) % n_p1]
+    stencil[6] = first % n_p1
 
     sent = (n_samp, 48 * count + 8, 128)
     bands, token = pl.pallas_call(
@@ -377,33 +385,33 @@
 
     cos_part, sin_part = phase_tables(samp, n_t2, n_p2)
     lists = jnp.concatenate([far_boxes.T * 24, offsets.T * 16], 0).reshape(24, 128).astype(f32)
-    factor, token, lists = pl.pallas_call(
+    factor, stencil, lists = pl.pallas_call(
         prepare_kernel,
-        in_specs=[smem(), vmem(), vmem(), anywhere()],
+        in_specs=[smem(), vmem(), vmem(), vmem(), anywhere()],
         out_specs=[vmem()] * 3,
         out_shape=[
             pltpu.VMEM((n_off, 16, 128), f32),
-            jax.ShapeDtypeStruct((8, 128), f32),
+            jax.ShapeDtypeStruct(stencil.shape, f32),
             jax.ShapeDtypeStruct((24, 128), f32),
         ],
         scratch_shapes=[pltpu.VMEM((n_off, 5, 2, 128), f32), pltpu.SemaphoreType.DMA((5,))],
         compiler_params=params(6),
         cost_estimate=pl.CostEstimate(flops=10**7, bytes_accessed=10**7, transcendentals=0),
         name="prepare",
-    )(box.reshape(1), token, lists, far_away(translation.transpose(0, 2, 1, 3)))
-    pairs = [[(i, i ^ k) for i in range(n_box)] for k in range(1, n_box)]
-    lists = jnp.stack([lists] + [lax.ppermute(lists, "box", p) for p in pairs]).astype(jnp.int32)
+    )(box.reshape(1), token, lists, stencil, far_away(translation.transpose(0, 2, 1, 3)))
+    pairs = [[(i, i ^ k) for i in range(n_box)] for k in range(n_box)]
+    lists = jnp.stack([lists, lax.ppermute(lists, "box", pairs[4])])
+    lists = jnp.concatenate([lists] + [lax.ppermute(lists, "box", pairs[k]) for k in (1, 2, 3)]).astype(jnp.int32)
 
     send = pl.pallas_call(
         phi_kernel,
-        in_specs=[smem(), vmem()] + [anywhere()] * 5 + [vmem()],
+        in_specs=[smem(), vmem()] + [anywhere()] * 3 + [vmem()],
         out_specs=vmem(),
         out_shape=pltpu.VMEM((n_box, 9 * parents, 128), f32),
         scratch_shapes=[
             pltpu.VMEM((parents, 24, n_p2), f32),
             pltpu.VMEM((2, 24 * count, n_p2), f32),
             pltpu.VMEM((parents * 72, 128), f32),
-            pltpu.VMEM((2, n_p1, n_p2), bf16),
             pltpu.VMEM(cos_part.shape, f32),
             pltpu.VMEM(cos_part.shape, f32),
             pltpu.VMEM((n_samp, 128), jnp.int32),
@@ -413,8 +421,7 @@
         compiler_params=params(12),
         name="phi",
     )(
-        parent_map[0], token, far_away(lists),
-        *[far_away(x) for x in (phi_high, phi_low, cos_part, sin_part)], held(bands),
+        parent_map[0], stencil, far_away(lists), far_away(cos_part), far_away(sin_part), held(bands),
     )
 
     everywhere = lax.all_to_all(send, "box", 0, 0)

time: 129 us -> 128 us (level)
  starting transfers between devices: 26.4 us -> 16.9 us
  waiting for transfers between devices: 32.6 us -> 42 us
    ppermute x7 -> x4, waiting for transfers between devices: 4.85 us -> 15.8 us  [the longest x1 11.8 us: shards(): lists = jnp.stack([lists, lax.ppermute(lists, 'box', pairs[4])])]
    ppermute x7 -> x4, starting transfers between devices: 16.7 us -> 7.07 us  [the longest x3 4.09 us: shards(): lax.ppermute(lists, 'box', pairs[k])]
    all_to_all x1, waiting for transfers between devices: 10.6 us -> 9.05 us  [shards(): bands = lax.all_to_all(bands, 'samp', 0, 0)]
  transfers between devices with their start and end apart: 9 -> 6, of which waited for: 5 -> 5; matrix products, arithmetic and copies ran while one was open for 2% -> 2% of each run, Pallas kernels for 7% -> 7%
where the time goes in v5:
time: 128 us; the launch traced here: 127 us
  waiting for transfers between devices  42 us (33%)
  Pallas kernels  37.9 us (30%)
  blocking collectives  25.6 us (20%)
  starting transfers between devices  16.9 us (13%)
  other arithmetic  2.38 us (2%)
  local copies, waits for them, and re-layouts  1.74 us (1%)
    all_to_all x1, blocking collectives, shards(): everywhere = lax.all_to_all(send, 'box', 0, 0)  25.6 us
    pallas_call x1, Pallas kernels, shards(): pl.pallas_call(translate_kernel, in_specs=[smem(), anywhere(), vmem(), vm...  18 us
    all_to_all x1, waiting for transfers between devices, shards(): back = lax.all_to_all(back, 'box', 0, 0)  17.1 us
    ppermute x1, waiting for transfers between devices, shards(): lists = jnp.stack([lists, lax.ppermute(lists, 'box', pairs[4])])  11.8 us
    all_to_all x1, waiting for transfers between devices, shards(): bands = lax.all_to_all(bands, 'samp', 0, 0)  9.05 us
    pallas_call x1, Pallas kernels, shards(): pl.pallas_call(prepare_kernel, in_specs=[smem(), vmem(), vmem(), vmem(),...  7.61 us
    all_to_all x1, starting transfers between devices, shards(): bands = lax.all_to_all(bands, 'samp', 0, 0)  6.08 us
    pallas_call x1, Pallas kernels, shards(): pl.pallas_call(phi_kernel, in_specs=[smem(), vmem()] + [anywhere()] * 3 +...  5.61 us
  transfers between devices with their start and end apart: 6, of which 5 were waited for; matrix products, arithmetic and copies ran while one was open for 2% of the time, Pallas kernels for 7%

profile of v5, /device:TPU:32, one launch (start us, length us, event | category | flops | bytes accessed | tf_op | source)
XLA Modules:
  0.0 127.3 jit_solution(12334164938521057442)
XLA Ops:
  0.6 4.2 %theta.1 = (f32[16,392,128]{2,1,0:T(8,128)}, f32[8,128]{1,0:T(8,128)S(1)}) custom-call(s32[1,8]{1,0:T(1,128)} %bitcast.22, bf16[192,128]{1,0:T(8,128)(2,1)} %constant.35.clone.table_high, bf16[192,128]{1,0:T(8,128)(2,1)} %constant.36.clone.table_low, f32[8,2,128,256]{3,2,1,0:T(8,128)} %child.1), custom_call_target="tpu_custom_call" | custom-call | tf_op jit(solution)/shard_map/theta/pallas_call | solution.py:369
  4.9 0.0 copy-start.6
  4.9 0.0 copy-start.4
  4.9 6.1 %all-to-all-start = ((f32[16,392,128]{2,1,0:T(8,128)}), f32[16,392,128]{2,1,0:T(8,128)S(1)}, u32[]{:S(2)}, u32[]{:S(2)}) async-start(f32[16,392,128]{2,1,0:T(8,128)} %get-tuple-element.10), calls=%async_computation | async-start | bytes 6422528 | tf_op jit(solution)/shard_map/all_to_all | solution.py:384
  11.0 0.1 add_convert_fusion
  11.1 0.1 copy.16
  11.2 0.1 convert_element_type.12.lists
  11.3 0.0 copy-done.4
  11.3 0.0 copy-start.11
  11.3 0.0 copy-start.10
  11.3 0.0 copy-start.8
  11.3 0.0 copy-start.9
  11.3 7.6 %prepare.1 = (f32[316,16,128]{2,1,0:T(8,128)S(1)}, f32[8,384]{1,0:T(8,128)S(1)}, f32[24,128]{1,0:T(8,128)S(1)}) custom-call(s32[1]{0:T(128)} %bitcast.1.box.box_id, f32[8,128]{1,0:T(8,128)S(1)} %get-tuple-element.7.token, f32[24,128]{1,0:T(8,128)S(1)} %convert_element_type.12.lists, f32[8,384]{1,0:T(8,128)S(1)} %copy-done.4, f32[316,12,2,384]{3,2,1,0:T(2,128)} %bitcast.18), custom_call_target="tpu_custom_call" | custom-call | flops 10000000 | bytes 10000000 | tf_op jit(solution)/shard_map/prepare/pallas_call | solution.py:388
  19.0 1.5 %copy-done.2 = f32[316,16,128]{2,1,0:T(8,128)} copy-done((f32[316,16,128]{2,1,0:T(8,128)}, f32[316,16,128]{2,1,0:T(8,128)S(1)}, u32[]{:S(2)}) %copy-start.2) | copy-done | bytes 2588696
  20.5 3.0 %collective-permute-start = (f32[24,128]{1,0:T(8,128)S(1)}, f32[24,128]{1,0:T(8,128)S(1)}, u32[]{:S(2)}, u32[]{:S(2)}) collective-permute-start(f32[24,128]{1,0:T(8,128)S(1)} %get-tuple-element.9), channel_id=1, source_target_pairs={{0,64},{16,80},{32,96},{48,112},{64,0},{80,16},{96,32},{112,48},{1... | collective-permute-start | bytes 36872 | tf_op jit(solution)/shard_map/ppermute | solution.py:403
  23.5 0.1 broadcast_multiply_fusion
  23.6 1.5 %sine_multiply_fusion = (f32[8,16,384]{2,1,0:T(8,128)}, f32[8,16,384]{2,1,0:T(8,128)}) fusion(f32[16]{0:T(128)S(1)} %copy-done.9, f32[8,16]{1,0:T(8,128)S(1)} %broadcast_multiply_fusion, f32[8,384]{1,0:T(8,128)S(1)} %copy-done.8, f32[16]{0:T(128)S(1)} %get-tuple-element.14), kind=kLoop, calls=%fused_computation | loop fusion | flops 196608 | bytes 406144 | tf_op jit(solution)/shard_map/mul | solution.py:322
  25.1 11.8 %collective-permute-done = f32[24,128]{1,0:T(8,128)S(1)} collective-permute-done((f32[24,128]{1,0:T(8,128)S(1)}, f32[24,128]{1,0:T(8,128)S(1)}, u32[]{:S(2)}, u32[]{:S(2)}) %collective-permute-start) | collective-permute-done | bytes 12320 | tf_op jit(solution)/shard_map/ppermute | solution.py:403
  36.9 2.8 %collective-permute-start.3 = (f32[2,24,128]{2,1,0:T(8,128)S(1)}, f32[2,24,128]{2,1,0:T(8,128)S(1)}, u32[]{:S(2)}, u32[]{:S(2)}) collective-permute-start(f32[2,24,128]{2,1,0:T(8,128)S(1)} %pad_maximum_fusion), channel_id=1, source_target_pairs={{0,48},{16,32},{32,16},{48,0},{64,112},{80,96},{96,80},{112,64},{1... | collective-permute-start | bytes 73736 | tf_op jit(solution)/shard_map/ppermute | solution.py:404
  39.7 0.8 collective-permute-start.2
  40.5 0.5 collective-permute-start.1
  41.0 3.3 %collective-permute-done.1 = f32[2,24,128]{2,1,0:T(8,128)S(1)} collective-permute-done((f32[2,24,128]{2,1,0:T(8,128)S(1)}, f32[2,24,128]{2,1,0:T(8,128)S(1)}, u32[]{:S(2)}, u32[]{:S(2)}) %collective-permute-start.1) | collective-permute-done | bytes 24608 | tf_op jit(solution)/shard_map/ppermute | solution.py:404
  44.3 0.7 collective-permute-done.2
  45.0 0.6 convert_element_type.13.lists
  45.7 9.1 %all-to-all-done.recv = f32[16,392,128]{2,1,0:T(8,128)S(1)} async-done(((f32[16,392,128]{2,1,0:T(8,128)}), f32[16,392,128]{2,1,0:T(8,128)S(1)}, u32[]{:S(2)}, u32[]{:S(2)}) %all-to-all-start) | async-done | bytes 3211296 | tf_op jit(solution)/shard_map/all_to_all | solution.py:384
  54.7 5.6 %phi.1.recv = f32[8,288,128]{2,1,0:T(8,128)S(1)} custom-call(s32[128]{0:T(128)S(1)} %bitcast.17, f32[8,384]{1,0:T(8,128)S(1)} %get-tuple-element.8.stencil, s32[8,24,128]{2,1,0:T(8,128)} %convert_element_type.13.lists, f32[8,16,384]{2,1,0:T(8,128)} %get-tuple-element.13.cos_hbm, f32[8,16,384]{2,1,0:T(8,128)} %get-tuple-element.12.sin_hbm, ...), custom_call_target="tpu_custom_call" | custom-call | tf_op jit(solution)/shard_map/phi/pallas_call | solution.py:406
  60.4 25.6 %all_to_all.15.recv = f32[8,288,128]{2,1,0:T(8,128)S(1)} all-to-all(f32[8,288,128]{2,1,0:T(8,128)S(1)} %phi.1.recv), channel_id=1, replica_groups=mesh['box'=8,'samp'=16] {'box'}, dimensions={0} | all-to-all | bytes 2359296 | tf_op jit(solution)/shard_map/all_to_all | solution.py:427
  86.0 18.0 %translate.1 = f32[8,288,128]{2,1,0:T(8,128)} custom-call(s32[1]{0:T(128)} %bitcast.1.box.box_id, s32[8,24,128]{2,1,0:T(8,128)} %convert_element_type.13.lists, f32[8,288,128]{2,1,0:T(8,128)S(1)} %all_to_all.15.recv, f32[5056,128]{1,0:T(8,128)S(1)} %bitcast.15), custom_call_target="tpu_custom_call" | custom-call | tf_op jit(solution)/shard_map/translate/pallas_call | solution.py:429
  104.0 3.7 %all-to-all-start.2 = ((f32[8,288,128]{2,1,0:T(8,128)}), f32[8,288,128]{2,1,0:T(8,128)S(1)}, u32[]{:S(2)}, u32[]{:S(2)}) async-start(f32[8,288,128]{2,1,0:T(8,128)} %translate.1), calls=%async_computation.2 | async-start | bytes 2359296 | tf_op jit(solution)/shard_map/all_to_all | solution.py:445
  107.7 1.2 place.2
  108.9 17.1 %all-to-all-done.2.recv = f32[8,288,128]{2,1,0:T(8,128)S(1)} async-done(((f32[8,288,128]{2,1,0:T(8,128)}), f32[8,288,128]{2,1,0:T(8,128)S(1)}, u32[]{:S(2)}, u32[]{:S(2)}) %all-to-all-start.2) | async-done | bytes 1179680 | tf_op jit(solution)/shard_map/all_to_all | solution.py:445
  126.0 1.2 place.3
  (25 shorter events, 0.1 us)
Async XLA Ops:
  4.9 6.1 %copy-start.6 = (s32[32,48]{1,0:T(8,128)S(1)}, s32[32,48]{1,0:T(8,128)}, u32[]{:S(2)}) copy-start(s32[32,48]{1,0:T(8,128)} %param.17) | copy-start | bytes 18436
  4.9 6.1 %copy-start.7 = (s32[32,48]{1,0:T(8,128)S(1)}, s32[32,48]{1,0:T(8,128)}, u32[]{:S(2)}) copy-start(s32[32,48]{1,0:T(8,128)} %param.16) | copy-start | bytes 18436
  4.9 6.4 %copy-start.4 = (f32[8,384]{1,0:T(8,128)S(1)}, f32[8,384]{1,0:T(8,128)}, u32[]{:S(2)}) copy-start(f32[8,384]{1,0:T(8,128)} %constant.41.clone.stencil) | copy-start | bytes 36868
  4.9 49.8 %all-to-all-start = ((f32[16,392,128]{2,1,0:T(8,128)}), f32[16,392,128]{2,1,0:T(8,128)S(1)}, u32[]{:S(2)}, u32[]{:S(2)}) async-start(f32[16,392,128]{2,1,0:T(8,128)} %get-tuple-element.10), calls=%async_computation | async-start | bytes 6422528 | tf_op jit(solution)/shard_map/all_to_all | solution.py:384
  11.3 12.2 %copy-start.11 = (s32[16]{0:T(128)S(1)}, s32[16]{0:T(128)}, u32[]{:S(2)}) copy-start(s32[16]{0:T(128)} %constant.37.clone) | copy-start | bytes 196
  11.3 12.2 %copy-start.10 = (f32[8]{0:T(128)S(1)}, f32[8]{0:T(128)}, u32[]{:S(2)}) copy-start(f32[8]{0:T(128)} %constant.47) | copy-start | bytes 100
  11.3 12.3 %copy-start.8 = (f32[8,384]{1,0:T(8,128)S(1)}, f32[8,384]{1,0:T(8,128)}, u32[]{:S(2)}) copy-start(f32[8,384]{1,0:T(8,128)} %constant.46) | copy-start | bytes 36868
  11.3 12.3 %copy-start.9 = (f32[16]{0:T(128)S(1)}, f32[16]{0:T(128)}, u32[]{:S(2)}) copy-start(f32[16]{0:T(128)} %constant.48) | copy-start | bytes 196
  11.3 43.4 %copy-start.5 = (s32[1,128]{1,0:T(1,128)S(1)}, s32[1,128]{1,0:T(1,128)}, u32[]{:S(2)}) copy-start(s32[1,128]{1,0:T(1,128)} %param.15) | copy-start | bytes 1540
  19.0 1.5 %copy-start.2 = (f32[316,16,128]{2,1,0:T(8,128)}, f32[316,16,128]{2,1,0:T(8,128)S(1)}, u32[]{:S(2)}) copy-start(f32[316,16,128]{2,1,0:T(8,128)S(1)} %get-tuple-element.11) | copy-start | bytes 7766020
  20.5 16.5 %collective-permute-start = (f32[24,128]{1,0:T(8,128)S(1)}, f32[24,128]{1,0:T(8,128)S(1)}, u32[]{:S(2)}, u32[]{:S(2)}) collective-permute-start(f32[24,128]{1,0:T(8,128)S(1)} %get-tuple-element.9), channel_id=1, source_target_pairs={{0,64},{16,80},{32,96},{48,112},{64,0},{80,16},{96,32},{112,48},{1... | collective-permute-start | bytes 36872 | tf_op jit(solution)/shard_map/ppermute | solution.py:403
  36.9 8.1 %collective-permute-start.3 = (f32[2,24,128]{2,1,0:T(8,128)S(1)}, f32[2,24,128]{2,1,0:T(8,128)S(1)}, u32[]{:S(2)}, u32[]{:S(2)}) collective-permute-start(f32[2,24,128]{2,1,0:T(8,128)S(1)} %pad_maximum_fusion), channel_id=1, source_target_pairs={{0,48},{16,32},{32,16},{48,0},{64,112},{80,96},{96,80},{112,64},{1... | collective-permute-start | bytes 73736 | tf_op jit(solution)/shard_map/ppermute | solution.py:404
  39.7 5.3 %collective-permute-start.2 = (f32[2,24,128]{2,1,0:T(8,128)S(1)}, f32[2,24,128]{2,1,0:T(8,128)S(1)}, u32[]{:S(2)}, u32[]{:S(2)}) collective-permute-start(f32[2,24,128]{2,1,0:T(8,128)S(1)} %pad_maximum_fusion), channel_id=1, source_target_pairs={{0,32},{16,48},{32,0},{48,16},{64,96},{80,112},{96,64},{112,80},{1... | collective-permute-start | bytes 73736 | tf_op jit(solution)/shard_map/ppermute | solution.py:404
  40.5 3.8 %collective-permute-start.1 = (f32[2,24,128]{2,1,0:T(8,128)S(1)}, f32[2,24,128]{2,1,0:T(8,128)S(1)}, u32[]{:S(2)}, u32[]{:S(2)}) collective-permute-start(f32[2,24,128]{2,1,0:T(8,128)S(1)} %pad_maximum_fusion), channel_id=1, source_target_pairs={{0,16},{16,0},{32,48},{48,32},{64,80},{80,64},{96,112},{112,96},{1... | collective-permute-start | bytes 73736 | tf_op jit(solution)/shard_map/ppermute | solution.py:404
  54.7 31.2 %copy-start.3 = (f32[316,16,128]{2,1,0:T(8,128)S(1)}, f32[316,16,128]{2,1,0:T(8,128)}, u32[]{:S(2)}) copy-start(f32[316,16,128]{2,1,0:T(8,128)} %copy-done.2) | copy-start | bytes 7766020
  60.4 25.6 %copy-start = (f32[8,288,128]{2,1,0:T(8,128)}, f32[8,288,128]{2,1,0:T(8,128)S(1)}, u32[]{:S(2)}) copy-start(f32[8,288,128]{2,1,0:T(8,128)S(1)} %phi.1.recv) | copy-start | bytes 3538948
  103.9 3.7 %copy-start.1 = (f32[8,288,128]{2,1,0:T(8,128)S(1)}, f32[8,288,128]{2,1,0:T(8,128)}, u32[]{:S(2)}) copy-start(f32[8,288,128]{2,1,0:T(8,128)} %copy-done) | copy-start | bytes 3538948
  104.0 22.1 %all-to-all-start.2 = ((f32[8,288,128]{2,1,0:T(8,128)}), f32[8,288,128]{2,1,0:T(8,128)S(1)}, u32[]{:S(2)}, u32[]{:S(2)}) async-start(f32[8,288,128]{2,1,0:T(8,128)} %translate.1), calls=%async_computation.2 | async-start | bytes 2359296 | tf_op jit(solution)/shard_map/all_to_all | solution.py:445

commit v6 on v5

--- a/solution.py
+++ b/solution.py
@@ -243,7 +243,8 @@
         acc = [[jnp.zeros((8, 128), jnp.float32) for _ in range(3)] for _ in range(8)]
         for j in range(n_far):
             for h in range(8):
-                f, o = index(j, b, 8 * i + h), index(n_far + j, b, 8 * i + h)
+                o = index(n_far + j, b, 8 * i + h)
+                f = index(j, b, 8 * i + h)
                 t = factor[pl.ds(o, 8), :]
                 acc[h][0] += t * source[pl.ds(f, 8), :]
                 acc[h][1] += t * source[pl.ds(f + 8, 8), :]
@@ -411,24 +412,24 @@
         scratch_shapes=[
             pltpu.VMEM((parents, 24, n_p2), f32),
             pltpu.VMEM((2, 24 * count, n_p2), f32),
-            pltpu.VMEM((parents * 72, 128), f32),
+            pltpu.VMEM((parents * 72 + 64, 128), f32),
             pltpu.VMEM(cos_part.shape, f32),
             pltpu.VMEM(cos_part.shape, f32),
-            pltpu.VMEM((n_samp, 128), jnp.int32),
-            pltpu.SMEM((n_samp, 128), jnp.int32),
+            pltpu.VMEM((n_samp + 8, 128), jnp.int32),
+            pltpu.SMEM((n_samp + 8, 128), jnp.int32),
             pltpu.SemaphoreType.DMA((10,)),
         ],
         compiler_params=params(12),
         name="phi",
     )(
-        parent_map[0], stencil, far_away(lists), far_away(cos_part), far_away(sin_part), held(bands),
+        parent_map[0], stencil, lists, far_away(cos_part), far_away(sin_part), held(bands),
     )
 
     everywhere = lax.all_to_all(send, "box", 0, 0)
     n_all = n_box * parents
     back = pl.pallas_call(
         translate_kernel,
-        in_specs=[smem(), anywhere(), vmem(), vmem()],
+        in_specs=[smem(), vmem(), vmem(), vmem()],
         out_specs=anywhere(),
         out_shape=pltpu.HBM((n_box, 9 * parents, 128), f32),
         scratch_shapes=[
@@ -441,7 +442,7 @@
         ],
         compiler_params=params(12),
         name="translate",
-    )(box.reshape(1), far_away(lists), held(everywhere), held(factor.reshape(n_off * 16, 128)))
+    )(box.reshape(1), lists, held(everywhere), held(factor.reshape(n_off * 16, 128)))
     back = lax.all_to_all(back, "box", 0, 0)
     shape = (parents, band, 2, n_p2)
     place = pl.pallas_call(
@@ -450,7 +451,7 @@
         out_specs=anywhere(),
         out_shape=pltpu.HBM(shape, f32),
         scratch_shapes=[
-            pltpu.VMEM((8 * parents, 128), f32),
+            pltpu.VMEM((8 * parents + 8, 128), f32),
             pltpu.VMEM(shape, f32),
             pltpu.SemaphoreType.DMA((4,)),
         ],

time: 128 us -> 128 us (level)
  no operation moved by 1% of the time
where the time goes in v6:
time: 128 us; the launch traced here: 127 us
  waiting for transfers between devices  42.6 us (33%)
  Pallas kernels  37.9 us (30%)
  blocking collectives  25.6 us (20%)
  starting transfers between devices  16.9 us (13%)
  local copies, waits for them, and re-layouts  1.74 us (1%)
  other arithmetic  1.74 us (1%)
    all_to_all x1, blocking collectives, shards(): everywhere = lax.all_to_all(send, 'box', 0, 0)  25.6 us
    pallas_call x1, Pallas kernels, shards(): pl.pallas_call(translate_kernel, in_specs=[smem(), vmem(), vmem(), vmem()...  18 us
    all_to_all x1, waiting for transfers between devices, shards(): back = lax.all_to_all(back, 'box', 0, 0)  17.1 us
    ppermute x1, waiting for transfers between devices, shards(): lists = jnp.stack([lists, lax.ppermute(lists, 'box', pairs[4])])  11.8 us
    all_to_all x1, waiting for transfers between devices, shards(): bands = lax.all_to_all(bands, 'samp', 0, 0)  9.68 us
    pallas_call x1, Pallas kernels, shards(): pl.pallas_call(prepare_kernel, in_specs=[smem(), vmem(), vmem(), vmem(),...  7.61 us
    all_to_all x1, starting transfers between devices, shards(): bands = lax.all_to_all(bands, 'samp', 0, 0)  6.08 us
    pallas_call x1, Pallas kernels, shards(): pl.pallas_call(phi_kernel, in_specs=[smem(), vmem()] + [anywhere()] * 3 +...  5.64 us
  transfers between devices with their start and end apart: 6, of which 5 were waited for; matrix products, arithmetic and copies ran while one was open for 2% of the time, Pallas kernels for 7%

profile of v6, /device:TPU:32, one launch (start us, length us, event | category | flops | bytes accessed | tf_op | source)
XLA Modules:
  0.0 127.3 jit_solution(5611008314325689710)
XLA Ops:
  0.6 4.2 %theta.1 = (f32[16,392,128]{2,1,0:T(8,128)}, f32[8,128]{1,0:T(8,128)S(1)}) custom-call(s32[1,8]{1,0:T(1,128)} %bitcast.22, bf16[192,128]{1,0:T(8,128)(2,1)} %constant.35.clone.table_high, bf16[192,128]{1,0:T(8,128)(2,1)} %constant.36.clone.table_low, f32[8,2,128,256]{3,2,1,0:T(8,128)} %child.1), custom_call_target="tpu_custom_call" | custom-call | tf_op jit(solution)/shard_map/theta/pallas_call | solution.py:370
  4.9 0.0 copy-start.6
  4.9 0.0 copy-start.4
  4.9 6.1 %all-to-all-start = ((f32[16,392,128]{2,1,0:T(8,128)}), f32[16,392,128]{2,1,0:T(8,128)S(1)}, u32[]{:S(2)}, u32[]{:S(2)}) async-start(f32[16,392,128]{2,1,0:T(8,128)} %get-tuple-element.10), calls=%async_computation | async-start | bytes 6422528 | tf_op jit(solution)/shard_map/all_to_all | solution.py:385
  11.0 0.1 add_convert_fusion
  11.1 0.1 copy.16
  11.2 0.1 convert_element_type.12.lists
  11.3 0.0 copy-done.4
  11.3 0.0 copy-start.11
  11.3 0.0 copy-start.10
  11.3 0.0 copy-start.8
  11.3 0.0 copy-start.9
  11.3 7.6 %prepare.1 = (f32[316,16,128]{2,1,0:T(8,128)S(1)}, f32[8,384]{1,0:T(8,128)S(1)}, f32[24,128]{1,0:T(8,128)S(1)}) custom-call(s32[1]{0:T(128)} %bitcast.1.box.box_id, f32[8,128]{1,0:T(8,128)S(1)} %get-tuple-element.7.token, f32[24,128]{1,0:T(8,128)S(1)} %convert_element_type.12.lists, f32[8,384]{1,0:T(8,128)S(1)} %copy-done.4, f32[316,12,2,384]{3,2,1,0:T(2,128)} %bitcast.18), custom_call_target="tpu_custom_call" | custom-call | flops 10000000 | bytes 10000000 | tf_op jit(solution)/shard_map/prepare/pallas_call | solution.py:389
  19.0 1.5 %copy-done.2 = f32[316,16,128]{2,1,0:T(8,128)} copy-done((f32[316,16,128]{2,1,0:T(8,128)}, f32[316,16,128]{2,1,0:T(8,128)S(1)}, u32[]{:S(2)}) %copy-start.2) | copy-done | bytes 2588696
  20.5 3.0 %collective-permute-start = (f32[24,128]{1,0:T(8,128)S(1)}, f32[24,128]{1,0:T(8,128)S(1)}, u32[]{:S(2)}, u32[]{:S(2)}) collective-permute-start(f32[24,128]{1,0:T(8,128)S(1)} %get-tuple-element.9), channel_id=1, source_target_pairs={{0,64},{16,80},{32,96},{48,112},{64,0},{80,16},{96,32},{112,48},{1... | collective-permute-start | bytes 36872 | tf_op jit(solution)/shard_map/ppermute | solution.py:404
  23.5 0.1 broadcast_multiply_fusion
  23.6 1.5 %sine_multiply_fusion = (f32[8,16,384]{2,1,0:T(8,128)}, f32[8,16,384]{2,1,0:T(8,128)}) fusion(f32[16]{0:T(128)S(1)} %copy-done.9, f32[8,16]{1,0:T(8,128)S(1)} %broadcast_multiply_fusion, f32[8,384]{1,0:T(8,128)S(1)} %copy-done.8, f32[16]{0:T(128)S(1)} %get-tuple-element.14), kind=kLoop, calls=%fused_computation | loop fusion | flops 196608 | bytes 406144 | tf_op jit(solution)/shard_map/mul | solution.py:323
  25.1 11.8 %collective-permute-done = f32[24,128]{1,0:T(8,128)S(1)} collective-permute-done((f32[24,128]{1,0:T(8,128)S(1)}, f32[24,128]{1,0:T(8,128)S(1)}, u32[]{:S(2)}, u32[]{:S(2)}) %collective-permute-start) | collective-permute-done | bytes 12320 | tf_op jit(solution)/shard_map/ppermute | solution.py:404
  36.9 2.8 %collective-permute-start.3 = (f32[2,24,128]{2,1,0:T(8,128)S(1)}, f32[2,24,128]{2,1,0:T(8,128)S(1)}, u32[]{:S(2)}, u32[]{:S(2)}) collective-permute-start(f32[2,24,128]{2,1,0:T(8,128)S(1)} %pad_maximum_fusion), channel_id=1, source_target_pairs={{0,48},{16,32},{32,16},{48,0},{64,112},{80,96},{96,80},{112,64},{1... | collective-permute-start | bytes 73736 | tf_op jit(solution)/shard_map/ppermute | solution.py:405
  39.7 0.8 collective-permute-start.2
  40.5 0.5 collective-permute-start.1
  41.0 3.3 %collective-permute-done.1 = f32[2,24,128]{2,1,0:T(8,128)S(1)} collective-permute-done((f32[2,24,128]{2,1,0:T(8,128)S(1)}, f32[2,24,128]{2,1,0:T(8,128)S(1)}, u32[]{:S(2)}, u32[]{:S(2)}) %collective-permute-start.1) | collective-permute-done | bytes 24608 | tf_op jit(solution)/shard_map/ppermute | solution.py:405
  44.3 0.7 collective-permute-done.2
  45.1 9.7 %all-to-all-done.recv = f32[16,392,128]{2,1,0:T(8,128)S(1)} async-done(((f32[16,392,128]{2,1,0:T(8,128)}), f32[16,392,128]{2,1,0:T(8,128)S(1)}, u32[]{:S(2)}, u32[]{:S(2)}) %all-to-all-start) | async-done | bytes 3211296 | tf_op jit(solution)/shard_map/all_to_all | solution.py:385
  54.7 5.6 %phi.1.recv = f32[8,288,128]{2,1,0:T(8,128)S(1)} custom-call(s32[128]{0:T(128)S(1)} %bitcast.17, f32[8,384]{1,0:T(8,128)S(1)} %get-tuple-element.8.stencil, s32[8,24,128]{2,1,0:T(8,128)S(1)} %convert_element_type.13.lists, f32[8,16,384]{2,1,0:T(8,128)} %get-tuple-element.13.cos_hbm, f32[8,16,384]{2,1,0:T(8,128)} %get-tuple-element.12.sin_hbm, ...), custom_call_target="tpu_custom_call" | custom-call | tf_op jit(solution)/shard_map/phi/pallas_call | solution.py:407
  60.4 25.6 %all_to_all.15.recv = f32[8,288,128]{2,1,0:T(8,128)S(1)} all-to-all(f32[8,288,128]{2,1,0:T(8,128)S(1)} %phi.1.recv), channel_id=1, replica_groups=mesh['box'=8,'samp'=16] {'box'}, dimensions={0} | all-to-all | bytes 2359296 | tf_op jit(solution)/shard_map/all_to_all | solution.py:428
  86.0 18.0 %translate.1 = f32[8,288,128]{2,1,0:T(8,128)} custom-call(s32[1]{0:T(128)} %bitcast.1.box.box_id, s32[8,24,128]{2,1,0:T(8,128)S(1)} %convert_element_type.13.lists, f32[8,288,128]{2,1,0:T(8,128)S(1)} %all_to_all.15.recv, f32[5056,128]{1,0:T(8,128)S(1)} %bitcast.15), custom_call_target="tpu_custom_call" | custom-call | tf_op jit(solution)/shard_map/translate/pallas_call | solution.py:430
  104.0 0.0 copy-start.1
  104.0 3.7 %all-to-all-start.2 = ((f32[8,288,128]{2,1,0:T(8,128)}), f32[8,288,128]{2,1,0:T(8,128)S(1)}, u32[]{:S(2)}, u32[]{:S(2)}) async-start(f32[8,288,128]{2,1,0:T(8,128)} %translate.1), calls=%async_computation.2 | async-start | bytes 2359296 | tf_op jit(solution)/shard_map/all_to_all | solution.py:446
  107.7 1.2 place.2
  109.0 17.1 %all-to-all-done.2.recv = f32[8,288,128]{2,1,0:T(8,128)S(1)} async-done(((f32[8,288,128]{2,1,0:T(8,128)}), f32[8,288,128]{2,1,0:T(8,128)S(1)}, u32[]{:S(2)}, u32[]{:S(2)}) %all-to-all-start.2) | async-done | bytes 1179680 | tf_op jit(solution)/shard_map/all_to_all | solution.py:446
  126.1 1.2 place.3
  (25 shorter events, 0.1 us)
Async XLA Ops:
  4.9 6.1 %copy-start.6 = (s32[32,48]{1,0:T(8,128)S(1)}, s32[32,48]{1,0:T(8,128)}, u32[]{:S(2)}) copy-start(s32[32,48]{1,0:T(8,128)} %param.17) | copy-start | bytes 18436
  4.9 6.1 %copy-start.7 = (s32[32,48]{1,0:T(8,128)S(1)}, s32[32,48]{1,0:T(8,128)}, u32[]{:S(2)}) copy-start(s32[32,48]{1,0:T(8,128)} %param.16) | copy-start | bytes 18436
  4.9 6.4 %copy-start.4 = (f32[8,384]{1,0:T(8,128)S(1)}, f32[8,384]{1,0:T(8,128)}, u32[]{:S(2)}) copy-start(f32[8,384]{1,0:T(8,128)} %constant.41.clone.stencil) | copy-start | bytes 36868
  4.9 49.8 %all-to-all-start = ((f32[16,392,128]{2,1,0:T(8,128)}), f32[16,392,128]{2,1,0:T(8,128)S(1)}, u32[]{:S(2)}, u32[]{:S(2)}) async-start(f32[16,392,128]{2,1,0:T(8,128)} %get-tuple-element.10), calls=%async_computation | async-start | bytes 6422528 | tf_op jit(solution)/shard_map/all_to_all | solution.py:385
  11.3 12.2 %copy-start.11 = (s32[16]{0:T(128)S(1)}, s32[16]{0:T(128)}, u32[]{:S(2)}) copy-start(s32[16]{0:T(128)} %constant.37.clone) | copy-start | bytes 196
  11.3 12.2 %copy-start.10 = (f32[8]{0:T(128)S(1)}, f32[8]{0:T(128)}, u32[]{:S(2)}) copy-start(f32[8]{0:T(128)} %constant.47) | copy-start | bytes 100
  11.3 12.3 %copy-start.8 = (f32[8,384]{1,0:T(8,128)S(1)}, f32[8,384]{1,0:T(8,128)}, u32[]{:S(2)}) copy-start(f32[8,384]{1,0:T(8,128)} %constant.46) | copy-start | bytes 36868
  11.3 12.3 %copy-start.9 = (f32[16]{0:T(128)S(1)}, f32[16]{0:T(128)}, u32[]{:S(2)}) copy-start(f32[16]{0:T(128)} %constant.48) | copy-start | bytes 196
  11.3 43.4 %copy-start.5 = (s32[1,128]{1,0:T(1,128)S(1)}, s32[1,128]{1,0:T(1,128)}, u32[]{:S(2)}) copy-start(s32[1,128]{1,0:T(1,128)} %param.15) | copy-start | bytes 1540
  19.0 1.5 %copy-start.2 = (f32[316,16,128]{2,1,0:T(8,128)}, f32[316,16,128]{2,1,0:T(8,128)S(1)}, u32[]{:S(2)}) copy-start(f32[316,16,128]{2,1,0:T(8,128)S(1)} %get-tuple-element.11) | copy-start | bytes 7766020
  20.5 16.5 %collective-permute-start = (f32[24,128]{1,0:T(8,128)S(1)}, f32[24,128]{1,0:T(8,128)S(1)}, u32[]{:S(2)}, u32[]{:S(2)}) collective-permute-start(f32[24,128]{1,0:T(8,128)S(1)} %get-tuple-element.9), channel_id=1, source_target_pairs={{0,64},{16,80},{32,96},{48,112},{64,0},{80,16},{96,32},{112,48},{1... | collective-permute-start | bytes 36872 | tf_op jit(solution)/shard_map/ppermute | solution.py:404
  36.9 8.1 %collective-permute-start.3 = (f32[2,24,128]{2,1,0:T(8,128)S(1)}, f32[2,24,128]{2,1,0:T(8,128)S(1)}, u32[]{:S(2)}, u32[]{:S(2)}) collective-permute-start(f32[2,24,128]{2,1,0:T(8,128)S(1)} %pad_maximum_fusion), channel_id=1, source_target_pairs={{0,48},{16,32},{32,16},{48,0},{64,112},{80,96},{96,80},{112,64},{1... | collective-permute-start | bytes 73736 | tf_op jit(solution)/shard_map/ppermute | solution.py:405
  39.7 5.3 %collective-permute-start.2 = (f32[2,24,128]{2,1,0:T(8,128)S(1)}, f32[2,24,128]{2,1,0:T(8,128)S(1)}, u32[]{:S(2)}, u32[]{:S(2)}) collective-permute-start(f32[2,24,128]{2,1,0:T(8,128)S(1)} %pad_maximum_fusion), channel_id=1, source_target_pairs={{0,32},{16,48},{32,0},{48,16},{64,96},{80,112},{96,64},{112,80},{1... | collective-permute-start | bytes 73736 | tf_op jit(solution)/shard_map/ppermute | solution.py:405
  40.5 3.8 %collective-permute-start.1 = (f32[2,24,128]{2,1,0:T(8,128)S(1)}, f32[2,24,128]{2,1,0:T(8,128)S(1)}, u32[]{:S(2)}, u32[]{:S(2)}) collective-permute-start(f32[2,24,128]{2,1,0:T(8,128)S(1)} %pad_maximum_fusion), channel_id=1, source_target_pairs={{0,16},{16,0},{32,48},{48,32},{64,80},{80,64},{96,112},{112,96},{1... | collective-permute-start | bytes 73736 | tf_op jit(solution)/shard_map/ppermute | solution.py:405
  54.7 31.2 %copy-start.3 = (f32[316,16,128]{2,1,0:T(8,128)S(1)}, f32[316,16,128]{2,1,0:T(8,128)}, u32[]{:S(2)}) copy-start(f32[316,16,128]{2,1,0:T(8,128)} %copy-done.2) | copy-start | bytes 7766020
  60.4 25.6 %copy-start = (f32[8,288,128]{2,1,0:T(8,128)}, f32[8,288,128]{2,1,0:T(8,128)S(1)}, u32[]{:S(2)}) copy-start(f32[8,288,128]{2,1,0:T(8,128)S(1)} %phi.1.recv) | copy-start | bytes 3538948
  104.0 3.7 %copy-start.1 = (f32[8,288,128]{2,1,0:T(8,128)S(1)}, f32[8,288,128]{2,1,0:T(8,128)}, u32[]{:S(2)}) copy-start(f32[8,288,128]{2,1,0:T(8,128)} %copy-done) | copy-start | bytes 3538948
  104.0 22.1 %all-to-all-start.2 = ((f32[8,288,128]{2,1,0:T(8,128)}), f32[8,288,128]{2,1,0:T(8,128)S(1)}, u32[]{:S(2)}, u32[]{:S(2)}) async-start(f32[8,288,128]{2,1,0:T(8,128)} %translate.1), calls=%async_computation.2 | async-start | bytes 2359296 | tf_op jit(solution)/shard_map/all_to_all | solution.py:446

commit v7 on v6

--- a/solution.py
+++ b/solution.py
@@ -300,7 +300,7 @@
                 out_v[p, at // 3, :, 128 * (at % 3) : 128 * (at % 3) + 128] = v
             return carry
 
-        lax.fori_loop(8 * q, 8 * q + 8, one, 0)
+        lax.fori_loop(8 * q, 8 * q + 8, one, 0, unroll=4)
         some = pl.ds(8 * q, 8)
         copies.append(pltpu.make_async_copy(out_v.at[some], out.at[some], sems.at[q]))
         copies[-1].start()

time: 128 us -> 128 us (level)
  no operation moved by 1% of the time
where the time goes in v7:
time: 128 us; the launch traced here: 127 us
  waiting for transfers between devices  42.7 us (33%)
  Pallas kernels  37.7 us (29%)
  blocking collectives  25.6 us (20%)
  starting transfers between devices  16.9 us (13%)
  local copies, waits for them, and re-layouts  1.74 us (1%)
  other arithmetic  1.74 us (1%)
    all_to_all x1, blocking collectives, shards(): everywhere = lax.all_to_all(send, 'box', 0, 0)  25.6 us
    pallas_call x1, Pallas kernels, shards(): pl.pallas_call(translate_kernel, in_specs=[smem(), vmem(), vmem(), vmem()...  18 us
    all_to_all x1, waiting for transfers between devices, shards(): back = lax.all_to_all(back, 'box', 0, 0)  17.2 us
    ppermute x1, waiting for transfers between devices, shards(): lists = jnp.stack([lists, lax.ppermute(lists, 'box', pairs[4])])  11.8 us
    all_to_all x1, waiting for transfers between devices, shards(): bands = lax.all_to_all(bands, 'samp', 0, 0)  9.68 us
    pallas_call x1, Pallas kernels, shards(): pl.pallas_call(prepare_kernel, in_specs=[smem(), vmem(), vmem(), vmem(),...  7.61 us
    all_to_all x1, starting transfers between devices, shards(): bands = lax.all_to_all(bands, 'samp', 0, 0)  6.08 us
    pallas_call x1, Pallas kernels, shards(): pl.pallas_call(phi_kernel, in_specs=[smem(), vmem()] + [anywhere()] * 3 +...  5.63 us
  transfers between devices with their start and end apart: 6, of which 5 were waited for; matrix products, arithmetic and copies ran while one was open for 2% of the time, Pallas kernels for 7%

profile of v7, /device:TPU:32, one launch (start us, length us, event | category | flops | bytes accessed | tf_op | source)
XLA Modules:
  0.0 127.2 jit_solution(11832006244744645952)
XLA Ops:
  0.6 4.2 %theta.1 = (f32[16,392,128]{2,1,0:T(8,128)}, f32[8,128]{1,0:T(8,128)S(1)}) custom-call(s32[1,8]{1,0:T(1,128)} %bitcast.22, bf16[192,128]{1,0:T(8,128)(2,1)} %constant.35.clone.table_high, bf16[192,128]{1,0:T(8,128)(2,1)} %constant.36.clone.table_low, f32[8,2,128,256]{3,2,1,0:T(8,128)} %child.1), custom_call_target="tpu_custom_call" | custom-call | tf_op jit(solution)/shard_map/theta/pallas_call | solution.py:370
  4.9 0.0 copy-start.7
  4.9 0.0 copy-start.4
  4.9 6.1 %all-to-all-start = ((f32[16,392,128]{2,1,0:T(8,128)}), f32[16,392,128]{2,1,0:T(8,128)S(1)}, u32[]{:S(2)}, u32[]{:S(2)}) async-start(f32[16,392,128]{2,1,0:T(8,128)} %get-tuple-element.10), calls=%async_computation | async-start | bytes 6422528 | tf_op jit(solution)/shard_map/all_to_all | solution.py:385
  11.0 0.1 add_convert_fusion
  11.1 0.1 copy.16
  11.2 0.1 convert_element_type.12.lists
  11.3 0.0 copy-done.4
  11.3 0.0 copy-start.11
  11.3 0.0 copy-start.10
  11.3 0.0 copy-start.8
  11.3 0.0 copy-start.9
  11.3 0.0 copy-start.5
  11.3 7.6 %prepare.1 = (f32[316,16,128]{2,1,0:T(8,128)S(1)}, f32[8,384]{1,0:T(8,128)S(1)}, f32[24,128]{1,0:T(8,128)S(1)}) custom-call(s32[1]{0:T(128)} %bitcast.1.box.box_id, f32[8,128]{1,0:T(8,128)S(1)} %get-tuple-element.7.token, f32[24,128]{1,0:T(8,128)S(1)} %convert_element_type.12.lists, f32[8,384]{1,0:T(8,128)S(1)} %copy-done.4, f32[316,12,2,384]{3,2,1,0:T(2,128)} %bitcast.18), custom_call_target="tpu_custom_call" | custom-call | flops 10000000 | bytes 10000000 | tf_op jit(solution)/shard_map/prepare/pallas_call | solution.py:389
  19.0 1.5 %copy-done.2 = f32[316,16,128]{2,1,0:T(8,128)} copy-done((f32[316,16,128]{2,1,0:T(8,128)}, f32[316,16,128]{2,1,0:T(8,128)S(1)}, u32[]{:S(2)}) %copy-start.2) | copy-done | bytes 2588696
  20.5 3.0 %collective-permute-start = (f32[24,128]{1,0:T(8,128)S(1)}, f32[24,128]{1,0:T(8,128)S(1)}, u32[]{:S(2)}, u32[]{:S(2)}) collective-permute-start(f32[24,128]{1,0:T(8,128)S(1)} %get-tuple-element.9), channel_id=1, source_target_pairs={{0,64},{16,80},{32,96},{48,112},{64,0},{80,16},{96,32},{112,48},{1... | collective-permute-start | bytes 36872 | tf_op jit(solution)/shard_map/ppermute | solution.py:404
  23.5 0.1 broadcast_multiply_fusion
  23.6 1.5 %sine_multiply_fusion = (f32[8,16,384]{2,1,0:T(8,128)}, f32[8,16,384]{2,1,0:T(8,128)}) fusion(f32[16]{0:T(128)S(1)} %copy-done.9, f32[8,16]{1,0:T(8,128)S(1)} %broadcast_multiply_fusion, f32[8,384]{1,0:T(8,128)S(1)} %copy-done.8, f32[16]{0:T(128)S(1)} %get-tuple-element.14), kind=kLoop, calls=%fused_computation | loop fusion | flops 196608 | bytes 406144 | tf_op jit(solution)/shard_map/mul | solution.py:323
  25.1 11.8 %collective-permute-done = f32[24,128]{1,0:T(8,128)S(1)} collective-permute-done((f32[24,128]{1,0:T(8,128)S(1)}, f32[24,128]{1,0:T(8,128)S(1)}, u32[]{:S(2)}, u32[]{:S(2)}) %collective-permute-start) | collective-permute-done | bytes 12320 | tf_op jit(solution)/shard_map/ppermute | solution.py:404
  36.9 2.8 %collective-permute-start.3 = (f32[2,24,128]{2,1,0:T(8,128)S(1)}, f32[2,24,128]{2,1,0:T(8,128)S(1)}, u32[]{:S(2)}, u32[]{:S(2)}) collective-permute-start(f32[2,24,128]{2,1,0:T(8,128)S(1)} %pad_maximum_fusion), channel_id=1, source_target_pairs={{0,48},{16,32},{32,16},{48,0},{64,112},{80,96},{96,80},{112,64},{1... | collective-permute-start | bytes 73736 | tf_op jit(solution)/shard_map/ppermute | solution.py:405
  39.7 0.8 collective-permute-start.2
  40.5 0.5 collective-permute-start.1
  41.0 3.3 %collective-permute-done.1 = f32[2,24,128]{2,1,0:T(8,128)S(1)} collective-permute-done((f32[2,24,128]{2,1,0:T(8,128)S(1)}, f32[2,24,128]{2,1,0:T(8,128)S(1)}, u32[]{:S(2)}, u32[]{:S(2)}) %collective-permute-start.1) | collective-permute-done | bytes 24608 | tf_op jit(solution)/shard_map/ppermute | solution.py:405
  44.3 0.7 collective-permute-done.2
  45.1 9.7 %all-to-all-done.recv = f32[16,392,128]{2,1,0:T(8,128)S(1)} async-done(((f32[16,392,128]{2,1,0:T(8,128)}), f32[16,392,128]{2,1,0:T(8,128)S(1)}, u32[]{:S(2)}, u32[]{:S(2)}) %all-to-all-start) | async-done | bytes 3211296 | tf_op jit(solution)/shard_map/all_to_all | solution.py:385
  54.7 5.6 %phi.1.recv = f32[8,288,128]{2,1,0:T(8,128)S(1)} custom-call(s32[128]{0:T(128)S(1)} %bitcast.17, f32[8,384]{1,0:T(8,128)S(1)} %get-tuple-element.8.stencil, s32[8,24,128]{2,1,0:T(8,128)S(1)} %convert_element_type.13.lists, f32[8,16,384]{2,1,0:T(8,128)} %get-tuple-element.13.cos_hbm, f32[8,16,384]{2,1,0:T(8,128)} %get-tuple-element.12.sin_hbm, ...), custom_call_target="tpu_custom_call" | custom-call | tf_op jit(solution)/shard_map/phi/pallas_call | solution.py:407
  60.4 25.6 %all_to_all.15.recv = f32[8,288,128]{2,1,0:T(8,128)S(1)} all-to-all(f32[8,288,128]{2,1,0:T(8,128)S(1)} %phi.1.recv), channel_id=1, replica_groups=mesh['box'=8,'samp'=16] {'box'}, dimensions={0} | all-to-all | bytes 2359296 | tf_op jit(solution)/shard_map/all_to_all | solution.py:428
  86.0 18.0 %translate.1 = f32[8,288,128]{2,1,0:T(8,128)} custom-call(s32[1]{0:T(128)} %bitcast.1.box.box_id, s32[8,24,128]{2,1,0:T(8,128)S(1)} %convert_element_type.13.lists, f32[8,288,128]{2,1,0:T(8,128)S(1)} %all_to_all.15.recv, f32[5056,128]{1,0:T(8,128)S(1)} %bitcast.15), custom_call_target="tpu_custom_call" | custom-call | tf_op jit(solution)/shard_map/translate/pallas_call | solution.py:430
  104.0 3.7 %all-to-all-start.2 = ((f32[8,288,128]{2,1,0:T(8,128)}), f32[8,288,128]{2,1,0:T(8,128)S(1)}, u32[]{:S(2)}, u32[]{:S(2)}) async-start(f32[8,288,128]{2,1,0:T(8,128)} %translate.1), calls=%async_computation.2 | async-start | bytes 2359296 | tf_op jit(solution)/shard_map/all_to_all | solution.py:446
  107.7 1.1 place.2
  108.9 17.2 %all-to-all-done.2.recv = f32[8,288,128]{2,1,0:T(8,128)S(1)} async-done(((f32[8,288,128]{2,1,0:T(8,128)}), f32[8,288,128]{2,1,0:T(8,128)S(1)}, u32[]{:S(2)}, u32[]{:S(2)}) %all-to-all-start.2) | async-done | bytes 1179680 | tf_op jit(solution)/shard_map/all_to_all | solution.py:446
  126.1 1.1 place.3
  (25 shorter events, 0.1 us)
Async XLA Ops:
  4.9 6.1 %copy-start.6 = (s32[32,48]{1,0:T(8,128)S(1)}, s32[32,48]{1,0:T(8,128)}, u32[]{:S(2)}) copy-start(s32[32,48]{1,0:T(8,128)} %param.17) | copy-start | bytes 18436
  4.9 6.1 %copy-start.7 = (s32[32,48]{1,0:T(8,128)S(1)}, s32[32,48]{1,0:T(8,128)}, u32[]{:S(2)}) copy-start(s32[32,48]{1,0:T(8,128)} %param.16) | copy-start | bytes 18436
  4.9 6.4 %copy-start.4 = (f32[8,384]{1,0:T(8,128)S(1)}, f32[8,384]{1,0:T(8,128)}, u32[]{:S(2)}) copy-start(f32[8,384]{1,0:T(8,128)} %constant.41.clone.stencil) | copy-start | bytes 36868
  4.9 49.8 %all-to-all-start = ((f32[16,392,128]{2,1,0:T(8,128)}), f32[16,392,128]{2,1,0:T(8,128)S(1)}, u32[]{:S(2)}, u32[]{:S(2)}) async-start(f32[16,392,128]{2,1,0:T(8,128)} %get-tuple-element.10), calls=%async_computation | async-start | bytes 6422528 | tf_op jit(solution)/shard_map/all_to_all | solution.py:385
  11.3 12.2 %copy-start.11 = (s32[16]{0:T(128)S(1)}, s32[16]{0:T(128)}, u32[]{:S(2)}) copy-start(s32[16]{0:T(128)} %constant.37.clone) | copy-start | bytes 196
  11.3 12.2 %copy-start.10 = (f32[8]{0:T(128)S(1)}, f32[8]{0:T(128)}, u32[]{:S(2)}) copy-start(f32[8]{0:T(128)} %constant.47) | copy-start | bytes 100
  11.3 12.3 %copy-start.8 = (f32[8,384]{1,0:T(8,128)S(1)}, f32[8,384]{1,0:T(8,128)}, u32[]{:S(2)}) copy-start(f32[8,384]{1,0:T(8,128)} %constant.46) | copy-start | bytes 36868
  11.3 12.3 %copy-start.9 = (f32[16]{0:T(128)S(1)}, f32[16]{0:T(128)}, u32[]{:S(2)}) copy-start(f32[16]{0:T(128)} %constant.48) | copy-start | bytes 196
  11.3 43.4 %copy-start.5 = (s32[1,128]{1,0:T(1,128)S(1)}, s32[1,128]{1,0:T(1,128)}, u32[]{:S(2)}) copy-start(s32[1,128]{1,0:T(1,128)} %param.15) | copy-start | bytes 1540
  19.0 1.5 %copy-start.2 = (f32[316,16,128]{2,1,0:T(8,128)}, f32[316,16,128]{2,1,0:T(8,128)S(1)}, u32[]{:S(2)}) copy-start(f32[316,16,128]{2,1,0:T(8,128)S(1)} %get-tuple-element.11) | copy-start | bytes 7766020
  20.5 16.5 %collective-permute-start = (f32[24,128]{1,0:T(8,128)S(1)}, f32[24,128]{1,0:T(8,128)S(1)}, u32[]{:S(2)}, u32[]{:S(2)}) collective-permute-start(f32[24,128]{1,0:T(8,128)S(1)} %get-tuple-element.9), channel_id=1, source_target_pairs={{0,64},{16,80},{32,96},{48,112},{64,0},{80,16},{96,32},{112,48},{1... | collective-permute-start | bytes 36872 | tf_op jit(solution)/shard_map/ppermute | solution.py:404
  36.9 8.1 %collective-permute-start.3 = (f32[2,24,128]{2,1,0:T(8,128)S(1)}, f32[2,24,128]{2,1,0:T(8,128)S(1)}, u32[]{:S(2)}, u32[]{:S(2)}) collective-permute-start(f32[2,24,128]{2,1,0:T(8,128)S(1)} %pad_maximum_fusion), channel_id=1, source_target_pairs={{0,48},{16,32},{32,16},{48,0},{64,112},{80,96},{96,80},{112,64},{1... | collective-permute-start | bytes 73736 | tf_op jit(solution)/shard_map/ppermute | solution.py:405
  39.7 5.3 %collective-permute-start.2 = (f32[2,24,128]{2,1,0:T(8,128)S(1)}, f32[2,24,128]{2,1,0:T(8,128)S(1)}, u32[]{:S(2)}, u32[]{:S(2)}) collective-permute-start(f32[2,24,128]{2,1,0:T(8,128)S(1)} %pad_maximum_fusion), channel_id=1, source_target_pairs={{0,32},{16,48},{32,0},{48,16},{64,96},{80,112},{96,64},{112,80},{1... | collective-permute-start | bytes 73736 | tf_op jit(solution)/shard_map/ppermute | solution.py:405
  40.5 3.8 %collective-permute-start.1 = (f32[2,24,128]{2,1,0:T(8,128)S(1)}, f32[2,24,128]{2,1,0:T(8,128)S(1)}, u32[]{:S(2)}, u32[]{:S(2)}) collective-permute-start(f32[2,24,128]{2,1,0:T(8,128)S(1)} %pad_maximum_fusion), channel_id=1, source_target_pairs={{0,16},{16,0},{32,48},{48,32},{64,80},{80,64},{96,112},{112,96},{1... | collective-permute-start | bytes 73736 | tf_op jit(solution)/shard_map/ppermute | solution.py:405
  54.7 31.3 %copy-start.3 = (f32[316,16,128]{2,1,0:T(8,128)S(1)}, f32[316,16,128]{2,1,0:T(8,128)}, u32[]{:S(2)}) copy-start(f32[316,16,128]{2,1,0:T(8,128)} %copy-done.2) | copy-start | bytes 7766020
  60.4 25.6 %copy-start = (f32[8,288,128]{2,1,0:T(8,128)}, f32[8,288,128]{2,1,0:T(8,128)S(1)}, u32[]{:S(2)}) copy-start(f32[8,288,128]{2,1,0:T(8,128)S(1)} %phi.1.recv) | copy-start | bytes 3538948
  104.0 3.7 %copy-start.1 = (f32[8,288,128]{2,1,0:T(8,128)S(1)}, f32[8,288,128]{2,1,0:T(8,128)}, u32[]{:S(2)}) copy-start(f32[8,288,128]{2,1,0:T(8,128)} %copy-done) | copy-start | bytes 3538948
  104.0 22.1 %all-to-all-start.2 = ((f32[8,288,128]{2,1,0:T(8,128)}), f32[8,288,128]{2,1,0:T(8,128)S(1)}, u32[]{:S(2)}, u32[]{:S(2)}) async-start(f32[8,288,128]{2,1,0:T(8,128)} %translate.1), calls=%async_computation.2 | async-start | bytes 2359296 | tf_op jit(solution)/shard_map/all_to_all | solution.py:446
